TPU v7x, 32 devices: a whole 2x2x4 slice. The times are simulated.
32 devices in a mesh: tok: 8 (over y, x, core), mlp: 4 (over z).
Axes of the slice: x: 2, y: 2, z: 4, core: 2. Of those that a mesh axis runs over, the one named last changes fastest.
Arguments:
- tokens: bfloat16 [37632, 384], P(('tok', 'mlp')), may hold values from -6 to 6
- action_mask: int32 [64, 588], P(('tok', 'mlp')), may hold values 0 or 1
- ln1_gain: bfloat16 [384], replicated, may hold values from 0.5 to 1.5
- ln1_bias: bfloat16 [384], replicated, may hold values from -3 to 3
- w_qkv: bfloat16 [384, 3072], P('tok'), may hold values from -0.3125 to 0.3125
- bias_qv: bfloat16 [2048], replicated, may hold values from -4 to 4
- w_out: bfloat16 [1024, 384], P('tok'), may hold values from -0.75 to 0.75
- bias_out: bfloat16 [384], replicated, may hold values from -3 to 3
- ln2_gain: bfloat16 [384], replicated, may hold values from 0.5 to 1.5
- ln2_bias: bfloat16 [384], replicated, may hold values from -3 to 3
- w_fc1: bfloat16 [384, 2048], P('tok', 'mlp'), may hold values from -0.3125 to 0.3125
- bias_fc1: bfloat16 [2048], P('mlp'), may hold values from -4 to 4
- w_fc2: bfloat16 [2048, 384], P('mlp', 'tok'), may hold values from -0.125 to 0.125
- bias_fc2: bfloat16 [384], replicated, may hold values from -3 to 3
- out_grad: bfloat16 [37632, 384], P(('tok', 'mlp')), may hold values from -6 to 6
Outputs:
- output: bfloat16 [37632, 384], P(('tok', 'mlp'))
- input_grad: float32 [37632, 384], P(('tok', 'mlp'))
- ln1_gain_grad: float32 [384], replicated
- ln1_bias_grad: float32 [384], replicated
- w_qkv_grad: float32 [384, 3072], P('tok')
- bias_qv_grad: float32 [2048], replicated
- w_out_grad: float32 [1024, 384], P('tok')
- bias_out_grad: float32 [384], replicated
- ln2_gain_grad: float32 [384], replicated
- ln2_bias_grad: float32 [384], replicated
- w_fc1_grad: float32 [384, 2048], P('tok', 'mlp')
- bias_fc1_grad: float32 [2048], P('mlp')
- w_fc2_grad: float32 [2048, 384], P('mlp', 'tok')
- bias_fc2_grad: float32 [384], replicated
All inputs are finite; a program needn't handle non-finite values. No bound on the sum of `action_mask` on one device may be relied on, other than what follows from the above.
Results may differ from a plain program's by a relative error of at most 0.017.
Values may be sent and summed in bfloat16 or wider, within the bound.
No kernel may reach another device: no remote copies, remote signals or barrier semaphores. Data moves between devices by JAX's collectives and lax.ppermute only.
A program may use at most 192 MiB of HBM per device.

v0:
```python
import jax
import jax.numpy as jnp
from jax import lax
from jax.sharding import PartitionSpec as P

HEADS = 16
HEAD_DIM = 64
FRAME_LEN = 196


epsilon = 1e-06
head_group = 4


def normalize(values, norm_gain, norm_shift):
    center = values - jnp.mean(values, axis=-1, keepdims=True)
    inverse = lax.rsqrt(jnp.mean(center * center, axis=-1, keepdims=True) + epsilon)
    scaled = center * inverse
    return (scaled * norm_gain + norm_shift, scaled, inverse)


def normalize_back(grad_rows, norm_gain, scaled, inverse):
    scaled_grad = grad_rows * norm_gain
    return inverse * (
        scaled_grad
        - jnp.mean(scaled_grad, axis=-1, keepdims=True)
        - scaled * jnp.mean(scaled_grad * scaled, axis=-1, keepdims=True)
    )


def gelu_values(hidden_pre):
    return jax.nn.gelu(hidden_pre, approximate=False)


def gelu_back(hidden_pre, grad_act):
    return jax.vjp(gelu_values, hidden_pre)[1](grad_act)[0]


def split_heads(values, seq_count, groups):
    shaped = values.reshape(seq_count, -1, groups, head_group, HEAD_DIM)
    return shaped.transpose(0, 2, 1, 3, 4).reshape(seq_count * groups, -1, head_group, HEAD_DIM)


def merge_heads(blocks, seq_count, groups):
    shaped = blocks.reshape(seq_count, groups, -1, head_group, HEAD_DIM)
    return shaped.transpose(0, 2, 1, 3, 4).reshape(-1, groups * head_group * HEAD_DIM)


def block_scores(query_block, key_block, mask_row):
    length = mask_row.shape[0]
    row_index = lax.broadcasted_iota(jnp.int32, (length, length), 0)
    col_index = lax.broadcasted_iota(jnp.int32, (length, length), 1)
    earlier = col_index // FRAME_LEN <= row_index // FRAME_LEN
    usable = earlier & (mask_row[None, :] == 1)
    allowed = usable | (row_index == col_index)
    raw_scores = jnp.einsum(
        "qhd,khd->hqk", query_block, key_block, preferred_element_type=jnp.float32
    ) * HEAD_DIM ** (-0.5)
    return jnp.where(allowed[None], raw_scores, -1e30)


def attend_block(operands):
    query_block, key_block, value_block, mask_row = operands
    scores = block_scores(query_block, key_block, mask_row)
    largest = jnp.max(scores, axis=-1, keepdims=True)
    exponent = jnp.exp(scores - largest)
    denominator = jnp.sum(exponent, axis=-1, keepdims=True)
    probabilities = exponent / denominator
    mixed_block = jnp.einsum(
        "hqk,khd->qhd",
        probabilities.astype(jnp.bfloat16),
        value_block,
        preferred_element_type=jnp.float32,
    )
    return (mixed_block, (largest + jnp.log(denominator))[..., 0])


def attend_back(operands):
    query_block, key_block, value_block, mask_row, grad_block, log_total = operands
    scores = block_scores(query_block, key_block, mask_row)
    probabilities = jnp.exp(scores - log_total[..., None])
    grad_prob = jnp.einsum(
        "qhd,khd->hqk", grad_block, value_block, preferred_element_type=jnp.float32
    )
    row_delta = jnp.sum(probabilities * grad_prob, axis=-1, keepdims=True)
    grad_scores = (probabilities * (grad_prob - row_delta)).astype(jnp.bfloat16)
    score_scale = HEAD_DIM ** (-0.5)
    grad_query = (
        jnp.einsum("hqk,khd->qhd", grad_scores, key_block, preferred_element_type=jnp.float32)
        * score_scale
    )
    grad_key = (
        jnp.einsum("hqk,qhd->khd", grad_scores, query_block, preferred_element_type=jnp.float32)
        * score_scale
    )
    grad_value = jnp.einsum(
        "hqk,qhd->khd",
        probabilities.astype(jnp.bfloat16),
        grad_block,
        preferred_element_type=jnp.float32,
    )
    return (grad_query, grad_key, grad_value)


def body(
    tokens,
    action_mask,
    ln1_gain,
    ln1_bias,
    w_qkv,
    bias_qv,
    w_out,
    bias_out,
    ln2_gain,
    ln2_bias,
    w_fc1,
    bias_fc1,
    w_fc2,
    bias_fc2,
    out_grad,
):
    seq_count = action_mask.shape[0]
    inner = HEADS * HEAD_DIM
    groups = HEADS // head_group
    wide_qkv, wide_out = (
        lax.all_gather(w_qkv, "tok", axis=0, tiled=True),
        lax.all_gather(w_out, "tok", axis=0, tiled=True),
    )
    fc1_part, fc2_part = (
        lax.all_gather(w_fc1, "tok", axis=0, tiled=True),
        lax.all_gather(w_fc2, "tok", axis=1, tiled=True),
    )
    gain_one = ln1_gain.astype(jnp.float32)
    gain_two = ln2_gain.astype(jnp.float32)
    inputs = tokens.astype(jnp.float32)
    first_norm, scaled_one, inverse_one = normalize(inputs, gain_one, ln1_bias.astype(jnp.float32))
    first_low = first_norm.astype(jnp.bfloat16)
    projected = jnp.dot(first_low, wide_qkv, preferred_element_type=jnp.float32)
    bias_full = bias_qv.astype(jnp.float32)
    queries = (projected[:, :inner] + bias_full[:inner]).astype(jnp.bfloat16)
    keys_all = projected[:, inner : 2 * inner].astype(jnp.bfloat16)
    values_all = (projected[:, 2 * inner :] + bias_full[inner:]).astype(jnp.bfloat16)
    query_blocks = split_heads(queries, seq_count, groups)
    key_blocks = split_heads(keys_all, seq_count, groups)
    value_blocks = split_heads(values_all, seq_count, groups)
    mask_blocks = jnp.repeat(action_mask, groups, axis=0)
    mixed_blocks, log_total = lax.map(
        attend_block, (query_blocks, key_blocks, value_blocks, mask_blocks)
    )
    mixed_low = merge_heads(mixed_blocks, seq_count, groups).astype(jnp.bfloat16)
    middle = (
        inputs
        + jnp.dot(mixed_low, wide_out, preferred_element_type=jnp.float32)
        + bias_out.astype(jnp.float32)
    )
    second_norm, scaled_two, inverse_two = normalize(middle, gain_two, ln2_bias.astype(jnp.float32))
    second_low = second_norm.astype(jnp.bfloat16)
    second_rows = lax.all_gather(second_low, "mlp", axis=0, tiled=True)
    hidden_pre = jnp.dot(
        second_rows, fc1_part, preferred_element_type=jnp.float32
    ) + bias_fc1.astype(jnp.float32)
    hidden_act = gelu_values(hidden_pre).astype(jnp.bfloat16)
    mlp_out = lax.psum_scatter(
        jnp.dot(hidden_act, fc2_part, preferred_element_type=jnp.float32).astype(jnp.bfloat16),
        "mlp",
        scatter_dimension=0,
        tiled=True,
    ).astype(jnp.float32)
    cotangent_all = lax.all_gather(out_grad, "mlp", axis=0, tiled=True)
    grad_act = jnp.dot(cotangent_all, fc2_part.T, preferred_element_type=jnp.float32)
    grad_pre = gelu_back(hidden_pre, grad_act).astype(jnp.bfloat16)
    fc1_grad = jnp.dot(second_rows.T, grad_pre, preferred_element_type=jnp.float32)
    fc2_grad = jnp.dot(hidden_act.T, cotangent_all, preferred_element_type=jnp.float32)
    hidden_bias_grad = jnp.sum(grad_pre.astype(jnp.float32), axis=0)
    grad_second = lax.psum_scatter(
        jnp.dot(grad_pre, fc1_part.T, preferred_element_type=jnp.float32).astype(jnp.bfloat16),
        "mlp",
        scatter_dimension=0,
        tiled=True,
    ).astype(jnp.float32)
    output = (middle + mlp_out + bias_fc2.astype(jnp.float32)).astype(jnp.bfloat16)
    cotangent = out_grad.astype(jnp.float32)
    fc2_bias_grad = jnp.sum(cotangent, axis=0)
    gain_two_grad = jnp.sum(grad_second * scaled_two, axis=0)
    shift_two_grad = jnp.sum(grad_second, axis=0)
    grad_middle = cotangent + normalize_back(grad_second, gain_two, scaled_two, inverse_two)
    grad_branch = grad_middle.astype(jnp.bfloat16)
    out_bias_grad = jnp.sum(grad_branch.astype(jnp.float32), axis=0)
    out_weight_grad = jnp.dot(mixed_low.T, grad_branch, preferred_element_type=jnp.float32)
    grad_mixed = jnp.dot(grad_branch, wide_out.T, preferred_element_type=jnp.float32).astype(
        jnp.bfloat16
    )
    grad_blocks = split_heads(grad_mixed, seq_count, groups)
    grad_query, grad_key, grad_value = lax.map(
        attend_back, (query_blocks, key_blocks, value_blocks, mask_blocks, grad_blocks, log_total)
    )
    query_grad = merge_heads(grad_query, seq_count, groups).astype(jnp.bfloat16)
    key_grad = merge_heads(grad_key, seq_count, groups).astype(jnp.bfloat16)
    value_grad = merge_heads(grad_value, seq_count, groups).astype(jnp.bfloat16)
    grad_qkv = jnp.concatenate([query_grad, key_grad, value_grad], axis=1)
    qv_bias_grad = jnp.concatenate(
        [
            jnp.sum(query_grad.astype(jnp.float32), axis=0),
            jnp.sum(value_grad.astype(jnp.float32), axis=0),
        ]
    )
    qkv_weight_grad = jnp.dot(first_low.T, grad_qkv, preferred_element_type=jnp.float32)
    grad_first = jnp.dot(grad_qkv, wide_qkv.T, preferred_element_type=jnp.float32)
    gain_one_grad = jnp.sum(grad_first * scaled_one, axis=0)
    shift_one_grad = jnp.sum(grad_first, axis=0)
    input_grad = grad_middle + normalize_back(grad_first, gain_one, scaled_one, inverse_one)
    summed = (
        lax.psum(qkv_weight_grad.astype(jnp.bfloat16), "mlp").astype(jnp.float32),
        lax.psum(out_weight_grad.astype(jnp.bfloat16), "mlp").astype(jnp.float32),
        lax.psum(gain_one_grad.astype(jnp.bfloat16), "mlp").astype(jnp.float32),
        lax.psum(shift_one_grad.astype(jnp.bfloat16), "mlp").astype(jnp.float32),
        lax.psum(qv_bias_grad.astype(jnp.bfloat16), "mlp").astype(jnp.float32),
        lax.psum(out_bias_grad.astype(jnp.bfloat16), "mlp").astype(jnp.float32),
        lax.psum(gain_two_grad.astype(jnp.bfloat16), "mlp").astype(jnp.float32),
        lax.psum(shift_two_grad.astype(jnp.bfloat16), "mlp").astype(jnp.float32),
        lax.psum(fc2_bias_grad.astype(jnp.bfloat16), "mlp").astype(jnp.float32),
    )
    qkv_shard, out_shard, fc1_shard, fc2_shard = (
        lax.psum_scatter(summed[0], "tok", scatter_dimension=0, tiled=True),
        lax.psum_scatter(summed[1], "tok", scatter_dimension=0, tiled=True),
        lax.psum_scatter(fc1_grad, "tok", scatter_dimension=0, tiled=True),
        lax.psum_scatter(fc2_grad, "tok", scatter_dimension=1, tiled=True),
    )
    small = lax.psum(
        (
            summed[2],
            summed[3],
            summed[4],
            summed[5],
            summed[6],
            summed[7],
            summed[8],
            hidden_bias_grad,
        ),
        "tok",
    )
    return (
        output,
        input_grad,
        small[0],
        small[1],
        qkv_shard,
        small[2],
        out_shard,
        small[3],
        small[4],
        small[5],
        fc1_shard,
        small[7],
        fc2_shard,
        small[6],
    )


def solution(mesh):
    placed = (
        P(("tok", "mlp"), None),
        P(("tok", "mlp"), None),
        P(),
        P(),
        P("tok", None),
        P(),
        P("tok", None),
        P(),
        P(),
        P(),
        P("tok", "mlp"),
        P("mlp"),
        P("mlp", "tok"),
        P(),
        P(("tok", "mlp"), None),
    )
    return jax.shard_map(
        body,
        mesh=mesh,
        in_specs=placed,
        out_specs=(
            P(("tok", "mlp"), None),
            P(("tok", "mlp"), None),
            P(),
            P(),
            P("tok", None),
            P(),
            P("tok", None),
            P(),
            P(),
            P(),
            P("tok", "mlp"),
            P("mlp"),
            P("mlp", "tok"),
            P(),
        ),
        check_vma=False,
    )
```

profile of v0, /device:TPU:0, one launch (start us, length us, event | category | flops | bytes accessed | tf_op | source)
XLA Modules:
  0.0 996.1 jit_solution(9010243356584652177)
XLA Ops:
  14.1 15.4 %all_gather.19 = bf16[1024,384]{1,0:T(8,128)(2,1)} all-gather(bf16[128,384]{1,0:T(8,128)(2,1)} %param.25), channel_id=1, replica_groups=mesh['tok'=8,'mlp'=4] {'tok'}, dimensions={0}, use_global_device_ids=true | all-gather | bytes 884736 | tf_op jit(solution)/shard_map/all_gather | solution.py:127
  31.9 11.8 %all-gather.4.cloned.1.call-done = bf16[384,3072]{1,0:T(8,128)(2,1)} async-done(((bf16[48,3072]{1,0:T(8,128)(2,1)}), bf16[384,3072]{1,0:T(8,128)(2,1)}) %all-gather.4.cloned.1.call-update) | async-done | bytes 2359312 | tf_op jit(solution)/shard_map/all_gather | solution.py:126
  43.7 5.7 fusion.97
  74.7 4.3 copy.89
  79.0 7.1 reshape.393
  91.7 69.7 %while.32 = (s32[]{:T(128)}, bf16[8,588,4,64]{1,3,2,0:T(8,128)(2,1)}, f32[8,4,588]{2,1,0:T(4,128)}, bf16[8,588,4,64]{1,3,2,0:T(8,128)(2,1)}, s32[8,588]{1,0:T(8,...) while((s32[]{:T(128)}, bf16[8,588,4,64]{1,3,2,0:T(8,128)(2,1)}, ...), condition=%wide.region_5.6_spmd, body=%wide.region_2.5_spmd.sunk | while | flops 372714368 | bytes 19743080 | solution.py:147
  161.4 6.9 copy.108
  168.3 6.5 convert_element_type.217
  181.0 9.5 all_gather.21
  190.6 8.6 all_gather.22
  199.2 52.3 %all-gather.6.cloned.1.call-done = bf16[4704,384]{1,0:T(8,128)(2,1)} async-done(((bf16[1176,384]{1,0:T(8,128)(2,1)}), bf16[4704,384]{1,0:T(8,128)(2,1)}) %all-gather.6.cloned.1.call-update) | async-done | bytes 3612688 | tf_op jit(solution)/shard_map/all_gather | solution.py:158
  251.5 26.1 %multiply_convert_fusion.1 = (bf16[4704,512]{1,0:T(8,128)(2,1)}, f32[4704,512]{1,0:T(8,128)}, f32[4704,512]{1,0:T(8,128)}) fusion(f32[512]{0:T(512)S(1)} %convert_element_type.222, bf16[4704,384]{1,0:T(8,128)(2,1)} %all-gather.6.cloned.1.call-done, bf16[384,512]{1,0:T(8,128)(2,1)S(1)} %all_gather.21), kind=kOutput, calls=%fused_computation.86 | convolution fusion | flops 2008645632 | bytes 28092416 | tf_op jit(solution)/shard_map/dot_general | solution.py:159
  277.6 45.3 %all-gather.8.cloned.1.call-done = bf16[4704,384]{1,0:T(8,128)(2,1)} async-done(((bf16[1176,384]{1,0:T(8,128)(2,1)}), bf16[4704,384]{1,0:T(8,128)(2,1)}) %all-gather.8.cloned.1.call-update) | async-done | bytes 3612688 | tf_op jit(solution)/shard_map/all_gather | solution.py:169
  322.9 10.8 %convert_reduce_fusion = (f32[512]{0:T(512)}, bf16[4704,512]{1,0:T(8,128)(2,1)S(1)}) fusion(f32[4704,512]{1,0:T(8,128)} %get-tuple-element.349, bf16[4704,384]{1,0:T(8,128)(2,1)} %all-gather.8.cloned.1.call-done, bf16[512,384]{0,1:T(8,128)(2,1)S(1)} %all_gather.22, f32[4704,512]{1,0:T(8,128)} %get-tuple-element.367, f32[512]{0:T(512)S(1)} %convert_element_type.222), kind=kOutput, calls=%fused_computation.84 | convolution fusion | flops 1890631168 | bytes 28094464 | tf_op jit(solution)/shard_map/dot_general | solution.py:170
  340.1 6.8 convolution_convert_fusion.1
  347.6 58.7 %reduce-scatter.21.cloned.1.call-done = bf16[1176,384]{1,0:T(8,128)(2,1)} async-done(((bf16[4704,384]{1,0:T(8,128)(2,1)}), bf16[1176,384]{1,0:T(8,128)(2,1)}) %reduce-scatter.21.cloned.1.call-update) | async-done | bytes 903184
  406.3 70.2 %reduce-scatter.19.cloned.1.call-done = bf16[1176,384]{1,0:T(8,128)(2,1)} async-done(((bf16[4704,384]{1,0:T(8,128)(2,1)}), bf16[1176,384]{1,0:T(8,128)(2,1)}) %reduce-scatter.19.cloned.1.call-update) | async-done | bytes 903184
  503.4 138.2 %while.33 = (s32[]{:T(128)}, bf16[8,588,4,64]{1,3,2,0:T(8,128)(2,1)}, bf16[8,588,4,64]{1,3,2,0:T(8,128)(2,1)}, bf16[8,588,4,64]{1,3,2,0:T(8,128)(2,1)}, bf16[8,5...) while((s32[]{:T(128)}, ...), condition=%wide.region_14.15_spmd, body=%wide.region_12.14_spmd.sunk | while | flops 908227200 | bytes 47217300 | solution.py:194
  641.6 5.9 copy.107
  647.5 5.5 convert_element_type.237
  659.9 6.7 convert_element_type.241
  670.8 6.9 convert_element_type.245
  682.1 8.3 convolution_convert_fusion.2
  690.4 6.5 fusion.103
  697.0 6.5 fusion.104
  703.6 108.8 %all-reduce.7.cloned.1.call-done = (bf16[384,3072]{1,0:T(8,128)(2,1)}, bf16[1024,384]{1,0:T(8,128)(2,1)}) async-done(((bf16[384,3072]{1,0:T(8,128)(2,1)}, bf16[1024,384]{1,0:T(8,128)(2,1)}), (bf16[384,3072]{1,0:T(8,128)(2,1)}, bf16[1024,384]{1,0:T(8,128)(2,1)})) %all-reduce.7.cloned.1.call-update) | async-done | bytes 3145744 | tf_op jit(solution)/shard_map/psum | solution.py:213
  824.0 10.3 %fusion.87 = (bf16[384]{0:T(512)(128)(2,1)S(1)}, f32[1176]{0:T(1024)S(1)}, f32[1176]{0:T(1024)S(1)}, bf16[384]{0:T(512)(128)(2,1)S(1)}, f32[1176,384]{1,0:T(8,128)}) fusion(bf16[1176,384]{1,0:T(8,128)(2,1)S(1)} %copy-done.5, f32[1176]{0:T(1024)S(1)} %copy-done.19, f32[1176]{0:T(1024)S(1)} %copy-done.17, f32[384]{0:T(512)S(1)} %copy-done.21, ...), kind=kOutput, calls=%fused_computation.136 | convolution fusion | flops 2779044352 | bytes 12316032 | tf_op jit(solution)/shard_map/dot_general | solution.py:208
  834.2 16.5 %all-reduce.3 = (bf16[384]{0:T(512)(128)(2,1)S(1)}, bf16[384]{0:T(512)(128)(2,1)S(1)}, bf16[2048]{0:T(1024)(128)(2,1)S(1)}, bf16[384]{0:T(512)(128)(2,1)S(1)}, b...) all-reduce(bf16[384]{0:T(512)(128)(2,1)S(1)} %get-tuple-element.290, ...), channel_id=1, replica_groups=mesh['tok'=8,'mlp'=4] {'mlp'}, use_global_device_ids=true, to_apply=%region_18.19 | all-reduce | flops 4352 | bytes 17408 | tf_op jit(solution)/shard_map/psum | solution.py:215
  850.8 23.0 %all-reduce.2 = (f32[384]{0:T(512)}, f32[384]{0:T(512)}, f32[2048]{0:T(1024)}, f32[384]{0:T(512)}, f32[384]{0:T(512)}, /*index=5*/f32[384]{0:T(512)}, f32[512]{0:T(512)}, f32[384]{0:T(512)}) all-reduce(bf16[384]{0:T(512)(128)(2,1)S(1)} %get-tuple-element.337, ...), channel_id=1, replica_groups=mesh['tok'=8,'mlp'=4] {'tok'}, use_global_device_ids=true, to_apply=%region_19.20 | all-reduce | flops 4864 | bytes 30208 | tf_op jit(solution)/shard_map/psum | solution.py:229
  876.8 12.0 %reduce-scatter.17.cloned.1.call-done = f32[512,48]{0,1:T(8,128)} async-done(((f32[512,384]{0,1:T(8,128)}), f32[512,48]{0,1:T(8,128)}) %reduce-scatter.17.cloned.1.call-update) | async-done | bytes 98320 | tf_op jit(solution)/shard_map/reduce_scatter | solution.py:227
  888.8 42.4 %reduce-scatter.13.cloned.1.call-done = f32[128,384]{1,0:T(8,128)} async-done(((f32[1024,384]{1,0:T(8,128)}), f32[128,384]{1,0:T(8,128)}) %reduce-scatter.13.cloned.1.call-update) | async-done | bytes 196624 | tf_op jit(solution)/shard_map/reduce_scatter | solution.py:225
  931.2 57.8 %reduce-scatter.11.cloned.1.call-done = f32[48,3072]{1,0:T(8,128)} async-done(((f32[384,3072]{1,0:T(8,128)}), f32[48,3072]{1,0:T(8,128)}) %reduce-scatter.11.cloned.1.call-update) | async-done | bytes 589840 | tf_op jit(solution)/shard_map/reduce_scatter | solution.py:224
  (296 shorter events, 316.9 us)
Async XLA Ops:
  7.2 36.5 %copy-start.4 = (bf16[1176,384]{1,0:T(8,128)(2,1)S(1)}, bf16[1176,384]{1,0:T(8,128)(2,1)}, u32[]{:S(2)}) copy-start(bf16[1176,384]{1,0:T(8,128)(2,1)} %param.19) | copy-start | bytes 2709508
  7.2 36.5 %all-gather.4.cloned.1.call-start = ((), (), s32[]{:S(2)}) async-start(), calls=%async_computation.6 | async-start | bytes 2654208 | tf_op jit(solution)/shard_map/all_gather | solution.py:126
  7.9 243.6 %all-gather.6.cloned.1.call-start = ((), (), s32[]{:S(2)}) async-start(), calls=%async_computation.7 | async-start | bytes 4515840 | tf_op jit(solution)/shard_map/all_gather | solution.py:158
  8.7 40.7 %copy-start.20 = (f32[384]{0:T(512)}, f32[384]{0:T(512)S(1)}, u32[]{:S(2)}) copy-start(f32[384]{0:T(512)S(1)} %convert_element_type.208) | copy-start | bytes 4612
  9.3 40.0 %copy-start.24 = (f32[384]{0:T(512)}, f32[384]{0:T(512)S(1)}, u32[]{:S(2)}) copy-start(f32[384]{0:T(512)S(1)} %convert_element_type.209) | copy-start | bytes 4612
  29.5 19.9 %copy-start.16 = (f32[1176]{0:T(1024)}, f32[1176]{0:T(1024)S(1)}, u32[]{:S(2)}) copy-start(f32[1176]{0:T(1024)S(1)} %broadcast_multiply_fusion.5) | copy-start | bytes 14116
  31.9 17.5 %copy-start.18 = (f32[1176]{0:T(1024)}, f32[1176]{0:T(1024)S(1)}, u32[]{:S(2)}) copy-start(f32[1176]{0:T(1024)S(1)} %add_rsqrt_fusion.1) | copy-start | bytes 14116
  161.4 6.9 copy-start.2
  178.4 12.2 %copy-start.30 = (bf16[512]{0:T(512)(128)(2,1)S(1)}, bf16[512]{0:T(512)(128)(2,1)}, u32[]{:S(2)}) copy-start(bf16[512]{0:T(512)(128)(2,1)} %param.30) | copy-start | bytes 3076
  178.4 12.1 %copy-start.23 = (bf16[512,48]{0,1:T(8,128)(2,1)S(1)}, bf16[512,48]{0,1:T(8,128)(2,1)}, u32[]{:S(2)}) copy-start(bf16[512,48]{0,1:T(8,128)(2,1)} %param.31) | copy-start | bytes 147460
  180.2 142.7 %all-gather.8.cloned.1.call-start = ((), (), s32[]{:S(2)}) async-start(), calls=%async_computation.8 | async-start | bytes 4515840 | tf_op jit(solution)/shard_map/all_gather | solution.py:169
  181.0 225.3 %reduce-scatter.21.cloned.1.call-start = ((), (), s32[]{:S(2)}) async-start(), calls=%async_computation.14 | async-start | bytes 4515840
  340.0 136.4 %reduce-scatter.19.cloned.1.call-start = ((), (), s32[]{:S(2)}) async-start(), calls=%async_computation.13 | async-start | bytes 4515840
  346.9 133.3 %copy-start.11 = (bf16[1176,384]{1,0:T(8,128)(2,1)S(1)}, bf16[1176,384]{1,0:T(8,128)(2,1)}, u32[]{:S(2)}) copy-start(bf16[1176,384]{1,0:T(8,128)(2,1)} %param.33) | copy-start | bytes 2709508
  346.9 465.4 %all-reduce.7.cloned.1.call-start = ((), (), s32[]{:S(2)}) async-start(), calls=%async_computation.15 | async-start | bytes 6291456 | tf_op jit(solution)/shard_map/psum | solution.py:213
  476.5 3.8 copy-start.12
  482.1 2.9 copy-start.6
  482.1 2.9 copy-start.14
  653.1 2.7 copy-start.8
  659.9 6.7 copy-start.1
  670.8 6.9 copy-start.9
  677.7 2.7 copy-start.10
  690.4 186.4 %reduce-scatter.15.cloned.1.call-start = ((), (), s32[]{:S(2)}) async-start(), calls=%async_computation.11 | async-start | bytes 884736 | tf_op jit(solution)/shard_map/reduce_scatter | solution.py:226
  696.9 191.9 %reduce-scatter.17.cloned.1.call-start = ((), (), s32[]{:S(2)}) async-start(), calls=%async_computation.12 | async-start | bytes 884736 | tf_op jit(solution)/shard_map/reduce_scatter | solution.py:227
  703.5 227.7 %reduce-scatter.13.cloned.1.call-start = ((), (), s32[]{:S(2)}) async-start(), calls=%async_computation.10 | async-start | bytes 1769472 | tf_op jit(solution)/shard_map/reduce_scatter | solution.py:225
  812.3 2.9 copy-start.15
  814.9 174.0 %reduce-scatter.11.cloned.1.call-start = ((), (), s32[]{:S(2)}) async-start(), calls=%async_computation.9 | async-start | bytes 5308416 | tf_op jit(solution)/shard_map/reduce_scatter | solution.py:224
  823.9 10.3 %copy-start.26 = (bf16[384]{0:T(512)(128)(2,1)S(1)}, bf16[384]{0:T(512)(128)(2,1)}, u32[]{:S(2)}) copy-start(bf16[384]{0:T(512)(128)(2,1)} %get-tuple-element.361) | copy-start | bytes 2308
  823.9 10.3 %copy-start.27 = (bf16[384]{0:T(512)(128)(2,1)S(1)}, bf16[384]{0:T(512)(128)(2,1)}, u32[]{:S(2)}) copy-start(bf16[384]{0:T(512)(128)(2,1)} %get-tuple-element.362) | copy-start | bytes 2308
  823.9 10.3 %copy-start.28 = (bf16[384]{0:T(512)(128)(2,1)S(1)}, bf16[384]{0:T(512)(128)(2,1)}, u32[]{:S(2)}) copy-start(bf16[384]{0:T(512)(128)(2,1)} %get-tuple-element.288) | copy-start | bytes 2308
  823.9 26.8 %copy-start.29 = (f32[512]{0:T(512)S(1)}, f32[512]{0:T(512)}, u32[]{:S(2)}) copy-start(f32[512]{0:T(512)} %get-tuple-element.369) | copy-start | bytes 6148
  824.0 49.8 %copy-start.7 = (f32[1176,384]{1,0:T(8,128)S(1)}, f32[1176,384]{1,0:T(8,128)}, u32[]{:S(2)}) copy-start(f32[1176,384]{1,0:T(8,128)} %copy-done.6) | copy-start | bytes 5419012
  (10 other events, 17.5 us)
Sparse Core Ops, SparseCore 0:
  9.9 33.7 all-gather.3
  180.3 71.1 all-gather.5
  253.1 69.7 all-gather.7
  340.1 66.1 reduce-scatter.20
  408.6 67.8 reduce-scatter.18
  690.5 121.7 all-reduce.6
  816.1 33.9 reduce-scatter.14
  853.8 34.9 reduce-scatter.16
  892.7 38.4 reduce-scatter.12
  935.1 53.8 reduce-scatter.10
where the time goes:
time: 1000 us; the launch traced here: 996 us
  waiting for transfers between devices  461 us (46%)
  matrix products  252 us (25%)
  local copies, waits for them, and re-layouts  120 us (12%)
  other arithmetic  73.2 us (7%)
  blocking collectives  73.1 us (7%)
  between operations  14.8 us (1%)
    unnamed x12, waiting for transfers between devices  130 us
    psum x1, waiting for transfers between devices, body(): lax.psum(qkv_weight_grad.astype(jnp.bfloat16), 'mlp').astype(jnp.float32)  109 us
    reduce_scatter x1, waiting for transfers between devices, body(): lax.psum_scatter(summed[0], 'tok', scatter_dimension=0, tiled=True)  57.8 us
    all_gather x1, waiting for transfers between devices, body(): second_rows = lax.all_gather(second_low, 'mlp', axis=0, tiled=True)  52.3 us
    all_gather x1, waiting for transfers between devices, body(): cotangent_all = lax.all_gather(out_grad, 'mlp', axis=0, tiled=True)  45.3 us
    reduce_scatter x1, waiting for transfers between devices, body(): lax.psum_scatter(summed[1], 'tok', scatter_dimension=0, tiled=True)  42.4 us
    dot_general x16, matrix products, block_scores(): jnp.einsum('qhd,khd->hqk', query_block, key_block, preferred_element_type...  34.6 us
    dot_general x8, matrix products, attend_block(): jnp.einsum('hqk,khd->qhd', probabilities.astype(jnp.bfloat16), value_bloc...  28.9 us
  transfers between devices with their start and end apart: 10, of which 9 were waited for; matrix products, arithmetic and copies ran while one was open for 8% of the time, Pallas kernels for 0%

commit v1 on v0

v1 whole, which is shorter than its diff:
```python
import functools

import jax
import jax.numpy as jnp
from jax import lax
from jax.experimental import pallas as pl
from jax.experimental.pallas import tpu as pltpu
from jax.sharding import PartitionSpec as P

HEADS = 16
HEAD_DIM = 64
FRAME_LEN = 196
LEN = 588
D = 384
FF = 2048
INNER = HEADS * HEAD_DIM
KEYS = 592
ROWS = 640
GROUP = 4
WIDE = GROUP * HEAD_DIM
GROUPS = HEADS // GROUP
QKV = 3 * WIDE
SMALL = 128
BLOCK = INNER + SMALL

epsilon = 1e-06
f32 = jnp.float32
bf16 = jnp.bfloat16

NN = (((1,), (0,)), ((), ()))
NT = (((1,), (1,)), ((), ()))
TN = (((0,), (0,)), ((), ()))

QUERY_BLOCKS = ((0, 128, 208), (128, 256, 400), (384, 256, 592))
KEY_RANGES = ((0, 208, 0), (208, 400, 128), (400, 592, 384))

VMEM = 56 * 1024 * 1024

BIAS_OUT, GAIN_TWO, SHIFT_TWO, BIAS_TWO, GAIN_ONE, SHIFT_ONE = (slice(k, k + 1) for k in range(6))


def dot(left, right, dims):
    return lax.dot_general(left, right, dims, preferred_element_type=f32)


def normalize(values):
    center = values - jnp.mean(values, axis=-1, keepdims=True)
    inverse = lax.rsqrt(jnp.mean(center * center, axis=-1, keepdims=True) + epsilon)
    return center * inverse, inverse


def normalize_back(grad_rows, norm_gain, scaled, inverse):
    scaled_grad = grad_rows * norm_gain
    return inverse * (
        scaled_grad
        - jnp.mean(scaled_grad, axis=-1, keepdims=True)
        - scaled * jnp.mean(scaled_grad * scaled, axis=-1, keepdims=True)
    )


def cost(micros):
    return pl.CostEstimate(flops=int(micros * 1.1e9), bytes_accessed=1024, transcendentals=0)


MASKS = (0, 2, 4, 6, 1, 3, 5, 7)


def owners(me, count):
    return [me ^ mask for mask in MASKS[:count]]


def whole(shape):
    return pl.BlockSpec(
        shape, lambda *step: (0,) * len(shape), pipeline_mode=pl.Buffered(buffer_count=1)
    )


def prepare_kernel(one_ref, two_ref, hidden_bias_ref, out_ref, bias_ref, *refs):
    row_refs, (pack_ref, block_ref, rows_ref, columns_ref, wide_bias_ref) = refs[:6], refs[6:]
    rows, slot = one_ref.shape
    pack_ref[:rows, :slot] = one_ref[...]
    pack_ref[:rows, slot:] = two_ref[...]
    pack_ref[rows:] = jnp.zeros_like(pack_ref[rows:])
    pack_ref[rows : rows + 1, :slot] = hidden_bias_ref[...].reshape(1, slot)
    turned = out_ref[...].T
    width = turned.shape[1]
    for r in range(D // rows):
        block_ref[:, r * width : (r + 1) * width] = turned[r * rows : (r + 1) * rows]
    rows_ref[...] = jnp.zeros_like(rows_ref)
    for k, ref in enumerate(row_refs):
        rows_ref[k : k + 1] = ref[...].astype(f32).reshape(1, D)
    columns_ref[...] = rows_ref[...].T
    wide_bias_ref[...] = bias_ref[...].astype(f32).reshape(1, 2 * INNER)


def prepare(w_fc1, w_fc2, bias_fc1, w_out, bias_qv, vectors):
    rows, slot = w_fc1.shape
    return pl.pallas_call(
        prepare_kernel,
        out_shape=[
            jax.ShapeDtypeStruct((rows + 16, 2 * slot), bf16),
            jax.ShapeDtypeStruct((rows, INNER), bf16),
            jax.ShapeDtypeStruct((8, D), f32),
            jax.ShapeDtypeStruct((D, 8), f32),
            jax.ShapeDtypeStruct((1, 2 * INNER), f32),
        ],
        cost_estimate=cost(2),
        name="prepare",
    )(w_fc1, w_fc2.T, bias_fc1, w_out, bias_qv, *vectors)


def norm_kernel(tokens_ref, rows_ref, out_ref, scaled_ref):
    for s in range(out_ref.shape[0]):
        values = tokens_ref[s * LEN : (s + 1) * LEN].astype(f32)
        scaled, _ = normalize(values)
        normed = scaled * rows_ref[GAIN_ONE] + rows_ref[SHIFT_ONE]
        for ref, rows in ((scaled_ref, scaled), (out_ref, normed)):
            ref[s, :LEN] = rows.astype(bf16)
            ref[s, LEN:] = jnp.zeros((ROWS - LEN, D), bf16)


def first_norm(tokens, rows_in):
    seqs = tokens.shape[0] // LEN
    shape = jax.ShapeDtypeStruct((seqs, ROWS, D), bf16)
    return pl.pallas_call(
        norm_kernel,
        out_shape=[shape, shape],
        compiler_params=pltpu.CompilerParams(vmem_limit_bytes=10 * 1024 * 1024),
        cost_estimate=cost(2.5),
        name="first_norm",
    )(tokens, rows_in)


def attend_kernel(pieces, me_ref, normed_ref, bias_ref, mask_ref, *refs):
    parts, refs = refs[:pieces], refs[pieces:]
    projected_ref, mixed_ref, exp_ref, inverse_ref, wide_ref = refs[:5]
    hide_scr, score_scr, mixed_scr, total_scr, mask_scr = refs[5:]
    group, seq = pl.program_id(0), pl.program_id(1)

    @pl.when((group == 0) & (seq == 0))
    def _():
        rows = D // pieces
        for j, owner in enumerate(owners(me_ref[0], pieces)):
            to = pl.ds(pl.multiple_of(owner * rows, 16), rows)
            for g in range(GROUPS):
                for k in range(3):
                    left = k * INNER + g * WIDE
                    at = g * QKV + k * WIDE
                    wide_ref[to, at : at + WIDE] = parts[j][:, left : left + WIDE]
        total_scr[...] = jnp.ones_like(total_scr)
        mask_scr[...] = jnp.zeros_like(mask_scr)
        count = hide_scr.shape[0]
        mask_scr[:count, :LEN] = mask_ref[...].astype(f32)
        turned = mask_scr[...].T
        key = lax.broadcasted_iota(jnp.int32, (KEYS, ROWS), 0)
        query = lax.broadcasted_iota(jnp.int32, (KEYS, ROWS), 1)
        later = ((query < FRAME_LEN) & (key >= FRAME_LEN)) | (
            (query < 2 * FRAME_LEN) & (key >= 2 * FRAME_LEN)
        )
        for s in range(count):
            usable = jnp.logical_not(later) & (turned[:KEYS, s : s + 1] > 0.5)
            hide_scr[s] = jnp.where(usable | (key == query), 0.0, -1e30)

    columns = pl.ds(pl.multiple_of(group * QKV, 128), QKV)
    projected = dot(normed_ref[seq, :KEYS], wide_ref[:, columns], NN)
    at = pl.multiple_of(group * WIDE, 128)
    queries = (projected[:, :WIDE] + bias_ref[:, pl.ds(at, WIDE)]).astype(bf16)
    projected_ref[0, :KEYS, :WIDE] = queries * bf16(HEAD_DIM**-0.5)
    projected_ref[0, :KEYS, WIDE : 2 * WIDE] = projected[:, WIDE : 2 * WIDE].astype(bf16)
    values = projected[:, 2 * WIDE :] + bias_ref[:, pl.ds(at + INNER, WIDE)]
    projected_ref[0, :KEYS, 2 * WIDE :] = values.astype(bf16)
    projected_ref[0, KEYS:] = jnp.zeros((ROWS - KEYS, QKV), bf16)
    from_ref = projected_ref.at[0]

    lane = lax.broadcasted_iota(jnp.int32, (1, 128), 1)
    row = lax.broadcasted_iota(jnp.int32, (128, 1), 0)
    units = [(h, b) for h in range(GROUP) for b in QUERY_BLOCKS]

    largest = {}
    flipped = {}

    def scores(unit):
        head, (start, width, keys) = units[unit]
        pair = head // 2 * 128
        mine = (lane < 64) if head % 2 == 0 else (lane >= 64)
        own_keys = from_ref[:keys, WIDE + pair : WIDE + pair + 128]
        own_keys = jnp.where(mine, own_keys, bf16(0))
        score = dot(own_keys, from_ref[start : start + width, pair : pair + 128], NT)
        score = score + hide_scr[seq, :keys, start : start + width]
        score_scr[unit % 2, :keys, :width] = score
        top = jnp.max(score.reshape(-1, 8, width), axis=0)
        largest[unit] = jnp.max(top, axis=0, keepdims=True)

    def exponents(unit):
        head, (start, width, keys) = units[unit]
        exponent = jnp.exp(score_scr[unit % 2, :keys, :width] - largest[unit])
        exp_ref[0, head, :keys, start : start + width] = exponent.astype(bf16)

    def mix(unit):
        head, (start, width, keys) = units[unit]
        pair = head // 2 * 128
        if head not in flipped:
            turned = from_ref[:KEYS, 2 * WIDE + pair : 2 * WIDE + pair + 128].T
            mine = (row < 64) if head % 2 == 0 else (row >= 64)
            flipped[head] = jnp.where(mine, turned, bf16(1))
        exponent = exp_ref[0, head, :keys, start : start + width]
        summed = dot(flipped[head][:, :keys], exponent, NN)
        if head % 2 == 0:
            values, total = summed[:64], summed[64:65]
        else:
            values, total = summed[64:], summed[0:1]
        inverse = 1.0 / total
        mixed_scr[head * 64 : (head + 1) * 64, start : start + width] = values * inverse
        total_scr[head : head + 1, start : start + width] = inverse

    count = len(units)
    scores(0)
    for unit in range(count + 1):
        if unit + 1 < count:
            scores(unit + 1)
        if unit < count:
            exponents(unit)
        if unit > 0:
            mix(unit - 1)
    mixed_ref[0] = mixed_scr[...].T.astype(bf16)
    inverse_ref[0, 0] = total_scr[...]


def attend(me, normed, parts, bias, mask):
    seqs = normed.shape[0]
    return pl.pallas_call(
        functools.partial(attend_kernel, len(parts)),
        grid=(GROUPS, seqs),
        in_specs=[
            pl.BlockSpec(memory_space=pltpu.SMEM),
            whole(normed.shape),
            whole(bias.shape),
            whole(mask.shape),
        ]
        + [whole(part.shape) for part in parts],
        out_specs=[
            pl.BlockSpec((1, ROWS, QKV), lambda g, s: (s, 0, g)),
            pl.BlockSpec((1, ROWS, WIDE), lambda g, s: (s, 0, g)),
            pl.BlockSpec((1, GROUP, KEYS, ROWS), lambda g, s: (s, g, 0, 0)),
            pl.BlockSpec((1, 1, 8, ROWS), lambda g, s: (s, g, 0, 0)),
            whole((D, GROUPS * QKV)),
        ],
        out_shape=[
            pltpu.HBM((seqs, ROWS, GROUPS * QKV), bf16),
            pltpu.HBM((seqs, ROWS, INNER), bf16),
            pltpu.HBM((seqs, HEADS, KEYS, ROWS), bf16),
            pltpu.HBM((seqs, GROUPS, 8, ROWS), f32),
            pltpu.HBM((D, GROUPS * QKV), bf16),
        ],
        scratch_shapes=[
            pltpu.VMEM((seqs, KEYS, ROWS), f32),
            pltpu.VMEM((2, KEYS, 256), f32),
            pltpu.VMEM((WIDE, ROWS), f32),
            pltpu.VMEM((8, ROWS), f32),
            pltpu.VMEM((8, ROWS), f32),
        ],
        compiler_params=pltpu.CompilerParams(vmem_limit_bytes=24 * 1024 * 1024),
        cost_estimate=cost(22),
        name="attend",
    )(me, normed, bias, mask, *parts)


def forward_kernel(pieces, n_bias, chunk, me_ref, tokens_ref, grad_ref, rows_ref, *refs):
    bias_refs, refs = refs[:n_bias], refs[n_bias:]
    mixed_ref, refs = refs[0], refs[1:]
    parts, refs = refs[:pieces], refs[pieces:]
    out_ref, middle_grad_ref, branch_ref, out_wide_ref = refs[:4]
    n_out = 2 if pieces > 1 else 1
    send_refs, refs = refs[4 : 4 + n_out], refs[4 + n_out :]
    one_scr, two_scr, middle_scr, scaled_scr, inverse_scr, second_scr, second_t, grad_scr = refs[:8]
    grad_t, total_scr, back_scr, weight_scr, small_scr, bias_scr = refs[8:14]
    stage_scrs = (refs[14:16], refs[16:18])
    seqs = branch_ref.shape[0]
    step = pl.program_id(0)
    rows = D // pieces
    per_slot = FF // 4
    ones = jnp.ones((16, seqs * KEYS), bf16)

    def send(value_ref, at, width, left):
        if pieces == 1:
            send_refs[0][0, :, left : left + width] = value_ref[:, at : at + width].astype(bf16)
            return
        for j, owner in enumerate(owners(me_ref[0], pieces)):
            first = pl.multiple_of(owner * rows, 16)
            send_refs[j // 4][j % 4, 0, :, left : left + width] = value_ref[
                pl.ds(first, rows), at : at + width
            ].astype(bf16)

    def send_vectors():
        vectors = small_scr[...].astype(bf16)
        if pieces == 1:
            send_refs[0][0, :48, INNER:] = vectors
        else:
            for j in range(pieces):
                send_refs[j // 4][j % 4, 0, :, INNER:] = vectors

    def produce(index, stage):
        act_scr, pre_scr = stage_scrs[stage]
        hidden = pl.ds(pl.multiple_of(index * chunk, 128), chunk)
        pre = dot(second_scr[...], one_scr[:, hidden], NN) + bias_scr[:, hidden]
        half = 0.5 + 0.5 * lax.erf(pre * (0.5**0.5))
        act_scr[...] = (pre * half).astype(bf16)
        slope = half + pre * (jnp.exp2(pre * pre * -0.7213475204444817) * 0.3989422804014327)
        grad_act = dot(grad_scr[...], two_scr[:, hidden], NN)
        pre_scr[...] = (grad_act * slope).astype(bf16)

    def consume(index, stage):
        act_scr, pre_scr = stage_scrs[stage]
        hidden = pl.ds(pl.multiple_of(index * chunk, 128), chunk)
        total_scr[...] += dot(act_scr[...], two_scr[:, hidden], NT)
        back_scr[...] += dot(pre_scr[...], one_scr[:, hidden], NT)
        left = stage * chunk
        weight_scr[:, :chunk] = dot(second_t[...], pre_scr[...], NN)
        send(weight_scr, 0, chunk, left)
        weight_scr[:, chunk : 2 * chunk] = dot(grad_t[...], act_scr[...], NN)
        send(weight_scr, chunk, chunk, left + per_slot)
        hidden_sum = dot(ones, pre_scr[...], NN)[0:1]
        for r in range(chunk // 128):
            at = stage * (chunk // 128) + r
            small_scr[at : at + 1] = hidden_sum[:, r * 128 : (r + 1) * 128]

    @pl.when(step == 0)
    def _():
        for j, owner in enumerate(owners(me_ref[0], pieces)):
            first = pl.multiple_of(owner * rows, 16)
            if pieces == 1:
                out_wide_ref[...] = parts[0][:, :INNER]
            else:
                to = pl.ds(pl.multiple_of(owner * 128, 128), 128)
                for r in range(pieces):
                    out_wide_ref[r * rows : (r + 1) * rows, to] = parts[j][
                        :, r * 128 : (r + 1) * 128
                    ]
            for z in range(4):
                left = INNER + 2 * per_slot * z
                slot = slice(z * per_slot, (z + 1) * per_slot)
                one_scr[pl.ds(first, rows), slot] = parts[j][:, left : left + per_slot]
                two_scr[pl.ds(first, rows), slot] = parts[j][
                    :, left + per_slot : left + 2 * per_slot
                ]
        if n_bias == 1:
            bias_scr[...] = bias_refs[0][...].astype(f32)
        else:
            for z in range(4):
                row = bias_refs[z][rows : rows + 1, :per_slot]
                bias_scr[:, z * per_slot : (z + 1) * per_slot] = row.astype(f32)
        for s in range(seqs):
            block = slice(s * KEYS, (s + 1) * KEYS)
            real = slice(s * KEYS, s * KEYS + LEN)
            spare = slice(s * KEYS + LEN, (s + 1) * KEYS)
            given = slice(s * LEN, (s + 1) * LEN)
            grad_scr[real] = grad_ref[given]
            grad_scr[spare] = jnp.zeros((KEYS - LEN, D), bf16)
            middle_scr[real] = tokens_ref[given].astype(f32) + rows_ref[BIAS_OUT]
            middle_scr[spare] = jnp.zeros((KEYS - LEN, D), f32)
            middle = middle_scr[block] + dot(mixed_ref[s, :KEYS], out_wide_ref[...], NT)
            middle_scr[block] = middle
            scaled, inverse = normalize(middle)
            scaled_scr[block] = scaled
            inverse_scr[block] = inverse
            second_scr[block] = (scaled * rows_ref[GAIN_TWO] + rows_ref[SHIFT_TWO]).astype(bf16)
        second_t[...] = second_scr[...].T
        grad_t[...] = grad_scr[...].T
        total_scr[...] = jnp.zeros_like(total_scr)
        back_scr[...] = jnp.zeros_like(back_scr)
        small_scr[...] = jnp.zeros_like(small_scr)
        produce(0, 0)

    @pl.when(step < 4)
    def _():
        produce(2 * step + 1, 1)
        consume(2 * step, 0)
        produce(jnp.minimum(2 * step + 2, FF // chunk - 1), 0)
        consume(2 * step + 1, 1)
        send_vectors()

    @pl.when(step == 4)
    def _():
        sums = [jnp.zeros((1, D), f32) for _ in range(2)]
        for s in range(seqs):
            block = slice(s * KEYS, (s + 1) * KEYS)
            given = slice(s * LEN, (s + 1) * LEN)
            output = (middle_scr[block] + total_scr[block] + rows_ref[BIAS_TWO]).astype(bf16)
            out_ref[given] = output[:LEN]
            scaled, inverse = scaled_scr[block], inverse_scr[block]
            grad_second = back_scr[block]
            grad_middle = grad_scr[block].astype(f32) + normalize_back(
                grad_second, rows_ref[GAIN_TWO], scaled, inverse
            )
            middle_grad_ref[s, :KEYS] = grad_middle
            branch_ref[s, :KEYS] = grad_middle.astype(bf16)
            branch_ref[s, KEYS:] = jnp.zeros((ROWS - KEYS, D), bf16)
            for k, term in enumerate((grad_second * scaled, grad_second)):
                sums[k] = sums[k] + jnp.sum(term, axis=0, keepdims=True)
        branch = jnp.concatenate([branch_ref[s, :KEYS] for s in range(seqs)], axis=0)
        sums.append(dot(ones, branch, NN)[0:1])
        sums.append(dot(ones, grad_scr[...], NN)[0:1])
        for k in range(4):
            for r in range(D // 128):
                at = 3 * k + r
                small_scr[at : at + 1] = sums[k][:, r * 128 : (r + 1) * 128]
        mixed = jnp.concatenate([mixed_ref[s, :KEYS] for s in range(seqs)], axis=0)
        weight_scr[...] = dot(branch, mixed, TN)
        if pieces == 1:
            send_refs[0][0, :, :INNER] = weight_scr[...].astype(bf16)
        else:
            for j, owner in enumerate(owners(me_ref[0], pieces)):
                to = pl.ds(pl.multiple_of(owner * 128, 128), 128)
                for r in range(pieces):
                    send_refs[j // 4][j % 4, 0, :, r * 128 : (r + 1) * 128] = weight_scr[
                        r * rows : (r + 1) * rows, to
                    ].astype(bf16)
        send_vectors()


def forward(me, tokens, cotangent, rows_in, biases, mixed, parts):
    seqs = tokens.shape[0] // LEN
    pieces = len(parts)
    chunk = 256
    if pieces > 1:
        send_shapes = [(pieces // 2, 5, D // pieces, BLOCK)] * 2
        send_specs = [pl.BlockSpec((pieces // 2, 1, D // pieces, BLOCK), lambda c: (0, c, 0, 0))] * 2
    else:
        send_shapes = [(5, D, BLOCK)]
        send_specs = [pl.BlockSpec((1, D, BLOCK), lambda c: (c, 0, 0))]
    rows3 = (seqs, ROWS, D)
    rows2 = (seqs * KEYS, D)
    mixed = pltpu.with_memory_space_constraint(mixed, pltpu.HBM)
    return pl.pallas_call(
        functools.partial(forward_kernel, pieces, len(biases), chunk),
        grid=(5,),
        in_specs=[
            pl.BlockSpec(memory_space=pltpu.SMEM),
            whole(tokens.shape),
            whole(tokens.shape),
            whole((8, D)),
        ]
        + [whole(b.shape) for b in biases]
        + [whole(mixed.shape)]
        + [whole(p.shape) for p in parts],
        out_specs=[whole(tokens.shape), whole(rows3), whole(rows3), whole((D, INNER))]
        + send_specs,
        out_shape=[
            jax.ShapeDtypeStruct(tokens.shape, bf16),
            jax.ShapeDtypeStruct(rows3, f32),
            jax.ShapeDtypeStruct(rows3, bf16),
            jax.ShapeDtypeStruct((D, INNER), bf16),
        ]
        + [jax.ShapeDtypeStruct(s, bf16) for s in send_shapes],
        scratch_shapes=[
            pltpu.VMEM((D, FF), bf16),
            pltpu.VMEM((D, FF), bf16),
            pltpu.VMEM(rows2, f32),
            pltpu.VMEM(rows2, f32),
            pltpu.VMEM((seqs * KEYS, 1), f32),
            pltpu.VMEM(rows2, bf16),
            pltpu.VMEM((D, seqs * KEYS), bf16),
            pltpu.VMEM(rows2, bf16),
            pltpu.VMEM((D, seqs * KEYS), bf16),
            pltpu.VMEM(rows2, f32),
            pltpu.VMEM(rows2, f32),
            pltpu.VMEM((D, INNER), f32),
            pltpu.VMEM((48, 128), f32),
            pltpu.VMEM((1, FF), f32),
        ]
        + [pltpu.VMEM((seqs * KEYS, chunk), bf16)] * 4,
        compiler_params=pltpu.CompilerParams(vmem_limit_bytes=36 * 1024 * 1024),
        cost_estimate=cost(30),
        name="forward",
    )(me, tokens, cotangent, rows_in, *biases, mixed, *parts)


def mixed_gradient_kernel(branch_ref, out_wide_ref, mixed_ref, grad_ref, delta_ref):
    lane = lax.broadcasted_iota(jnp.int32, (8, WIDE), 1)
    gather = (lane >> 6 == lax.broadcasted_iota(jnp.int32, (8, WIDE), 0)).astype(bf16)
    for g in range(delta_ref.shape[1]):
        columns = slice(g * WIDE, (g + 1) * WIDE)
        grad = dot(branch_ref[0], out_wide_ref[:, columns], NN).astype(bf16)
        grad_ref[0, :, columns] = grad
        product = grad.astype(f32) * mixed_ref[0, :, columns].astype(f32)
        first = product.astype(bf16)
        second = (product - first.astype(f32)).astype(bf16)
        delta_ref[0, g] = dot(gather, first, NT) + dot(gather, second, NT)


def mixed_gradient(branch, out_wide, mixed):
    seqs = branch.shape[0]
    each = 2
    columns = pl.BlockSpec((1, ROWS, each * WIDE), lambda s, g: (s, 0, g))
    return pl.pallas_call(
        mixed_gradient_kernel,
        grid=(seqs, GROUPS // each),
        in_specs=[
            pl.BlockSpec((1, ROWS, D), lambda s, g: (s, 0, 0)),
            pl.BlockSpec((D, each * WIDE), lambda s, g: (0, g)),
            columns,
        ],
        out_specs=[columns, pl.BlockSpec((1, each, 8, ROWS), lambda s, g: (s, g, 0, 0))],
        out_shape=[
            pltpu.HBM((seqs, ROWS, INNER), bf16),
            pltpu.HBM((seqs, GROUPS, 8, ROWS), f32),
        ],
        compiler_params=pltpu.CompilerParams(vmem_limit_bytes=16 * 1024 * 1024),
        cost_estimate=cost(5),
        name="mixed_gradient",
    )(branch, out_wide, mixed)


def backward_kernel(pieces, me_ref, *refs):
    grad_ref, delta_ref, scaled_ref, projected_ref, exp_ref, inverse_ref = refs[:6]
    wide_ref, norm_ref = refs[6:8]
    refs = refs[8:]
    n_out = 2 if pieces > 1 else 1
    back_ref = refs[0]
    send_refs = refs[1 : 1 + n_out]
    grad_scr, prob_scr, turned_scr, weight_scr, small_scr, sum_scr, norm_scr = refs[1 + n_out :]
    group, seq = pl.program_id(0), pl.program_id(1)
    groups, seqs = pl.num_programs(0), pl.num_programs(1)
    rows = D // pieces

    @pl.when((group == 0) & (seq == 0))
    def _():
        small_scr[...] = jnp.zeros_like(small_scr)
        norm_scr[...] = jnp.zeros_like(norm_scr)

    lane = lax.broadcasted_iota(jnp.int32, (1, 128), 1)
    low = lane < 64
    kept = {}
    for pair in range(GROUP // 2):
        columns = slice(pair * 128, pair * 128 + 128)
        grad = grad_ref[0, :, columns]
        query = projected_ref[0, :, columns]
        value = projected_ref[0, :KEYS, 2 * WIDE + pair * 128 : 2 * WIDE + pair * 128 + 128]
        turned = projected_ref[0, :KEYS, WIDE + pair * 128 : WIDE + pair * 128 + 128].T
        for half in range(2):
            head = 2 * pair + half
            mine = low if half == 0 else jnp.logical_not(low)
            own_value = jnp.where(mine, value, bf16(0))
            inverse = inverse_ref[0, 0, head : head + 1].astype(bf16)
            delta = delta_ref[0, 0, head : head + 1]
            side = slice(64 * half, 64 * half + 64)
            for start, width, keys in QUERY_BLOCKS:
                block = slice(start, start + width)
                change = dot(own_value[:keys], grad[block], NT) - delta[:, block]
                probability = exp_ref[0, head, :keys, block] * inverse[:, block]
                prob_scr[half, :keys, block] = probability
                grad_scr[half, :keys, block] = probability * change.astype(bf16)
            for start, width, keys in QUERY_BLOCKS:
                block = slice(start, start + width)
                turned_scr[head * 64 : (head + 1) * 64, block] = dot(
                    turned[side, :keys], grad_scr[half, :keys, block], NN
                ) * (HEAD_DIM**-0.5)
            for start, stop, seen in KEY_RANGES:
                value_grad = dot(prob_scr[half, start:stop, seen:], grad[seen:], NN)
                key_grad = dot(grad_scr[half, start:stop, seen:], query[seen:], NN)
                if half == 0:
                    kept[start] = (value_grad, key_grad)
                else:
                    at = slice(WIDE + pair * 128, WIDE + pair * 128 + 128)
                    back_ref[0, start:stop, at] = jnp.where(low, kept[start][1], key_grad).astype(
                        bf16
                    )
                    at = slice(2 * WIDE + pair * 128, 2 * WIDE + pair * 128 + 128)
                    back_ref[0, start:stop, at] = jnp.where(low, kept[start][0], value_grad).astype(
                        bf16
                    )
    back_ref[0, :KEYS, :WIDE] = turned_scr[...].T[:KEYS].astype(bf16)

    back = back_ref[0, :KEYS]
    weight = dot(scaled_ref[0, :KEYS], back, TN)
    total = dot(jnp.ones((16, KEYS), bf16), back, NN)[0:1]

    @pl.when(seq == 0)
    def _():
        weight_scr[...] = weight
        sum_scr[0:1] = total

    @pl.when(seq > 0)
    def _():
        weight_scr[...] += weight
        sum_scr[0:1] += total

    @pl.when(seq == seqs - 1)
    def _():
        sums = sum_scr[0:1]
        for r in range(WIDE // 128):
            at = group * (2 * WIDE // 128) + r
            small_scr[pl.ds(at, 1)] = sums[:, r * 128 : r * 128 + 128]
            at = at + WIDE // 128
            small_scr[pl.ds(at, 1)] = sums[:, 2 * WIDE + r * 128 : 2 * WIDE + r * 128 + 128]
        wide = wide_ref[...].astype(f32)
        scaled_weight = weight_scr[...]
        norm_scr[:, 0:1] += jnp.sum(scaled_weight * wide, axis=1, keepdims=True)
        norm_scr[:, 1:2] += jnp.sum(sums * wide, axis=1, keepdims=True)
        weight_scr[...] = scaled_weight * norm_ref[:, GAIN_ONE] + sums * norm_ref[:, SHIFT_ONE]
        start = pl.multiple_of(group * QKV, 128)
        if pieces == 1:
            send_refs[0][:, pl.ds(start, QKV)] = weight_scr[...].astype(bf16)
        else:
            for j, owner in enumerate(owners(me_ref[0], pieces)):
                first = pl.multiple_of(owner * rows, 16)
                send_refs[j // 4][j % 4, :, pl.ds(start, QKV)] = weight_scr[
                    pl.ds(first, rows)
                ].astype(bf16)

    @pl.when((group == groups - 1) & (seq == seqs - 1))
    def _():
        turned = norm_scr[...].T
        for k in range(2):
            for r in range(D // 128):
                small_scr[40 + 3 * k + r : 41 + 3 * k + r] = turned[
                    k : k + 1, r * 128 : (r + 1) * 128
                ]
        small = small_scr[...].astype(bf16)
        if pieces == 1:
            send_refs[0][:48, send_refs[0].shape[1] - SMALL :] = small
        else:
            for j in range(pieces):
                edge = send_refs[0].shape[2] - SMALL
                send_refs[j // 4][j % 4, :, edge:] = small


def backward(me, pieces, first_group, groups, grads, scaled, norm, saved):
    operands = [
        pltpu.with_memory_space_constraint(x, pltpu.HBM)
        for x in (*grads, scaled, saved[0], saved[2], saved[3], saved[4])
    ]
    seqs = scaled.shape[0]
    width = groups * QKV + SMALL
    if pieces > 1:
        send_shapes = [(pieces // 2, D // pieces, width)] * 2
    else:
        send_shapes = [(D, width)]
    columns = pl.BlockSpec((1, ROWS, WIDE), lambda g, s: (s, 0, g + first_group))
    heads = pl.BlockSpec((1, 1, 8, ROWS), lambda g, s: (s, g + first_group, 0, 0))
    rows_block = pl.BlockSpec((1, ROWS, D), lambda g, s: (s, 0, 0))
    return pl.pallas_call(
        functools.partial(backward_kernel, pieces),
        grid=(groups, seqs),
        in_specs=[
            pl.BlockSpec(memory_space=pltpu.SMEM),
            columns,
            heads,
            rows_block,
            pl.BlockSpec((1, ROWS, QKV), lambda g, s: (s, 0, g + first_group)),
            pl.BlockSpec((1, GROUP, KEYS, ROWS), lambda g, s: (s, g + first_group, 0, 0)),
            heads,
            pl.BlockSpec((D, QKV), lambda g, s: (0, g + first_group)),
            whole((D, 8)),
        ],
        out_specs=[pl.BlockSpec((1, ROWS, QKV), lambda g, s: (s, 0, g))]
        + [whole(s) for s in send_shapes],
        out_shape=[jax.ShapeDtypeStruct((seqs, ROWS, groups * QKV), bf16)]
        + [jax.ShapeDtypeStruct(s, bf16) for s in send_shapes],
        scratch_shapes=[
            pltpu.VMEM((2, KEYS, ROWS), bf16),
            pltpu.VMEM((2, KEYS, ROWS), bf16),
            pltpu.VMEM((WIDE, ROWS), f32),
            pltpu.VMEM((D, QKV), f32),
            pltpu.VMEM((48, 128), f32),
            pltpu.VMEM((8, QKV), f32),
            pltpu.VMEM((D, 128), f32),
        ],
        compiler_params=pltpu.CompilerParams(vmem_limit_bytes=20 * 1024 * 1024),
        cost_estimate=cost(11 * groups),
        name="backward",
    )(me, *operands, norm)


def input_kernel(tokens_ref, middle_grad_ref, rows_ref, early_ref, late_ref, wide_ref, out_ref, sum_scr):
    step, last = pl.program_id(0), pl.num_programs(0) - 1
    seqs = middle_grad_ref.shape[0]

    @pl.when(step < last)
    def _():
        for s in range(seqs):
            grad = dot(early_ref[s, :KEYS], wide_ref[...], NT)
            sum_scr[s] = jnp.where(step == 0, grad, sum_scr[s] + grad)

    @pl.when(step == last)
    def _():
        for s in range(seqs):
            grad_first = sum_scr[s] + dot(late_ref[s, :KEYS], wide_ref[...], NT)
            given = slice(s * LEN, (s + 1) * LEN)
            scaled, inverse = normalize(tokens_ref[given].astype(f32))
            out_ref[given] = middle_grad_ref[s, :LEN] + normalize_back(
                grad_first[:LEN], rows_ref[GAIN_ONE], scaled, inverse
            )


def input_gradient(tokens, middle_grad, rows_in, early, late, weights):
    seqs = middle_grad.shape[0]
    block = (seqs, ROWS, QKV)
    return pl.pallas_call(
        input_kernel,
        grid=(GROUPS,),
        in_specs=[
            whole(tokens.shape),
            whole(middle_grad.shape),
            whole(rows_in.shape),
            pl.BlockSpec(block, lambda g: (0, 0, jnp.minimum(g, GROUPS - 2))),
            whole(block),
            pl.BlockSpec((D, QKV), lambda g: (0, g)),
        ],
        out_specs=whole(tokens.shape),
        out_shape=jax.ShapeDtypeStruct(tokens.shape, f32),
        scratch_shapes=[pltpu.VMEM((seqs, KEYS, D), f32)],
        compiler_params=pltpu.CompilerParams(vmem_limit_bytes=16 * 1024 * 1024),
        cost_estimate=cost(8),
        name="input_gradient",
    )(tokens, middle_grad, rows_in, early, late, weights)


def swap(values, mask):
    size = lax.axis_size("tok")
    return lax.ppermute(values, "tok", [(i, i ^ mask) for i in range(size)])


def swap_half_line(values, stage):
    tok, mlp = lax.axis_size("tok"), lax.axis_size("mlp")
    pairs = []
    for t in range(tok):
        for z in range(mlp):
            far = (t % 2 == 0) == (stage == 0)
            pairs.append((t * mlp + z, t * mlp + (z ^ (2 if far else 1))))
    return lax.ppermute(values.astype(bf16), ("tok", "mlp"), pairs)


def after(values, *earlier):
    return lax.optimization_barrier((values,) + earlier)


def wide(values):
    return values.astype(f32)


def join(kept, arrived):
    return (wide(kept) + wide(arrived)).astype(bf16)


def body(
    tokens,
    action_mask,
    ln1_gain,
    ln1_bias,
    w_qkv,
    bias_qv,
    w_out,
    bias_out,
    ln2_gain,
    ln2_bias,
    w_fc1,
    bias_fc1,
    w_fc2,
    bias_fc2,
    out_grad,
):
    rows = w_qkv.shape[0]
    tok = lax.axis_size("tok")
    mlp = lax.axis_size("mlp")
    slot = w_fc1.shape[1]
    fast = tok == 8 and mlp == 4
    pieces = tok if fast else 1
    me = lax.axis_index("tok").astype(jnp.int32).reshape(1)
    chips = (2, 4, 6)
    odd = (me[0] & 1) == 1

    def pick(if_odd, if_even):
        return jnp.where(odd, if_odd, if_even)


    vectors = (bias_out, ln2_gain, ln2_bias, bias_fc2, ln1_gain, ln1_bias)
    me_a = me
    if fast:
        first_near = [swap(w_qkv, mask) for mask in chips]
        first_other = swap(w_qkv, 1)
        hidden_pack, out_block, rows_in, columns_in, bias_pair = prepare(
            w_fc1, w_fc2, bias_fc1, w_out, bias_qv, vectors
        )
        line = jnp.stack([hidden_pack, swap_half_line(hidden_pack, 0)])
        line = jnp.concatenate([line, swap_half_line(line, 1)])
        line = [line[0], pick(line[1], line[2]), pick(line[2], line[1]), line[3]]
        norm_tokens, first_near[0] = after(tokens, first_near[0])
        normed, scaled = first_norm(norm_tokens, rows_in)
        first_parts = [w_qkv] + first_near + [first_other] + [swap(p, 1) for p in first_near]
        hidden_own = jnp.concatenate([out_block] + [part[:rows] for part in line], axis=1)
        me_a, hidden_own = after(me, hidden_own)
        hidden_near = [swap(hidden_own, mask) for mask in chips + (1,)]
        biases = line
    else:
        rows_in = jnp.pad(wide(jnp.stack(vectors)), ((0, 2), (0, 0)))
        columns_in = rows_in.T
        bias_pair = wide(bias_qv).reshape(1, -1)
        normed, scaled = first_norm(tokens, rows_in)
        first_parts = [lax.all_gather(w_qkv, "tok", axis=0, tiled=True)]
        line = lax.all_gather(jnp.concatenate([w_fc1, w_fc2.T], axis=1), "mlp", axis=1, tiled=True)
        line = lax.all_gather(line, "tok", axis=0, tiled=True)
        biases = [lax.all_gather(bias_fc1, "mlp", axis=0, tiled=True).reshape(1, -1)]
        out_all = lax.all_gather(w_out, "tok", axis=0, tiled=True).T
        hidden_parts = [jnp.concatenate([out_all, line], axis=1)]

    saved = list(attend(me_a, normed, first_parts, bias_pair, action_mask))
    weights = saved[4]
    if fast:
        saved[1], *hidden_near = after(saved[1], *hidden_near)
        hidden_other = hidden_near.pop()
        hidden_parts = [hidden_own] + hidden_near + [hidden_other]
        hidden_parts = hidden_parts + [swap(part, 1) for part in hidden_near]

    output, middle_grad, branch, out_wide, *hidden_sends = forward(
        me, tokens, out_grad, rows_in, biases, saved[1], hidden_parts
    )

    grads = list(mixed_gradient(branch, out_wide, saved[1]))

    def back(me, group, count):
        return backward(me, pieces, group, count, grads, scaled, columns_in, saved)

    if not fast:
        back_a, sends_a = back(me, 0, 3)
        back_b, sends_b = back(me, 3, 1)
        input_grad = input_gradient(tokens, middle_grad, rows_in, back_a, back_b, weights)
        return slow_end(output, input_grad, hidden_sends[0], (sends_a, sends_b), slot)

    arrived = swap(hidden_sends[1], 1)
    grads[0], arrived = after(grads[0], arrived)
    hidden = join(hidden_sends[0], arrived)
    me_1, hidden = after(me, hidden)
    near = [swap(hidden[k], chips[k - 1]) for k in (1, 2, 3)]
    back_a, *sends_a = back(me_1, 0, 3)

    back_a, *near = after(back_a, *near)
    hidden = wide(hidden[0]) + wide(near[0]) + wide(near[1]) + wide(near[2])
    sent = jnp.stack([pick(hidden[1], hidden[2]), hidden[3], hidden[4]]).astype(bf16)
    group_a = join(sends_a[0], swap(sends_a[1], 1))
    me_2, group_a, sent = after(me, group_a, sent)
    line_1 = swap_half_line(sent, 0)
    near_a = [swap(group_a[k], chips[k - 1]) for k in (1, 2, 3)]
    back_b, *sends_b = back(me_2, 3, 1)

    back_b, line_1, *near_a = after(back_b, line_1, *near_a)
    total_a = wide(group_a[0]) + wide(near_a[0]) + wide(near_a[1]) + wide(near_a[2])
    block = hidden[0] + wide(line_1[0])
    middle_block = pick(hidden[2], hidden[1]) + wide(line_1[1])
    rest = hidden[4] + wide(line_1[2])
    sent = jnp.concatenate([middle_block, rest, total_a], axis=1).astype(bf16)
    sent, kept_b, sent_b = after(sent, *sends_b)
    line_2 = swap_half_line(sent, 1)
    group_b = join(kept_b, swap(sent_b, 1))
    near_b = [swap(group_b[k], chips[k - 1]) for k in (1, 2, 3)]
    block = block + wide(line_2[:, :BLOCK])
    rest = rest + wide(line_2[:, BLOCK : 2 * BLOCK])
    total_a = total_a + wide(line_2[:, 2 * BLOCK :])
    total_b = wide(group_b[0]) + wide(near_b[0]) + wide(near_b[1]) + wide(near_b[2])
    edge = total_a.shape[1]
    sent = jnp.concatenate([total_a, total_b], axis=1).astype(bf16)
    middle_grad, sent, block, rest = after(middle_grad, sent, block, rest)
    line_3 = swap_half_line(sent, 0)
    input_grad = input_gradient(tokens, middle_grad, rows_in, back_a, back_b, weights)

    input_grad, line_3 = after(input_grad, line_3)
    total_a = total_a + wide(line_3[:, :edge])
    total_b = total_b + wide(line_3[:, edge:])
    total_b = total_b + wide(swap_half_line(total_b, 1))

    out_rows = rest[:, :INNER].reshape(rows, tok, -1).transpose(1, 0, 2).reshape(D, -1).T
    return results(
        output,
        input_grad,
        [total_a[:, :-SMALL], total_b[:, :-SMALL]],
        [total_a[:, -SMALL:], total_b[:, -SMALL:]],
        out_rows,
        rest[:, INNER:],
        block[:, :INNER],
        block[: slot // 128, INNER:],
    )


def slow_end(output, input_grad, hidden, sends, slot):
    def scatter(values):
        values = lax.psum_scatter(wide(values), "tok", scatter_dimension=0, tiled=True)
        return lax.psum(values, "mlp")

    hidden = wide(hidden)
    blocks = jnp.concatenate([hidden[k, :, :INNER] for k in range(4)], axis=1)
    blocks = lax.psum_scatter(blocks, "tok", scatter_dimension=0, tiled=True)
    hidden_sum = lax.psum_scatter(blocks, "mlp", scatter_dimension=1, tiled=True)
    out_rows = scatter(hidden[4, :, :INNER].T)
    lines = slot // 128
    small = lax.psum(hidden[:, :48, INNER:], ("tok", "mlp"))
    bias_sum = lax.dynamic_index_in_dim(small[:4, :lines], lax.axis_index("mlp"), 0, False)
    small = small[4]
    weights = [scatter(s[:, :-SMALL]) for s in sends]
    smalls = [lax.psum(wide(s[:48, -SMALL:]), ("tok", "mlp")) for s in sends]
    return results(output, input_grad, weights, smalls, out_rows, small, hidden_sum, bias_sum)


def results(output, input_grad, weights, smalls, out_rows, small, hidden_sum, bias_sum):
    blocks = []
    for part in weights:
        blocks += [part[:, at : at + WIDE] for at in range(0, part.shape[1], WIDE)]
    qkv_grad = jnp.concatenate([block for k in range(3) for block in blocks[k::3]], axis=1)
    lines = WIDE // 128
    biases = []
    for part, weight in zip(smalls, weights):
        count = 2 * (weight.shape[1] // QKV)
        biases += [part[k * lines : (k + 1) * lines] for k in range(count)]
    bias_grad = jnp.concatenate(biases[0::2] + biases[1::2], axis=0).reshape(-1)
    norm_grad = smalls[0][40:46] + smalls[1][40:46]
    vectors = [small[3 * k : 3 * k + 3].reshape(-1) for k in range(4)]
    slot = hidden_sum.shape[1] // 2
    return (
        output,
        input_grad,
        norm_grad[:3].reshape(-1),
        norm_grad[3:].reshape(-1),
        qkv_grad,
        bias_grad,
        out_rows,
        vectors[2],
        vectors[0],
        vectors[1],
        hidden_sum[:, :slot],
        bias_sum.reshape(-1),
        hidden_sum[:, slot:].T,
        vectors[3],
    )


def solution(mesh):
    placed = (
        P(("tok", "mlp"), None),
        P(("tok", "mlp"), None),
        P(),
        P(),
        P("tok", None),
        P(),
        P("tok", None),
        P(),
        P(),
        P(),
        P("tok", "mlp"),
        P("mlp"),
        P("mlp", "tok"),
        P(),
        P(("tok", "mlp"), None),
    )
    return jax.shard_map(
        body,
        mesh=mesh,
        in_specs=placed,
        out_specs=(
            P(("tok", "mlp"), None),
            P(("tok", "mlp"), None),
            P(),
            P(),
            P("tok", None),
            P(),
            P("tok", None),
            P(),
            P(),
            P(),
            P("tok", "mlp"),
            P("mlp"),
            P("mlp", "tok"),
            P(),
        ),
        check_vma=False,
    )
```

time: 1000 us -> 173 us (0.17)
  waiting for transfers between devices: 461 us -> 24.2 us
  matrix products: 252 us -> 0 us
  local copies, waits for them, and re-layouts: 120 us -> 9.02 us
  Pallas kernels: 0 us -> 103 us
  blocking collectives: 73.1 us -> 0 us
  other arithmetic: 73.2 us -> 6.74 us
  starting transfers between devices: 0.66 us -> 29.1 us
  between operations: 14.8 us -> 1.19 us
    dot_general x68 -> x0, matrix products: 252 us -> none  [the longest x16 34.6 us: block_scores(): jnp.einsum('qhd,khd->hqk', query_block, key_block, preferred_element_type...]
    unnamed x12 -> x0, waiting for transfers between devices: 130 us -> none
    reduce_scatter x4 -> x0, waiting for transfers between devices: 112 us -> none  [the longest x1 57.8 us: body(): lax.psum_scatter(summed[0], 'tok', scatter_dimension=0, tiled=True)]
    all_gather x3 -> x0, waiting for transfers between devices: 109 us -> none  [the longest x1 52.3 us: body(): second_rows = lax.all_gather(second_low, 'mlp', axis=0, tiled=True)]
    psum x1 -> x0, waiting for transfers between devices: 109 us -> none  [body(): lax.psum(qkv_weight_grad.astype(jnp.bfloat16), 'mlp').astype(jnp.float32)]
    pallas_call x0 -> x8, Pallas kernels: none -> 103 us  [the longest x2 36.6 us: backward(): pl.pallas_call(functools.partial(backward_kernel, pieces), grid=(groups,...]
    convert_element_type x11 -> x0, local copies, waits for them, and re-layouts: 55.8 us -> none  [the longest x2 13.4 us: body(): merge_heads(mixed_blocks, seq_count, groups).astype(jnp.bfloat16)]
    psum x2 -> x0, blocking collectives: 39.5 us -> none  [the longest x1 23 us: body(): lax.psum((summed[2], summed[3], summed[4], summed[5], summed[6], summed[7...]
  transfers between devices with their start and end apart: 10 -> 32, of which waited for: 9 -> 13; matrix products, arithmetic and copies ran while one was open for 8% -> 4% of each run, Pallas kernels for 0% -> 42%
where the time goes in v1:
time: 173 us
  Pallas kernels  103 us (60%)
  starting transfers between devices  29.1 us (17%)
  waiting for transfers between devices  24.2 us (14%)
  local copies, waits for them, and re-layouts  9.02 us (5%)
  other arithmetic  6.74 us (4%)
    pallas_call x2, Pallas kernels, backward(): pl.pallas_call(functools.partial(backward_kernel, pieces), grid=(groups,...  36.6 us
    pallas_call x1, Pallas kernels, forward(): pl.pallas_call(functools.partial(forward_kernel, pieces, len(biases), chu...  27.4 us
    pallas_call x1, Pallas kernels, attend(): pl.pallas_call(functools.partial(attend_kernel, len(parts)), grid=(GROUPS...  23.4 us
    ppermute x26, starting transfers between devices, swap(): return lax.ppermute(values, 'tok', [(i, i ^ mask) for i in range(size)])  19.8 us
    ppermute x26, waiting for transfers between devices, swap(): return lax.ppermute(values, 'tok', [(i, i ^ mask) for i in range(size)])  16.6 us
    ppermute x6, starting transfers between devices, swap_half_line(): return lax.ppermute(values.astype(bf16), ('tok', 'mlp'), pairs)  9.26 us
    ppermute x6, waiting for transfers between devices, swap_half_line(): return lax.ppermute(values.astype(bf16), ('tok', 'mlp'), pairs)  7.62 us
    pallas_call x1, Pallas kernels, input_gradient(): pl.pallas_call(input_kernel, grid=(GROUPS,), in_specs=[whole(tokens.shape...  7.13 us
  transfers between devices with their start and end apart: 32, of which 13 were waited for; matrix products, arithmetic and copies ran while one was open for 4% of the time, Pallas kernels for 42%

profile of v1, /device:TPU:0, one launch (start us, length us, event | category | flops | bytes accessed | tf_op | source)
XLA Modules:
  0.0 172.9 jit_solution(4048941111502184881)
XLA Ops:
  0.7 1.9 %prepare.1 = (bf16[64,1024]{1,0:T(8,128)(2,1)}, bf16[48,1024]{1,0:T(8,128)(2,1)}, f32[8,384]{1,0:T(8,128)}, f32[384,8]{1,0:T(8,128)}, f32[1,2048]{1,0:T(1,128)}) custom-call(bf16[48,512]{1,0:T(8,128)(2,1)} %one_ref.1, bf16[48,512]{1,0:T(8,128)(2,1)} %bitcast.100, bf16[512]{0:T(512)(128)(2,1)} %hidden_bias_ref.1, bf16[128,384]{1,0:T(8,128)(2,1)} %out_ref.1, ...), custom_call_target="tpu_custom_call" | custom-call | flops 2200000000 | bytes 1024 | tf_op jit(solution)/shard_map/prepare/pallas_call | solution.py:98
  2.5 4.0 %collective-permute-start = (bf16[64,1024]{1,0:T(8,128)(2,1)}, bf16[64,1024]{1,0:T(8,128)(2,1)S(1)}, u32[]{:S(2)}, u32[]{:S(2)}) collective-permute-start(bf16[64,1024]{1,0:T(8,128)(2,1)} %get-tuple-element.75.refs_0_), channel_id=1, source_target_pairs={{0,2},{1,3},{2,0},{3,1},{4,5},{5,4},{6,7},{7,6},{8,10},{9,11},{10,... | collective-permute-start | bytes 393224 | tf_op jit(solution)/shard_map/ppermute | solution.py:731
  6.6 1.5 collective-permute-start.2
  8.1 1.5 collective-permute-start.3
  11.9 1.6 collective-permute-start.1
  14.5 2.1 %collective-permute-done.2.refs_1_ = bf16[48,3072]{1,0:T(8,128)(2,1)S(1)} collective-permute-done((bf16[48,3072]{1,0:T(8,128)(2,1)S(1)}, bf16[48,3072]{1,0:T(8,128)(2,1)S(1)}, u32[]{:S(2)}, u32[]{:S(2)}) %collective-permute-start.2) | collective-permute-done | bytes 294944 | tf_op jit(solution)/shard_map/ppermute | solution.py:721
  16.5 5.0 %collective-permute-done.3.refs_2_ = bf16[48,3072]{1,0:T(8,128)(2,1)S(1)} collective-permute-done((bf16[48,3072]{1,0:T(8,128)(2,1)S(1)}, bf16[48,3072]{1,0:T(8,128)(2,1)S(1)}, u32[]{:S(2)}, u32[]{:S(2)}) %collective-permute-start.3) | collective-permute-done | bytes 294944 | tf_op jit(solution)/shard_map/ppermute | solution.py:721
  24.6 1.3 collective-permute-start.10
  25.9 1.4 collective-permute-start.11
  27.4 23.4 %attend.1 = (bf16[2,640,3072]{2,1,0:T(8,128)(2,1)}, bf16[2,640,1024]{2,1,0:T(8,128)(2,1)}, bf16[2,16,592,640]{3,2,1,0:T(8,128)(2,1)}, f32[2,4,8,640]{3,2,1,0:T(8,128)}, bf16[384,3072]{1,0:T(8,128)(2,1)}) custom-call(s32[1]{0:T(128)} %bitcast.me_ref, bf16[2,640,384]{2,1,0:T(8,128)(2,1)S(1)} %get-tuple-element.79.normed_ref, f32[1,2048]{1,0:T(1,128)S(1)} %copy-done.11, ...), custom_call_target="tpu_custom_call" | custom-call | flops 24199999488 | bytes 1024 | tf_op jit(solution)/shard_map/attend/pallas_call | solution.py:231
  54.3 27.4 %forward.1 = (bf16[1176,384]{1,0:T(8,128)(2,1)}, f32[2,640,384]{2,1,0:T(8,128)S(1)}, bf16[2,640,384]{2,1,0:T(8,128)(2,1)S(1)}, bf16[384,1024]{1,0:T(8,128)(2,1)S...) custom-call(s32[1]{0:T(128)} %bitcast.me_ref, bf16[1176,384]{1,0:T(8,128)(2,1)S(1)} %copy-done.2, ...), custom_call_target="tpu_custom_call" | custom-call | flops 32999999488 | bytes 1024 | tf_op jit(solution)/shard_map/forward/pallas_call | solution.py:434
  82.1 5.5 %mixed_gradient.1 = (bf16[2,640,1024]{2,1,0:T(8,128)(2,1)}, f32[2,4,8,640]{3,2,1,0:T(8,128)}) custom-call(bf16[2,640,384]{2,1,0:T(8,128)(2,1)S(1)} %get-tuple-element.92.branch_ref, bf16[384,1024]{1,0:T(8,128)(2,1)S(1)} %get-tuple-element.93.out_wide_ref, bf16[2,640,1024]{2,1,0:T(8,128)(2,1)S(1)} %copy-done.7), custom_call_target="tpu_custom_call" | custom-call | flops 5500000256 | bytes 1024 | tf_op jit(solution)/shard_map/mixed_gradient/pallas_call | solution.py:495
  89.1 1.4 collective-permute-start.19
  90.4 1.4 collective-permute-start.20
  91.8 26.0 %backward.2 = (bf16[2,640,2304]{2,1,0:T(8,128)(2,1)S(1)}, bf16[4,48,2432]{2,1,0:T(8,128)(2,1)S(1)}, bf16[4,48,2432]{2,1,0:T(8,128)(2,1)S(1)}) custom-call(s32[1]{0:T(128)} %bitcast.me_ref, bf16[2,640,1024]{2,1,0:T(8,128)(2,1)} %get-tuple-element.98.refs_0_, f32[2,4,8,640]{3,2,1,0:T(8,128)} %get-tuple-element.99.refs_1_, bf16[2,640,384]{2,1,0:T(8,128)(2,1)} %copy-done.6, ...), custom_call_target="tpu_custom_call" | custom-call | flops 36300001280 | bytes 1024 | tf_op jit(solution)/shard_map/backward/pallas_call | solution.py:642
  118.4 2.0 %collective-permute-done.17 = bf16[4,48,2432]{2,1,0:T(8,128)(2,1)S(1)} collective-permute-done((bf16[4,48,2432]{2,1,0:T(8,128)(2,1)S(1)}, bf16[4,48,2432]{2,1,0:T(8,128)(2,1)S(1)}, u32[]{:S(2)}, u32[]{:S(2)}) %collective-permute-start.17) | collective-permute-done | bytes 933920 | tf_op jit(solution)/shard_map/ppermute | solution.py:721
  120.7 2.7 %collective-permute-start.21 = (bf16[3,48,1152]{2,1,0:T(8,128)(2,1)S(1)}, bf16[3,48,1152]{2,1,0:T(8,128)(2,1)S(1)}, u32[]{:S(2)}, u32[]{:S(2)}) collective-permute-start(bf16[3,48,1152]{2,1,0:T(8,128)(2,1)S(1)} %pad_maximum_fusion.1), channel_id=1, source_target_pairs={{0,2},{1,3},{2,0},{3,1},{4,5},{5,4},{6,7},{7,6},{8,10},{9,11},{10,... | collective-permute-start | bytes 995336 | tf_op jit(solution)/shard_map/ppermute | solution.py:731
  124.2 1.3 collective-permute-start.23
  125.5 1.4 collective-permute-start.24
  127.0 10.6 %backward.3 = (bf16[2,640,768]{2,1,0:T(8,128)(2,1)S(1)}, bf16[4,48,896]{2,1,0:T(8,128)(2,1)S(1)}, bf16[4,48,896]{2,1,0:T(8,128)(2,1)S(1)}) custom-call(s32[1]{0:T(128)} %bitcast.me_ref, bf16[2,640,1024]{2,1,0:T(8,128)(2,1)} %get-tuple-element.98.refs_0_, f32[2,4,8,640]{3,2,1,0:T(8,128)} %get-tuple-element.99.refs_1_, bf16[2,640,384]{2,1,0:T(8,128)(2,1)} %copy-done.6, ...), custom_call_target="tpu_custom_call" | custom-call | flops 12099999744 | bytes 1024 | tf_op jit(solution)/shard_map/backward/pallas_call | solution.py:642
  138.4 1.1 collective-permute-done.26
  139.7 1.6 collective-permute-start.29
  141.9 1.3 collective-permute-start.27
  143.2 2.3 %collective-permute-done.29 = bf16[48,896]{1,0:T(8,128)(2,1)S(1)} collective-permute-done((bf16[48,896]{1,0:T(8,128)(2,1)S(1)}, bf16[48,896]{1,0:T(8,128)(2,1)S(1)}, u32[]{:S(2)}, u32[]{:S(2)}) %collective-permute-start.29) | collective-permute-done | bytes 86048 | tf_op jit(solution)/shard_map/ppermute | solution.py:721
  145.6 1.5 collective-permute-done.28
  147.8 3.1 %collective-permute-done.25 = bf16[48,4736]{1,0:T(8,128)(2,1)S(1)} collective-permute-done((bf16[48,4736]{1,0:T(8,128)(2,1)S(1)}, bf16[48,4736]{1,0:T(8,128)(2,1)S(1)}, u32[]{:S(2)}, u32[]{:S(2)}) %collective-permute-start.25) | collective-permute-done | bytes 454688 | tf_op jit(solution)/shard_map/ppermute | solution.py:731
  152.9 7.1 %input_gradient.1 = f32[1176,384]{1,0:T(8,128)} custom-call(bf16[1176,384]{1,0:T(8,128)(2,1)S(1)} %copy-done.2, f32[2,640,384]{2,1,0:T(8,128)S(1)} %get-tuple-element.126.middle_grad_ref, f32[8,384]{1,0:T(8,128)S(1)} %copy-done.10, bf16[2,640,2304]{2,1,0:T(8,128)(2,1)S(1)} %get-tuple-element.127.early_ref, ...), custom_call_target="tpu_custom_call" | custom-call | flops 8800000000 | bytes 1024 | tf_op jit(solution)/shard_map/input_gradient/pallas_call | solution.py:699
  161.4 1.6 slice_bitcast_fusion.10
  164.0 1.1 fusion.11
  165.2 1.1 convert_add_fusion.2
  166.4 3.6 %collective-permute-done.31 = bf16[48,896]{1,0:T(8,128)(2,1)S(1)} collective-permute-done((bf16[48,896]{1,0:T(8,128)(2,1)S(1)}, bf16[48,896]{1,0:T(8,128)(2,1)S(1)}, u32[]{:S(2)}, u32[]{:S(2)}) %collective-permute-start.31) | collective-permute-done | bytes 86048 | tf_op jit(solution)/shard_map/ppermute | solution.py:731
  171.6 1.3 concatenate.21
  (130 shorter events, 21.6 us)
Async XLA Ops:
  2.5 8.4 %collective-permute-start = (bf16[64,1024]{1,0:T(8,128)(2,1)}, bf16[64,1024]{1,0:T(8,128)(2,1)S(1)}, u32[]{:S(2)}, u32[]{:S(2)}) collective-permute-start(bf16[64,1024]{1,0:T(8,128)(2,1)} %get-tuple-element.75.refs_0_), channel_id=1, source_target_pairs={{0,2},{1,3},{2,0},{3,1},{4,5},{5,4},{6,7},{7,6},{8,10},{9,11},{10,... | collective-permute-start | bytes 393224 | tf_op jit(solution)/shard_map/ppermute | solution.py:731
  6.6 9.9 %collective-permute-start.2 = (bf16[48,3072]{1,0:T(8,128)(2,1)S(1)}, bf16[48,3072]{1,0:T(8,128)(2,1)S(1)}, u32[]{:S(2)}, u32[]{:S(2)}) collective-permute-start(bf16[48,3072]{1,0:T(8,128)(2,1)S(1)} %copy-done.3), channel_id=1, source_target_pairs={{0,8},{4,12},{8,0},{12,4},{16,24},{20,28},{24,16},{28,20},{1,9},{5... | collective-permute-start | bytes 884744 | tf_op jit(solution)/shard_map/ppermute | solution.py:721
  8.1 13.5 %collective-permute-start.3 = (bf16[48,3072]{1,0:T(8,128)(2,1)S(1)}, bf16[48,3072]{1,0:T(8,128)(2,1)S(1)}, u32[]{:S(2)}, u32[]{:S(2)}) collective-permute-start(bf16[48,3072]{1,0:T(8,128)(2,1)S(1)} %copy-done.3), channel_id=1, source_target_pairs={{0,16},{4,20},{8,24},{12,28},{16,0},{20,4},{24,8},{28,12},{1,17},{... | collective-permute-start | bytes 884744 | tf_op jit(solution)/shard_map/ppermute | solution.py:721
  9.6 12.0 %collective-permute-start.4 = (bf16[48,3072]{1,0:T(8,128)(2,1)S(1)}, bf16[48,3072]{1,0:T(8,128)(2,1)S(1)}, u32[]{:S(2)}, u32[]{:S(2)}) collective-permute-start(bf16[48,3072]{1,0:T(8,128)(2,1)S(1)} %copy-done.3), channel_id=1, source_target_pairs={{0,24},{4,28},{8,16},{12,20},{16,8},{20,12},{24,0},{28,4},{1,25},{... | collective-permute-start | bytes 884744 | tf_op jit(solution)/shard_map/ppermute | solution.py:721
  10.1 14.5 %collective-permute-start.5 = (bf16[48,3072]{1,0:T(8,128)(2,1)S(1)}, bf16[48,3072]{1,0:T(8,128)(2,1)S(1)}, u32[]{:S(2)}, u32[]{:S(2)}) collective-permute-start(bf16[48,3072]{1,0:T(8,128)(2,1)S(1)} %copy-done.3), channel_id=1, source_target_pairs={{0,4},{4,0},{8,12},{12,8},{16,20},{20,16},{24,28},{28,24},{1,5},{5... | collective-permute-start | bytes 884744 | tf_op jit(solution)/shard_map/ppermute | solution.py:721
  11.9 11.8 %collective-permute-start.1 = (bf16[2,64,1024]{2,1,0:T(8,128)(2,1)S(1)}, bf16[2,64,1024]{2,1,0:T(8,128)(2,1)S(1)}, u32[]{:S(2)}, u32[]{:S(2)}) collective-permute-start(bf16[2,64,1024]{2,1,0:T(8,128)(2,1)S(1)} %pad_maximum_fusion.3), channel_id=1, source_target_pairs={{0,1},{1,0},{2,3},{3,2},{4,6},{5,7},{6,4},{7,5},{8,9},{9,8},{10,11... | collective-permute-start | bytes 786440 | tf_op jit(solution)/shard_map/ppermute | solution.py:731
  16.5 9.4 %collective-permute-start.6 = (bf16[48,3072]{1,0:T(8,128)(2,1)S(1)}, bf16[48,3072]{1,0:T(8,128)(2,1)S(1)}, u32[]{:S(2)}, u32[]{:S(2)}) collective-permute-start(bf16[48,3072]{1,0:T(8,128)(2,1)S(1)} %collective-permute-done.2.refs_1_), channel_id=1, source_target_pairs={{0,4},{4,0},{8,12},{12,8},{16,20},{20,16},{24,28},{28,24},{1,5},{5... | collective-permute-start | bytes 884744 | tf_op jit(solution)/shard_map/ppermute | solution.py:721
  21.6 5.8 %collective-permute-start.7 = (bf16[48,3072]{1,0:T(8,128)(2,1)S(1)}, bf16[48,3072]{1,0:T(8,128)(2,1)S(1)}, u32[]{:S(2)}, u32[]{:S(2)}) collective-permute-start(bf16[48,3072]{1,0:T(8,128)(2,1)S(1)} %collective-permute-done.3.refs_2_), channel_id=1, source_target_pairs={{0,4},{4,0},{8,12},{12,8},{16,20},{20,16},{24,28},{28,24},{1,5},{5... | collective-permute-start | bytes 884744 | tf_op jit(solution)/shard_map/ppermute | solution.py:721
  21.6 5.8 %collective-permute-start.8 = (bf16[48,3072]{1,0:T(8,128)(2,1)S(1)}, bf16[48,3072]{1,0:T(8,128)(2,1)S(1)}, u32[]{:S(2)}, u32[]{:S(2)}) collective-permute-start(bf16[48,3072]{1,0:T(8,128)(2,1)S(1)} %collective-permute-done.4.refs_3_), channel_id=1, source_target_pairs={{0,4},{4,0},{8,12},{12,8},{16,20},{20,16},{24,28},{28,24},{1,5},{5... | collective-permute-start | bytes 884744 | tf_op jit(solution)/shard_map/ppermute | solution.py:721
  23.8 27.0 %collective-permute-start.9 = (bf16[48,5120]{1,0:T(8,128)(2,1)S(1)}, bf16[48,5120]{1,0:T(8,128)(2,1)S(1)}, u32[]{:S(2)}, u32[]{:S(2)}) collective-permute-start(bf16[48,5120]{1,0:T(8,128)(2,1)S(1)} %fusion.13.refs_5_), channel_id=1, source_target_pairs={{0,8},{4,12},{8,0},{12,4},{16,24},{20,28},{24,16},{28,20},{1,9},{5... | collective-permute-start | bytes 1474568 | tf_op jit(solution)/shard_map/ppermute | solution.py:721
  24.6 26.2 %collective-permute-start.10 = (bf16[48,5120]{1,0:T(8,128)(2,1)S(1)}, bf16[48,5120]{1,0:T(8,128)(2,1)S(1)}, u32[]{:S(2)}, u32[]{:S(2)}) collective-permute-start(bf16[48,5120]{1,0:T(8,128)(2,1)S(1)} %fusion.13.refs_5_), channel_id=1, source_target_pairs={{0,16},{4,20},{8,24},{12,28},{16,0},{20,4},{24,8},{28,12},{1,17},{... | collective-permute-start | bytes 1474568 | tf_op jit(solution)/shard_map/ppermute | solution.py:721
  25.9 24.9 %collective-permute-start.11 = (bf16[48,5120]{1,0:T(8,128)(2,1)S(1)}, bf16[48,5120]{1,0:T(8,128)(2,1)S(1)}, u32[]{:S(2)}, u32[]{:S(2)}) collective-permute-start(bf16[48,5120]{1,0:T(8,128)(2,1)S(1)} %fusion.13.refs_5_), channel_id=1, source_target_pairs={{0,24},{4,28},{8,16},{12,20},{16,8},{20,12},{24,0},{28,4},{1,25},{... | collective-permute-start | bytes 1474568 | tf_op jit(solution)/shard_map/ppermute | solution.py:721
  27.3 23.5 %collective-permute-start.12 = (bf16[48,5120]{1,0:T(8,128)(2,1)S(1)}, bf16[48,5120]{1,0:T(8,128)(2,1)S(1)}, u32[]{:S(2)}, u32[]{:S(2)}) collective-permute-start(bf16[48,5120]{1,0:T(8,128)(2,1)S(1)} %fusion.13.refs_5_), channel_id=1, source_target_pairs={{0,4},{4,0},{8,12},{12,8},{16,20},{20,16},{24,28},{28,24},{1,5},{5... | collective-permute-start | bytes 1474568 | tf_op jit(solution)/shard_map/ppermute | solution.py:721
  50.8 2.0 %collective-permute-start.13 = (bf16[48,5120]{1,0:T(8,128)(2,1)S(1)}, bf16[48,5120]{1,0:T(8,128)(2,1)S(1)}, u32[]{:S(2)}, u32[]{:S(2)}) collective-permute-start(bf16[48,5120]{1,0:T(8,128)(2,1)S(1)} %collective-permute-done.9.refs_6_), channel_id=1, source_target_pairs={{0,4},{4,0},{8,12},{12,8},{16,20},{20,16},{24,28},{28,24},{1,5},{5... | collective-permute-start | bytes 1474568 | tf_op jit(solution)/shard_map/ppermute | solution.py:721
  51.4 2.2 %collective-permute-start.14 = (bf16[48,5120]{1,0:T(8,128)(2,1)S(1)}, bf16[48,5120]{1,0:T(8,128)(2,1)S(1)}, u32[]{:S(2)}, u32[]{:S(2)}) collective-permute-start(bf16[48,5120]{1,0:T(8,128)(2,1)S(1)} %collective-permute-done.10.refs_7_), channel_id=1, source_target_pairs={{0,4},{4,0},{8,12},{12,8},{16,20},{20,16},{24,28},{28,24},{1,5},{5... | collective-permute-start | bytes 1474568 | tf_op jit(solution)/shard_map/ppermute | solution.py:721
  51.5 2.8 %collective-permute-start.15 = (bf16[48,5120]{1,0:T(8,128)(2,1)S(1)}, bf16[48,5120]{1,0:T(8,128)(2,1)S(1)}, u32[]{:S(2)}, u32[]{:S(2)}) collective-permute-start(bf16[48,5120]{1,0:T(8,128)(2,1)S(1)} %collective-permute-done.11.refs_8_), channel_id=1, source_target_pairs={{0,4},{4,0},{8,12},{12,8},{16,20},{20,16},{24,28},{28,24},{1,5},{5... | collective-permute-start | bytes 1474568 | tf_op jit(solution)/shard_map/ppermute | solution.py:721
  81.7 5.8 %collective-permute-start.16 = (bf16[4,5,48,1152]{3,2,1,0:T(8,128)(2,1)S(1)}, bf16[4,5,48,1152]{3,2,1,0:T(8,128)(2,1)S(1)}, u32[]{:S(2)}, u32[]{:S(2)}) collective-permute-start(bf16[4,5,48,1152]{3,2,1,0:T(8,128)(2,1)S(1)} %get-tuple-element.95), channel_id=1, source_target_pairs={{0,4},{4,0},{8,12},{12,8},{16,20},{20,16},{24,28},{28,24},{1,5},{5... | collective-permute-start | bytes 6635528 | tf_op jit(solution)/shard_map/ppermute | solution.py:721
  88.3 29.7 %collective-permute-start.18 = (bf16[5,48,1152]{2,1,0:T(8,128)(2,1)S(1)}, bf16[5,48,1152]{2,1,0:T(8,128)(2,1)S(1)}, u32[]{:S(2)}, u32[]{:S(2)}) collective-permute-start(bf16[5,48,1152]{2,1,0:T(8,128)(2,1)S(1)} %get-tuple-element.150), channel_id=1, source_target_pairs={{0,8},{4,12},{8,0},{12,4},{16,24},{20,28},{24,16},{28,20},{1,9},{5... | collective-permute-start | bytes 1658888 | tf_op jit(solution)/shard_map/ppermute | solution.py:721
  89.1 28.9 %collective-permute-start.19 = (bf16[5,48,1152]{2,1,0:T(8,128)(2,1)S(1)}, bf16[5,48,1152]{2,1,0:T(8,128)(2,1)S(1)}, u32[]{:S(2)}, u32[]{:S(2)}) collective-permute-start(bf16[5,48,1152]{2,1,0:T(8,128)(2,1)S(1)} %get-tuple-element.149), channel_id=1, source_target_pairs={{0,16},{4,20},{8,24},{12,28},{16,0},{20,4},{24,8},{28,12},{1,17},{... | collective-permute-start | bytes 1658888 | tf_op jit(solution)/shard_map/ppermute | solution.py:721
  90.4 27.5 %collective-permute-start.20 = (bf16[5,48,1152]{2,1,0:T(8,128)(2,1)S(1)}, bf16[5,48,1152]{2,1,0:T(8,128)(2,1)S(1)}, u32[]{:S(2)}, u32[]{:S(2)}) collective-permute-start(bf16[5,48,1152]{2,1,0:T(8,128)(2,1)S(1)} %get-tuple-element.148), channel_id=1, source_target_pairs={{0,24},{4,28},{8,16},{12,20},{16,8},{20,12},{24,0},{28,4},{1,25},{... | collective-permute-start | bytes 1658888 | tf_op jit(solution)/shard_map/ppermute | solution.py:721
  117.9 2.6 %collective-permute-start.17 = (bf16[4,48,2432]{2,1,0:T(8,128)(2,1)S(1)}, bf16[4,48,2432]{2,1,0:T(8,128)(2,1)S(1)}, u32[]{:S(2)}, u32[]{:S(2)}) collective-permute-start(bf16[4,48,2432]{2,1,0:T(8,128)(2,1)S(1)} %get-tuple-element.107), channel_id=1, source_target_pairs={{0,4},{4,0},{8,12},{12,8},{16,20},{20,16},{24,28},{28,24},{1,5},{5... | collective-permute-start | bytes 2801672 | tf_op jit(solution)/shard_map/ppermute | solution.py:721
  120.7 16.9 %collective-permute-start.21 = (bf16[3,48,1152]{2,1,0:T(8,128)(2,1)S(1)}, bf16[3,48,1152]{2,1,0:T(8,128)(2,1)S(1)}, u32[]{:S(2)}, u32[]{:S(2)}) collective-permute-start(bf16[3,48,1152]{2,1,0:T(8,128)(2,1)S(1)} %pad_maximum_fusion.1), channel_id=1, source_target_pairs={{0,2},{1,3},{2,0},{3,1},{4,5},{5,4},{6,7},{7,6},{8,10},{9,11},{10,... | collective-permute-start | bytes 995336 | tf_op jit(solution)/shard_map/ppermute | solution.py:731
  123.4 14.1 %collective-permute-start.22 = (bf16[48,2432]{1,0:T(8,128)(2,1)S(1)}, bf16[48,2432]{1,0:T(8,128)(2,1)S(1)}, u32[]{:S(2)}, u32[]{:S(2)}) collective-permute-start(bf16[48,2432]{1,0:T(8,128)(2,1)S(1)} %get-tuple-element.157), channel_id=1, source_target_pairs={{0,8},{4,12},{8,0},{12,4},{16,24},{20,28},{24,16},{28,20},{1,9},{5... | collective-permute-start | bytes 700424 | tf_op jit(solution)/shard_map/ppermute | solution.py:721
  124.2 13.3 %collective-permute-start.23 = (bf16[48,2432]{1,0:T(8,128)(2,1)S(1)}, bf16[48,2432]{1,0:T(8,128)(2,1)S(1)}, u32[]{:S(2)}, u32[]{:S(2)}) collective-permute-start(bf16[48,2432]{1,0:T(8,128)(2,1)S(1)} %get-tuple-element.156), channel_id=1, source_target_pairs={{0,16},{4,20},{8,24},{12,28},{16,0},{20,4},{24,8},{28,12},{1,17},{... | collective-permute-start | bytes 700424 | tf_op jit(solution)/shard_map/ppermute | solution.py:721
  125.5 12.0 %collective-permute-start.24 = (bf16[48,2432]{1,0:T(8,128)(2,1)S(1)}, bf16[48,2432]{1,0:T(8,128)(2,1)S(1)}, u32[]{:S(2)}, u32[]{:S(2)}) collective-permute-start(bf16[48,2432]{1,0:T(8,128)(2,1)S(1)} %get-tuple-element.155), channel_id=1, source_target_pairs={{0,24},{4,28},{8,16},{12,20},{16,8},{20,12},{24,0},{28,4},{1,25},{... | collective-permute-start | bytes 700424 | tf_op jit(solution)/shard_map/ppermute | solution.py:721
  137.8 1.7 collective-permute-start.26
  137.9 13.0 %collective-permute-start.25 = (bf16[48,4736]{1,0:T(8,128)(2,1)S(1)}, bf16[48,4736]{1,0:T(8,128)(2,1)S(1)}, u32[]{:S(2)}, u32[]{:S(2)}) collective-permute-start(bf16[48,4736]{1,0:T(8,128)(2,1)S(1)} %pad_maximum_fusion), channel_id=1, source_target_pairs={{0,1},{1,0},{2,3},{3,2},{4,6},{5,7},{6,4},{7,5},{8,9},{9,8},{10,11... | collective-permute-start | bytes 1363976 | tf_op jit(solution)/shard_map/ppermute | solution.py:731
  139.7 5.9 %collective-permute-start.29 = (bf16[48,896]{1,0:T(8,128)(2,1)S(1)}, bf16[48,896]{1,0:T(8,128)(2,1)S(1)}, u32[]{:S(2)}, u32[]{:S(2)}) collective-permute-start(bf16[48,896]{1,0:T(8,128)(2,1)S(1)} %get-tuple-element.167), channel_id=1, source_target_pairs={{0,24},{4,28},{8,16},{12,20},{16,8},{20,12},{24,0},{28,4},{1,25},{... | collective-permute-start | bytes 258056 | tf_op jit(solution)/shard_map/ppermute | solution.py:721
  141.2 5.8 %collective-permute-start.28 = (bf16[48,896]{1,0:T(8,128)(2,1)S(1)}, bf16[48,896]{1,0:T(8,128)(2,1)S(1)}, u32[]{:S(2)}, u32[]{:S(2)}) collective-permute-start(bf16[48,896]{1,0:T(8,128)(2,1)S(1)} %get-tuple-element.168), channel_id=1, source_target_pairs={{0,16},{4,20},{8,24},{12,28},{16,0},{20,4},{24,8},{28,12},{1,17},{... | collective-permute-start | bytes 258056 | tf_op jit(solution)/shard_map/ppermute | solution.py:721
  141.9 5.2 %collective-permute-start.27 = (bf16[48,896]{1,0:T(8,128)(2,1)S(1)}, bf16[48,896]{1,0:T(8,128)(2,1)S(1)}, u32[]{:S(2)}, u32[]{:S(2)}) collective-permute-start(bf16[48,896]{1,0:T(8,128)(2,1)S(1)} %get-tuple-element.166), channel_id=1, source_target_pairs={{0,8},{4,12},{8,0},{12,4},{16,24},{20,28},{24,16},{28,20},{1,9},{5... | collective-permute-start | bytes 258056 | tf_op jit(solution)/shard_map/ppermute | solution.py:721
  152.6 11.5 %collective-permute-start.30 = (bf16[48,3328]{1,0:T(8,128)(2,1)}, bf16[48,3328]{1,0:T(8,128)(2,1)}, u32[]{:S(2)}, u32[]{:S(2)}) collective-permute-start(bf16[48,3328]{1,0:T(8,128)(2,1)} %pad_maximum_fusion.2), channel_id=1, source_target_pairs={{0,2},{1,3},{2,0},{3,1},{4,5},{5,4},{6,7},{7,6},{8,10},{9,11},{10,... | collective-permute-start | bytes 958472 | tf_op jit(solution)/shard_map/ppermute | solution.py:731
  165.1 4.8 %collective-permute-start.31 = (bf16[48,896]{1,0:T(8,128)(2,1)S(1)}, bf16[48,896]{1,0:T(8,128)(2,1)S(1)}, u32[]{:S(2)}, u32[]{:S(2)}) collective-permute-start(bf16[48,896]{1,0:T(8,128)(2,1)S(1)} %fusion.11), channel_id=1, source_target_pairs={{0,1},{1,0},{2,3},{3,2},{4,6},{5,7},{6,4},{7,5},{8,9},{9,8},{10,11... | collective-permute-start | bytes 258056 | tf_op jit(solution)/shard_map/ppermute | solution.py:731
  (20 other events, 210.8 us)

commit v2 on v1

--- a/solution.py
+++ b/solution.py
@@ -67,6 +67,15 @@
 
 def owners(me, count):
     return [me ^ mask for mask in MASKS[:count]]
+
+
+def staged_owners(me, count):
+    if count == 1:
+        return [0]
+    first = 2 + 2 * (me & 1)
+    second = 6 - first
+    other = me ^ 1
+    return [me, me ^ first, me ^ second, me ^ 6, other, other ^ second, other ^ first, other ^ 6]
 
 
 def whole(shape):
@@ -140,7 +149,7 @@
     @pl.when((group == 0) & (seq == 0))
     def _():
         rows = D // pieces
-        for j, owner in enumerate(owners(me_ref[0], pieces)):
+        for j, owner in enumerate(staged_owners(me_ref[0], pieces)):
             to = pl.ds(pl.multiple_of(owner * rows, 16), rows)
             for g in range(GROUPS):
                 for k in range(3):
@@ -173,7 +182,6 @@
     from_ref = projected_ref.at[0]
 
     lane = lax.broadcasted_iota(jnp.int32, (1, 128), 1)
-    row = lax.broadcasted_iota(jnp.int32, (128, 1), 0)
     units = [(h, b) for h in range(GROUP) for b in QUERY_BLOCKS]
 
     largest = {}
@@ -187,13 +195,13 @@
         own_keys = jnp.where(mine, own_keys, bf16(0))
         score = dot(own_keys, from_ref[start : start + width, pair : pair + 128], NT)
         score = score + hide_scr[seq, :keys, start : start + width]
-        score_scr[unit % 2, :keys, :width] = score
+        score_scr[unit % 3, :keys, :width] = score
         top = jnp.max(score.reshape(-1, 8, width), axis=0)
         largest[unit] = jnp.max(top, axis=0, keepdims=True)
 
     def exponents(unit):
         head, (start, width, keys) = units[unit]
-        exponent = jnp.exp(score_scr[unit % 2, :keys, :width] - largest[unit])
+        exponent = jnp.exp(score_scr[unit % 3, :keys, :width] - largest[unit])
         exp_ref[0, head, :keys, start : start + width] = exponent.astype(bf16)
 
     def mix(unit):
@@ -201,27 +209,26 @@
         pair = head // 2 * 128
         if head not in flipped:
             turned = from_ref[:KEYS, 2 * WIDE + pair : 2 * WIDE + pair + 128].T
-            mine = (row < 64) if head % 2 == 0 else (row >= 64)
-            flipped[head] = jnp.where(mine, turned, bf16(1))
+            side = head % 2 * 64
+            ones = jnp.ones((16, KEYS), bf16)
+            flipped[head] = jnp.concatenate([turned[side : side + 64], ones])
         exponent = exp_ref[0, head, :keys, start : start + width]
         summed = dot(flipped[head][:, :keys], exponent, NN)
-        if head % 2 == 0:
-            values, total = summed[:64], summed[64:65]
-        else:
-            values, total = summed[64:], summed[0:1]
+        values, total = summed[:64], summed[64:65]
         inverse = 1.0 / total
         mixed_scr[head * 64 : (head + 1) * 64, start : start + width] = values * inverse
         total_scr[head : head + 1, start : start + width] = inverse
 
     count = len(units)
     scores(0)
-    for unit in range(count + 1):
-        if unit + 1 < count:
-            scores(unit + 1)
+    scores(1)
+    for unit in range(count + 2):
+        if unit + 2 < count:
+            scores(unit + 2)
         if unit < count:
             exponents(unit)
-        if unit > 0:
-            mix(unit - 1)
+        if unit > 1:
+            mix(unit - 2)
     mixed_ref[0] = mixed_scr[...].T.astype(bf16)
     inverse_ref[0, 0] = total_scr[...]
 
@@ -254,7 +261,7 @@
         ],
         scratch_shapes=[
             pltpu.VMEM((seqs, KEYS, ROWS), f32),
-            pltpu.VMEM((2, KEYS, 256), f32),
+            pltpu.VMEM((3, KEYS, 256), f32),
             pltpu.VMEM((WIDE, ROWS), f32),
             pltpu.VMEM((8, ROWS), f32),
             pltpu.VMEM((8, ROWS), f32),
@@ -666,59 +673,151 @@
             pltpu.VMEM((8, QKV), f32),
             pltpu.VMEM((D, 128), f32),
         ],
-        compiler_params=pltpu.CompilerParams(vmem_limit_bytes=20 * 1024 * 1024),
+        compiler_params=pltpu.CompilerParams(vmem_limit_bytes=23 * 1024 * 1024),
         cost_estimate=cost(11 * groups),
         name="backward",
     )(me, *operands, norm)
 
 
-def input_kernel(tokens_ref, middle_grad_ref, rows_ref, early_ref, late_ref, wide_ref, out_ref, sum_scr):
-    step, last = pl.program_id(0), pl.num_programs(0) - 1
-    seqs = middle_grad_ref.shape[0]
-
-    @pl.when(step < last)
-    def _():
-        for s in range(seqs):
-            grad = dot(early_ref[s, :KEYS], wide_ref[...], NT)
-            sum_scr[s] = jnp.where(step == 0, grad, sum_scr[s] + grad)
-
-    @pl.when(step == last)
-    def _():
-        for s in range(seqs):
-            grad_first = sum_scr[s] + dot(late_ref[s, :KEYS], wide_ref[...], NT)
-            given = slice(s * LEN, (s + 1) * LEN)
-            scaled, inverse = normalize(tokens_ref[given].astype(f32))
-            out_ref[given] = middle_grad_ref[s, :LEN] + normalize_back(
-                grad_first[:LEN], rows_ref[GAIN_ONE], scaled, inverse
-            )
-
-
-def input_gradient(tokens, middle_grad, rows_in, early, late, weights):
-    seqs = middle_grad.shape[0]
-    block = (seqs, ROWS, QKV)
+def early_kernel(back_ref, wide_ref, out_ref):
+    for s in range(out_ref.shape[0]):
+        grad = dot(back_ref[s, :KEYS], wide_ref[...], NT)
+        before = jnp.where(pl.program_id(0) == 0, 0.0, out_ref[s])
+        out_ref[s] = before + grad
+
+
+def early_gradient(back, weights):
+    seqs, groups = back.shape[0], back.shape[2] // QKV
+    return pl.pallas_call(
+        early_kernel,
+        grid=(groups,),
+        in_specs=[
+            pl.BlockSpec((seqs, ROWS, QKV), lambda g: (0, 0, g)),
+            pl.BlockSpec((D, QKV), lambda g: (0, g)),
+        ],
+        out_specs=whole((seqs, KEYS, D)),
+        out_shape=jax.ShapeDtypeStruct((seqs, KEYS, D), f32),
+        compiler_params=pltpu.CompilerParams(vmem_limit_bytes=14 * 1024 * 1024),
+        cost_estimate=cost(5),
+        name="early_gradient",
+    )(back, weights)
+
+
+def input_kernel(tokens_ref, middle_grad_ref, rows_ref, early_ref, back_ref, wide_ref, out_ref):
+    for s in range(middle_grad_ref.shape[0]):
+        grad_first = early_ref[s] + dot(back_ref[s, :KEYS], wide_ref[...], NT)
+        given = slice(s * LEN, (s + 1) * LEN)
+        scaled, inverse = normalize(tokens_ref[given].astype(f32))
+        out_ref[given] = middle_grad_ref[s, :LEN] + normalize_back(
+            grad_first[:LEN], rows_ref[GAIN_ONE], scaled, inverse
+        )
+
+
+def input_gradient(tokens, middle_grad, rows_in, early, back, weights):
     return pl.pallas_call(
         input_kernel,
-        grid=(GROUPS,),
+        grid=(1,),
         in_specs=[
             whole(tokens.shape),
             whole(middle_grad.shape),
             whole(rows_in.shape),
-            pl.BlockSpec(block, lambda g: (0, 0, jnp.minimum(g, GROUPS - 2))),
-            whole(block),
-            pl.BlockSpec((D, QKV), lambda g: (0, g)),
+            whole(early.shape),
+            whole(back.shape),
+            pl.BlockSpec((D, QKV), lambda g: (0, GROUPS - 1)),
         ],
         out_specs=whole(tokens.shape),
         out_shape=jax.ShapeDtypeStruct(tokens.shape, f32),
-        scratch_shapes=[pltpu.VMEM((seqs, KEYS, D), f32)],
         compiler_params=pltpu.CompilerParams(vmem_limit_bytes=16 * 1024 * 1024),
-        cost_estimate=cost(8),
+        cost_estimate=cost(4),
         name="input_gradient",
-    )(tokens, middle_grad, rows_in, early, late, weights)
+    )(tokens, middle_grad, rows_in, early, back, weights)
+
+
+def join_lines(values):
+    return jnp.concatenate([values[k : k + 1] for k in range(values.shape[0])], axis=1)
+
+
+def hidden_end_kernel(block_ref, rest_ref, arrived_ref, one_ref, two_ref, bias_ref, out_ref, *refs):
+    rows, slot = one_ref.shape
+    block = block_ref[...] + arrived_ref[:, :BLOCK].astype(f32)
+    rest = rest_ref[...] + arrived_ref[:, BLOCK:].astype(f32)
+    one_ref[...] = block[:, :slot]
+    two_ref[...] = block[:, slot : 2 * slot]
+    bias_ref[...] = join_lines(block[: slot // 128, INNER:]).reshape(slot)
+    width = out_ref.shape[0]
+    parts = [rest[:, r * width : (r + 1) * width] for r in range(INNER // width)]
+    out_ref[...] = jnp.concatenate(parts, axis=0).T
+    for k, ref in enumerate(refs):
+        ref[...] = join_lines(rest[3 * k : 3 * k + 3, INNER:]).reshape(D)
+
+
+def hidden_end(block, rest, arrived, slot):
+    rows = block.shape[0]
+    width = INNER // (D // rows)
+    vector = jax.ShapeDtypeStruct((D,), f32)
+    return pl.pallas_call(
+        hidden_end_kernel,
+        out_shape=[
+            jax.ShapeDtypeStruct((rows, slot), f32),
+            jax.ShapeDtypeStruct((rows, slot), f32),
+            jax.ShapeDtypeStruct((slot,), f32),
+            jax.ShapeDtypeStruct((width, D), f32),
+        ]
+        + [vector] * 4,
+        compiler_params=pltpu.CompilerParams(vmem_limit_bytes=8 * 1024 * 1024),
+        cost_estimate=cost(2),
+        name="hidden_end",
+    )(block, rest, arrived)
+
+
+def heads_end_kernel(early_ref, early_line_ref, late_ref, late_line_ref, weight_ref, bias_ref, *refs):
+    early = early_ref[...] + early_line_ref[...].astype(f32)
+    late = late_ref[...] + late_line_ref[...].astype(f32)
+    lines = WIDE // 128
+    norms, group = 0.0, 0
+    for part in (early, late):
+        edge = part.shape[1] - SMALL
+        for g in range(edge // QKV):
+            for k in range(3):
+                left = g * QKV + k * WIDE
+                to = k * INNER + group * WIDE
+                weight_ref[:, to : to + WIDE] = part[:, left : left + WIDE]
+            for k in range(2):
+                first = (2 * g + k) * lines
+                values = join_lines(part[first : first + lines, edge:])
+                at = k * INNER + group * WIDE
+                bias_ref[at : at + WIDE] = values.reshape(WIDE)
+            group += 1
+        norms = norms + part[40:48, edge:]
+    for k, ref in enumerate(refs):
+        ref[...] = join_lines(norms[3 * k : 3 * k + 3]).reshape(D)
+
+
+def heads_end(early, early_line, late, late_line):
+    vector = jax.ShapeDtypeStruct((D,), f32)
+    return pl.pallas_call(
+        heads_end_kernel,
+        out_shape=[
+            jax.ShapeDtypeStruct((early.shape[0], 3 * INNER), f32),
+            jax.ShapeDtypeStruct((2 * INNER,), f32),
+            vector,
+            vector,
+        ],
+        compiler_params=pltpu.CompilerParams(vmem_limit_bytes=8 * 1024 * 1024),
+        cost_estimate=cost(2),
+        name="heads_end",
+    )(early, early_line, late, late_line)
 
 
 def swap(values, mask):
     size = lax.axis_size("tok")
     return lax.ppermute(values, "tok", [(i, i ^ mask) for i in range(size)])
+
+
+def swap_half_plane(values, stage):
+    size = lax.axis_size("tok")
+    pairs = [(t, t ^ (2 if (t % 2 == 0) == (stage == 0) else 4)) for t in range(size)]
+    return lax.ppermute(values, "tok", pairs)
 
 
 def swap_half_line(values, stage):
@@ -777,7 +876,8 @@
     vectors = (bias_out, ln2_gain, ln2_bias, bias_fc2, ln1_gain, ln1_bias)
     me_a = me
     if fast:
-        first_near = [swap(w_qkv, mask) for mask in chips]
+        first_near = [swap_half_plane(w_qkv, stage) for stage in (0, 1)]
+        first_near.append(swap_half_plane(first_near[0], 1))
         first_other = swap(w_qkv, 1)
         hidden_pack, out_block, rows_in, columns_in, bias_pair = prepare(
             w_fc1, w_fc2, bias_fc1, w_out, bias_qv, vectors
@@ -824,7 +924,8 @@
     if not fast:
         back_a, sends_a = back(me, 0, 3)
         back_b, sends_b = back(me, 3, 1)
-        input_grad = input_gradient(tokens, middle_grad, rows_in, back_a, back_b, weights)
+        early = early_gradient(back_a, weights)
+        input_grad = input_gradient(tokens, middle_grad, rows_in, early, back_b, weights)
         return slow_end(output, input_grad, hidden_sends[0], (sends_a, sends_b), slot)
 
     arrived = swap(hidden_sends[1], 1)
@@ -845,39 +946,51 @@
 
     back_b, line_1, *near_a = after(back_b, line_1, *near_a)
     total_a = wide(group_a[0]) + wide(near_a[0]) + wide(near_a[1]) + wide(near_a[2])
+    sent, kept_b, sent_b = after(total_a.astype(bf16), *sends_b)
+    line_a = swap_half_line(sent, 1)
+    group_b = join(kept_b, swap(sent_b, 1))
+    line_1, group_b = after(line_1, group_b)
     block = hidden[0] + wide(line_1[0])
     middle_block = pick(hidden[2], hidden[1]) + wide(line_1[1])
     rest = hidden[4] + wide(line_1[2])
-    sent = jnp.concatenate([middle_block, rest, total_a], axis=1).astype(bf16)
-    sent, kept_b, sent_b = after(sent, *sends_b)
+    sent = jnp.concatenate([middle_block, rest], axis=1).astype(bf16)
+    group_b, sent = after(group_b, sent)
     line_2 = swap_half_line(sent, 1)
-    group_b = join(kept_b, swap(sent_b, 1))
     near_b = [swap(group_b[k], chips[k - 1]) for k in (1, 2, 3)]
-    block = block + wide(line_2[:, :BLOCK])
-    rest = rest + wide(line_2[:, BLOCK : 2 * BLOCK])
-    total_a = total_a + wide(line_2[:, 2 * BLOCK :])
+    line_a, *near_b = after(line_a, *near_b)
     total_b = wide(group_b[0]) + wide(near_b[0]) + wide(near_b[1]) + wide(near_b[2])
-    edge = total_a.shape[1]
-    sent = jnp.concatenate([total_a, total_b], axis=1).astype(bf16)
-    middle_grad, sent, block, rest = after(middle_grad, sent, block, rest)
-    line_3 = swap_half_line(sent, 0)
-    input_grad = input_gradient(tokens, middle_grad, rows_in, back_a, back_b, weights)
-
-    input_grad, line_3 = after(input_grad, line_3)
-    total_a = total_a + wide(line_3[:, :edge])
-    total_b = total_b + wide(line_3[:, edge:])
-    total_b = total_b + wide(swap_half_line(total_b, 1))
-
-    out_rows = rest[:, :INNER].reshape(rows, tok, -1).transpose(1, 0, 2).reshape(D, -1).T
-    return results(
+    total_a = total_a + wide(line_a)
+    back_a, sent_b, sent_a = after(back_a, total_b.astype(bf16), total_a.astype(bf16))
+    line_b = swap_half_line(sent_b, 0)
+    line_a = swap_half_line(sent_a, 0)
+    early = early_gradient(back_a, weights)
+
+    early, line_b = after(early, line_b)
+    total_b = total_b + wide(line_b)
+    early, sent = after(early, total_b.astype(bf16))
+    line_b = swap_half_line(sent, 1)
+    input_grad = input_gradient(tokens, middle_grad, rows_in, early, back_b, weights)
+
+    input_grad, line_a, line_b, line_2 = after(input_grad, line_a, line_b, line_2)
+    hidden_grads = hidden_end(block, rest, line_2, slot)
+    one_grad = hidden_grads[0]
+    qkv_grad, bias_grad, gain_grad, shift_grad = heads_end(total_a, line_a, total_b, line_b)
+    _, two_grad, hidden_bias_grad, out_rows, *vector_grads = hidden_grads
+    return (
         output,
         input_grad,
-        [total_a[:, :-SMALL], total_b[:, :-SMALL]],
-        [total_a[:, -SMALL:], total_b[:, -SMALL:]],
+        gain_grad,
+        shift_grad,
+        qkv_grad,
+        bias_grad,
         out_rows,
-        rest[:, INNER:],
-        block[:, :INNER],
-        block[: slot // 128, INNER:],
+        vector_grads[2],
+        vector_grads[0],
+        vector_grads[1],
+        one_grad,
+        hidden_bias_grad,
+        two_grad.T,
+        vector_grads[3],
     )
 
 

time: 173 us -> 163 us (0.942)
  waiting for transfers between devices: 24.2 us -> 17.6 us
  local copies, waits for them, and re-layouts: 9.02 us -> 2.83 us
  starting transfers between devices: 29.1 us -> 34.9 us
  other arithmetic: 6.74 us -> 2.77 us
    ppermute x26 -> x23, waiting for transfers between devices: 16.6 us -> 6.98 us  [swap(): return lax.ppermute(values, 'tok', [(i, i ^ mask) for i in range(size)])]
    ppermute x6 -> x8, starting transfers between devices: 9.26 us -> 14.4 us  [swap_half_line(): return lax.ppermute(values.astype(bf16), ('tok', 'mlp'), pairs)]
    ppermute x0 -> x3, starting transfers between devices: none -> 3.55 us  [swap_half_plane(): return lax.ppermute(values, 'tok', pairs)]
    ppermute x0 -> x3, waiting for transfers between devices: none -> 2.85 us  [swap_half_plane(): return lax.ppermute(values, 'tok', pairs)]
    ppermute x26 -> x23, starting transfers between devices: 19.8 us -> 17 us  [swap(): return lax.ppermute(values, 'tok', [(i, i ^ mask) for i in range(size)])]
    add x5 -> x0, other arithmetic: 2.25 us -> none  [the longest x1 1.14 us: body(): total_a = total_a + wide(line_3[:, :edge])]
    reshape x4 -> x0, local copies, waits for them, and re-layouts: 1.81 us -> none  [the longest x1 0.63 us: results(): vectors = [small[3 * k:3 * k + 3].reshape(-1) for k in range(4)]]
    pallas_call x1 -> x4, Pallas kernels: 7.13 us -> 8.79 us  [the longest x1 3.9 us: early_gradient(): pl.pallas_call(early_kernel, grid=(groups,), in_specs=[pl.BlockSpec((seqs...]
  transfers between devices with their start and end apart: 32 -> 34, of which waited for: 13 -> 13; matrix products, arithmetic and copies ran while one was open for 4% -> 2% of each run, Pallas kernels for 42% -> 45%
where the time goes in v2:
time: 163 us
  Pallas kernels  104 us (64%)
  starting transfers between devices  34.9 us (21%)
  waiting for transfers between devices  17.6 us (11%)
  local copies, waits for them, and re-layouts  2.83 us (2%)
  other arithmetic  2.77 us (2%)
    pallas_call x2, Pallas kernels, backward(): pl.pallas_call(functools.partial(backward_kernel, pieces), grid=(groups,...  36.5 us
    pallas_call x1, Pallas kernels, forward(): pl.pallas_call(functools.partial(forward_kernel, pieces, len(biases), chu...  27.4 us
    pallas_call x1, Pallas kernels, attend(): pl.pallas_call(functools.partial(attend_kernel, len(parts)), grid=(GROUPS...  22.8 us
    ppermute x23, starting transfers between devices, swap(): return lax.ppermute(values, 'tok', [(i, i ^ mask) for i in range(size)])  17 us
    ppermute x8, starting transfers between devices, swap_half_line(): return lax.ppermute(values.astype(bf16), ('tok', 'mlp'), pairs)  14.4 us
    ppermute x8, waiting for transfers between devices, swap_half_line(): return lax.ppermute(values.astype(bf16), ('tok', 'mlp'), pairs)  7.73 us
    ppermute x23, waiting for transfers between devices, swap(): return lax.ppermute(values, 'tok', [(i, i ^ mask) for i in range(size)])  6.98 us
    pallas_call x1, Pallas kernels, mixed_gradient(): pl.pallas_call(mixed_gradient_kernel, grid=(seqs, GROUPS // each), in_spe...  5.45 us
  transfers between devices with their start and end apart: 34, of which 13 were waited for; matrix products, arithmetic and copies ran while one was open for 2% of the time, Pallas kernels for 45%

profile of v2, /device:TPU:0, one launch (start us, length us, event | category | flops | bytes accessed | tf_op | source)
XLA Modules:
  0.0 162.8 jit_solution(4013558190127294635)
XLA Ops:
  0.7 1.9 %prepare.1 = (bf16[64,1024]{1,0:T(8,128)(2,1)}, bf16[48,1024]{1,0:T(8,128)(2,1)}, f32[8,384]{1,0:T(8,128)}, f32[384,8]{1,0:T(8,128)}, f32[1,2048]{1,0:T(1,128)}) custom-call(bf16[48,512]{1,0:T(8,128)(2,1)} %one_ref.1, bf16[48,512]{1,0:T(8,128)(2,1)} %bitcast.63, bf16[512]{0:T(512)(128)(2,1)} %hidden_bias_ref.1, bf16[128,384]{1,0:T(8,128)(2,1)} %out_ref.1, ...), custom_call_target="tpu_custom_call" | custom-call | flops 2200000000 | bytes 1024 | tf_op jit(solution)/shard_map/prepare/pallas_call | solution.py:107
  2.5 4.0 %collective-permute-start = (bf16[64,1024]{1,0:T(8,128)(2,1)}, bf16[64,1024]{1,0:T(8,128)(2,1)S(1)}, u32[]{:S(2)}, u32[]{:S(2)}) collective-permute-start(bf16[64,1024]{1,0:T(8,128)(2,1)} %get-tuple-element.100.refs_0_), channel_id=1, source_target_pairs={{0,2},{1,3},{2,0},{3,1},{4,5},{5,4},{6,7},{7,6},{8,10},{9,11},{10,... | collective-permute-start | bytes 393224 | tf_op jit(solution)/shard_map/ppermute | solution.py:830
  6.6 1.5 collective-permute-start.2
  8.1 1.5 collective-permute-start.3
  11.4 1.8 %collective-permute-start.1 = (bf16[2,64,1024]{2,1,0:T(8,128)(2,1)S(1)}, bf16[2,64,1024]{2,1,0:T(8,128)(2,1)S(1)}, u32[]{:S(2)}, u32[]{:S(2)}) collective-permute-start(bf16[2,64,1024]{2,1,0:T(8,128)(2,1)S(1)} %pad_maximum_fusion.1), channel_id=1, source_target_pairs={{0,1},{1,0},{2,3},{3,2},{4,6},{5,7},{6,4},{7,5},{8,9},{9,8},{10,11... | collective-permute-start | bytes 786440 | tf_op jit(solution)/shard_map/ppermute | solution.py:830
  14.2 1.1 collective-permute-done.2.refs_1_
  15.8 1.2 collective-permute-start.7
  18.6 1.7 %collective-permute-done.1 = bf16[2,64,1024]{2,1,0:T(8,128)(2,1)S(1)} collective-permute-done((bf16[2,64,1024]{2,1,0:T(8,128)(2,1)S(1)}, bf16[2,64,1024]{2,1,0:T(8,128)(2,1)S(1)}, u32[]{:S(2)}, u32[]{:S(2)}) %collective-permute-start.1) | collective-permute-done | bytes 262176 | tf_op jit(solution)/shard_map/ppermute | solution.py:830
  20.3 1.7 %collective-permute-done.4.refs_3_ = bf16[48,3072]{1,0:T(8,128)(2,1)S(1)} collective-permute-done((bf16[48,3072]{1,0:T(8,128)(2,1)S(1)}, bf16[48,3072]{1,0:T(8,128)(2,1)S(1)}, u32[]{:S(2)}, u32[]{:S(2)}) %collective-permute-start.4) | collective-permute-done | bytes 294944 | tf_op jit(solution)/shard_map/ppermute | solution.py:820
  22.0 1.6 collective-permute-start.9
  24.1 1.5 collective-permute-start.11
  25.7 22.8 %attend.1 = (bf16[2,640,3072]{2,1,0:T(8,128)(2,1)}, bf16[2,640,1024]{2,1,0:T(8,128)(2,1)}, bf16[2,16,592,640]{3,2,1,0:T(8,128)(2,1)}, f32[2,4,8,640]{3,2,1,0:T(8,128)}, bf16[384,3072]{1,0:T(8,128)(2,1)}) custom-call(s32[1]{0:T(128)} %bitcast.me_ref, bf16[2,640,384]{2,1,0:T(8,128)(2,1)S(1)} %get-tuple-element.104.normed_ref, f32[1,2048]{1,0:T(1,128)S(1)} %copy-done.11, ...), custom_call_target="tpu_custom_call" | custom-call | flops 24199999488 | bytes 1024 | tf_op jit(solution)/shard_map/attend/pallas_call | solution.py:238
  52.0 27.4 %forward.1 = (bf16[1176,384]{1,0:T(8,128)(2,1)}, f32[2,640,384]{2,1,0:T(8,128)S(1)}, bf16[2,640,384]{2,1,0:T(8,128)(2,1)S(1)}, bf16[384,1024]{1,0:T(8,128)(2,1)S...) custom-call(s32[1]{0:T(128)} %bitcast.me_ref, bf16[1176,384]{1,0:T(8,128)(2,1)S(1)} %copy-done.2, ...), custom_call_target="tpu_custom_call" | custom-call | flops 32999999488 | bytes 1024 | tf_op jit(solution)/shard_map/forward/pallas_call | solution.py:441
  79.8 5.4 %mixed_gradient.1 = (bf16[2,640,1024]{2,1,0:T(8,128)(2,1)}, f32[2,4,8,640]{3,2,1,0:T(8,128)}) custom-call(bf16[2,640,384]{2,1,0:T(8,128)(2,1)S(1)} %get-tuple-element.117.branch_ref, bf16[384,1024]{1,0:T(8,128)(2,1)S(1)} %get-tuple-element.118.out_wide_ref, bf16[2,640,1024]{2,1,0:T(8,128)(2,1)S(1)} %copy-done.7), custom_call_target="tpu_custom_call" | custom-call | flops 5500000256 | bytes 1024 | tf_op jit(solution)/shard_map/mixed_gradient/pallas_call | solution.py:502
  86.0 1.6 collective-permute-start.17
  88.1 1.4 collective-permute-start.19
  89.6 26.0 %backward.2 = (bf16[2,640,2304]{2,1,0:T(8,128)(2,1)S(1)}, bf16[4,48,2432]{2,1,0:T(8,128)(2,1)S(1)}, bf16[4,48,2432]{2,1,0:T(8,128)(2,1)S(1)}) custom-call(s32[1]{0:T(128)} %bitcast.me_ref, bf16[2,640,1024]{2,1,0:T(8,128)(2,1)} %get-tuple-element.123.refs_0_, f32[2,4,8,640]{3,2,1,0:T(8,128)} %get-tuple-element.124.refs_1_, bf16[2,640,384]{2,1,0:T(8,128)(2,1)} %copy-done.6, ...), custom_call_target="tpu_custom_call" | custom-call | flops 36300001280 | bytes 1024 | tf_op jit(solution)/shard_map/backward/pallas_call | solution.py:649
  116.1 2.0 %collective-permute-done.20 = bf16[4,48,2432]{2,1,0:T(8,128)(2,1)S(1)} collective-permute-done((bf16[4,48,2432]{2,1,0:T(8,128)(2,1)S(1)}, bf16[4,48,2432]{2,1,0:T(8,128)(2,1)S(1)}, u32[]{:S(2)}, u32[]{:S(2)}) %collective-permute-start.20) | collective-permute-done | bytes 933920 | tf_op jit(solution)/shard_map/ppermute | solution.py:814
  118.4 2.4 %collective-permute-start.21 = (bf16[3,48,1152]{2,1,0:T(8,128)(2,1)S(1)}, bf16[3,48,1152]{2,1,0:T(8,128)(2,1)S(1)}, u32[]{:S(2)}, u32[]{:S(2)}) collective-permute-start(bf16[3,48,1152]{2,1,0:T(8,128)(2,1)S(1)} %pad_maximum_fusion), channel_id=1, source_target_pairs={{0,2},{1,3},{2,0},{3,1},{4,5},{5,4},{6,7},{7,6},{8,10},{9,11},{10,... | collective-permute-start | bytes 995336 | tf_op jit(solution)/shard_map/ppermute | solution.py:830
  120.8 1.6 collective-permute-start.22
  122.4 1.6 collective-permute-start.23
  124.3 10.5 %backward.3 = (bf16[2,640,768]{2,1,0:T(8,128)(2,1)S(1)}, bf16[4,48,896]{2,1,0:T(8,128)(2,1)S(1)}, bf16[4,48,896]{2,1,0:T(8,128)(2,1)S(1)}) custom-call(s32[1]{0:T(128)} %bitcast.me_ref, bf16[2,640,1024]{2,1,0:T(8,128)(2,1)} %get-tuple-element.123.refs_0_, f32[2,4,8,640]{3,2,1,0:T(8,128)} %get-tuple-element.124.refs_1_, bf16[2,640,384]{2,1,0:T(8,128)(2,1)} %copy-done.6, ...), custom_call_target="tpu_custom_call" | custom-call | flops 12099999744 | bytes 1024 | tf_op jit(solution)/shard_map/backward/pallas_call | solution.py:649
  135.1 1.2 collective-permute-start.26
  137.0 1.6 collective-permute-start.27
  138.6 1.6 collective-permute-start.28
  140.6 1.1 collective-permute-start.33
  141.7 1.8 %collective-permute-done.26 = bf16[48,2432]{1,0:T(8,128)(2,1)S(1)} collective-permute-done((bf16[48,2432]{1,0:T(8,128)(2,1)S(1)}, bf16[48,2432]{1,0:T(8,128)(2,1)S(1)}, u32[]{:S(2)}, u32[]{:S(2)}) %collective-permute-start.26) | collective-permute-done | bytes 233504 | tf_op jit(solution)/shard_map/ppermute | solution.py:830
  144.0 1.5 collective-permute-done.29
  146.7 3.9 %early_gradient.1.early_ref = f32[2,592,384]{2,1,0:T(8,128)S(1)} custom-call(bf16[2,640,2304]{2,1,0:T(8,128)(2,1)S(1)} %get-tuple-element.159.back_ref, bf16[384,3072]{1,0:T(8,128)(2,1)S(1)} %copy-done.5), custom_call_target="tpu_custom_call" | custom-call | flops 5500000256 | bytes 1024 | tf_op jit(solution)/shard_map/early_gradient/pallas_call | solution.py:691
  150.7 2.1 %collective-permute-start.31 = (bf16[48,2432]{1,0:T(8,128)(2,1)S(1)}, bf16[48,2432]{1,0:T(8,128)(2,1)S(1)}, u32[]{:S(2)}, u32[]{:S(2)}) collective-permute-start(bf16[48,2432]{1,0:T(8,128)(2,1)S(1)} %get-tuple-element.165), channel_id=1, source_target_pairs={{0,2},{1,3},{2,0},{3,1},{4,5},{5,4},{6,7},{7,6},{8,10},{9,11},{10,... | collective-permute-start | bytes 700424 | tf_op jit(solution)/shard_map/ppermute | solution.py:830
  153.7 3.2 %input_gradient.1 = f32[1176,384]{1,0:T(8,128)} custom-call(bf16[1176,384]{1,0:T(8,128)(2,1)S(1)} %copy-done.2, f32[2,640,384]{2,1,0:T(8,128)S(1)} %get-tuple-element.115.middle_grad_ref, f32[8,384]{1,0:T(8,128)S(1)} %copy-done.10, f32[2,592,384]{2,1,0:T(8,128)S(1)} %early_gradient.1.early_ref, bf16[2,640,768]{2,1,0:T(8,128)(2,1)S(1)} %get-tuple-element.164.back_ref, ...), custom_call_target="tpu_custom_call" | custom-call | flops 4400000000 | bytes 1024 | tf_op jit(solution)/shard_map/input_gradient/pallas_call | solution.py:717
  157.9 3.2 %collective-permute-done.31.early_line_ref = bf16[48,2432]{1,0:T(8,128)(2,1)S(1)} collective-permute-done((bf16[48,2432]{1,0:T(8,128)(2,1)S(1)}, bf16[48,2432]{1,0:T(8,128)(2,1)S(1)}, u32[]{:S(2)}, u32[]{:S(2)}) %collective-permute-start.31) | collective-permute-done | bytes 233504 | tf_op jit(solution)/shard_map/ppermute | solution.py:830
  (95 shorter events, 18.5 us)
Async XLA Ops:
  2.5 8.0 %collective-permute-start = (bf16[64,1024]{1,0:T(8,128)(2,1)}, bf16[64,1024]{1,0:T(8,128)(2,1)S(1)}, u32[]{:S(2)}, u32[]{:S(2)}) collective-permute-start(bf16[64,1024]{1,0:T(8,128)(2,1)} %get-tuple-element.100.refs_0_), channel_id=1, source_target_pairs={{0,2},{1,3},{2,0},{3,1},{4,5},{5,4},{6,7},{7,6},{8,10},{9,11},{10,... | collective-permute-start | bytes 393224 | tf_op jit(solution)/shard_map/ppermute | solution.py:830
  6.6 8.7 %collective-permute-start.2 = (bf16[48,3072]{1,0:T(8,128)(2,1)S(1)}, bf16[48,3072]{1,0:T(8,128)(2,1)S(1)}, u32[]{:S(2)}, u32[]{:S(2)}) collective-permute-start(bf16[48,3072]{1,0:T(8,128)(2,1)S(1)} %copy-done.3), channel_id=1, source_target_pairs={{0,8},{4,20},{8,0},{12,28},{16,24},{20,4},{24,16},{28,12},{1,9},{5... | collective-permute-start | bytes 884744 | tf_op jit(solution)/shard_map/ppermute | solution.py:820
  8.1 7.7 %collective-permute-start.3 = (bf16[48,3072]{1,0:T(8,128)(2,1)S(1)}, bf16[48,3072]{1,0:T(8,128)(2,1)S(1)}, u32[]{:S(2)}, u32[]{:S(2)}) collective-permute-start(bf16[48,3072]{1,0:T(8,128)(2,1)S(1)} %copy-done.3), channel_id=1, source_target_pairs={{0,16},{4,12},{8,24},{12,4},{16,0},{20,28},{24,8},{28,20},{1,17},{... | collective-permute-start | bytes 884744 | tf_op jit(solution)/shard_map/ppermute | solution.py:820
  9.6 14.0 %collective-permute-start.5 = (bf16[48,3072]{1,0:T(8,128)(2,1)S(1)}, bf16[48,3072]{1,0:T(8,128)(2,1)S(1)}, u32[]{:S(2)}, u32[]{:S(2)}) collective-permute-start(bf16[48,3072]{1,0:T(8,128)(2,1)S(1)} %copy-done.3), channel_id=1, source_target_pairs={{0,4},{4,0},{8,12},{12,8},{16,20},{20,16},{24,28},{28,24},{1,5},{5... | collective-permute-start | bytes 884744 | tf_op jit(solution)/shard_map/ppermute | solution.py:814
  11.4 8.8 %collective-permute-start.1 = (bf16[2,64,1024]{2,1,0:T(8,128)(2,1)S(1)}, bf16[2,64,1024]{2,1,0:T(8,128)(2,1)S(1)}, u32[]{:S(2)}, u32[]{:S(2)}) collective-permute-start(bf16[2,64,1024]{2,1,0:T(8,128)(2,1)S(1)} %pad_maximum_fusion.1), channel_id=1, source_target_pairs={{0,1},{1,0},{2,3},{3,2},{4,6},{5,7},{6,4},{7,5},{8,9},{9,8},{10,11... | collective-permute-start | bytes 786440 | tf_op jit(solution)/shard_map/ppermute | solution.py:830
  15.3 8.9 %collective-permute-start.6 = (bf16[48,3072]{1,0:T(8,128)(2,1)S(1)}, bf16[48,3072]{1,0:T(8,128)(2,1)S(1)}, u32[]{:S(2)}, u32[]{:S(2)}) collective-permute-start(bf16[48,3072]{1,0:T(8,128)(2,1)S(1)} %collective-permute-done.2.refs_1_), channel_id=1, source_target_pairs={{0,4},{4,0},{8,12},{12,8},{16,20},{20,16},{24,28},{28,24},{1,5},{5... | collective-permute-start | bytes 884744 | tf_op jit(solution)/shard_map/ppermute | solution.py:814
  15.3 6.7 %collective-permute-start.4 = (bf16[48,3072]{1,0:T(8,128)(2,1)S(1)}, bf16[48,3072]{1,0:T(8,128)(2,1)S(1)}, u32[]{:S(2)}, u32[]{:S(2)}) collective-permute-start(bf16[48,3072]{1,0:T(8,128)(2,1)S(1)} %collective-permute-done.2.refs_1_), channel_id=1, source_target_pairs={{0,16},{4,12},{8,24},{12,4},{16,0},{20,28},{24,8},{28,20},{1,17},{... | collective-permute-start | bytes 884744 | tf_op jit(solution)/shard_map/ppermute | solution.py:820
  15.8 9.8 %collective-permute-start.7 = (bf16[48,3072]{1,0:T(8,128)(2,1)S(1)}, bf16[48,3072]{1,0:T(8,128)(2,1)S(1)}, u32[]{:S(2)}, u32[]{:S(2)}) collective-permute-start(bf16[48,3072]{1,0:T(8,128)(2,1)S(1)} %collective-permute-done.3.refs_2_), channel_id=1, source_target_pairs={{0,4},{4,0},{8,12},{12,8},{16,20},{20,16},{24,28},{28,24},{1,5},{5... | collective-permute-start | bytes 884744 | tf_op jit(solution)/shard_map/ppermute | solution.py:814
  22.0 3.6 %collective-permute-start.8 = (bf16[48,3072]{1,0:T(8,128)(2,1)S(1)}, bf16[48,3072]{1,0:T(8,128)(2,1)S(1)}, u32[]{:S(2)}, u32[]{:S(2)}) collective-permute-start(bf16[48,3072]{1,0:T(8,128)(2,1)S(1)} %collective-permute-done.4.refs_3_), channel_id=1, source_target_pairs={{0,4},{4,0},{8,12},{12,8},{16,20},{20,16},{24,28},{28,24},{1,5},{5... | collective-permute-start | bytes 884744 | tf_op jit(solution)/shard_map/ppermute | solution.py:814
  22.0 26.5 %collective-permute-start.9 = (bf16[48,5120]{1,0:T(8,128)(2,1)S(1)}, bf16[48,5120]{1,0:T(8,128)(2,1)S(1)}, u32[]{:S(2)}, u32[]{:S(2)}) collective-permute-start(bf16[48,5120]{1,0:T(8,128)(2,1)S(1)} %fusion.10.refs_5_), channel_id=1, source_target_pairs={{0,8},{4,12},{8,0},{12,4},{16,24},{20,28},{24,16},{28,20},{1,9},{5... | collective-permute-start | bytes 1474568 | tf_op jit(solution)/shard_map/ppermute | solution.py:814
  23.6 24.9 %collective-permute-start.10 = (bf16[48,5120]{1,0:T(8,128)(2,1)S(1)}, bf16[48,5120]{1,0:T(8,128)(2,1)S(1)}, u32[]{:S(2)}, u32[]{:S(2)}) collective-permute-start(bf16[48,5120]{1,0:T(8,128)(2,1)S(1)} %fusion.10.refs_5_), channel_id=1, source_target_pairs={{0,16},{4,20},{8,24},{12,28},{16,0},{20,4},{24,8},{28,12},{1,17},{... | collective-permute-start | bytes 1474568 | tf_op jit(solution)/shard_map/ppermute | solution.py:814
  24.1 24.4 %collective-permute-start.11 = (bf16[48,5120]{1,0:T(8,128)(2,1)S(1)}, bf16[48,5120]{1,0:T(8,128)(2,1)S(1)}, u32[]{:S(2)}, u32[]{:S(2)}) collective-permute-start(bf16[48,5120]{1,0:T(8,128)(2,1)S(1)} %fusion.10.refs_5_), channel_id=1, source_target_pairs={{0,24},{4,28},{8,16},{12,20},{16,8},{20,12},{24,0},{28,4},{1,25},{... | collective-permute-start | bytes 1474568 | tf_op jit(solution)/shard_map/ppermute | solution.py:814
  25.6 22.9 %collective-permute-start.12 = (bf16[48,5120]{1,0:T(8,128)(2,1)S(1)}, bf16[48,5120]{1,0:T(8,128)(2,1)S(1)}, u32[]{:S(2)}, u32[]{:S(2)}) collective-permute-start(bf16[48,5120]{1,0:T(8,128)(2,1)S(1)} %fusion.10.refs_5_), channel_id=1, source_target_pairs={{0,4},{4,0},{8,12},{12,8},{16,20},{20,16},{24,28},{28,24},{1,5},{5... | collective-permute-start | bytes 1474568 | tf_op jit(solution)/shard_map/ppermute | solution.py:814
  49.1 2.2 %collective-permute-start.14 = (bf16[48,5120]{1,0:T(8,128)(2,1)S(1)}, bf16[48,5120]{1,0:T(8,128)(2,1)S(1)}, u32[]{:S(2)}, u32[]{:S(2)}) collective-permute-start(bf16[48,5120]{1,0:T(8,128)(2,1)S(1)} %collective-permute-done.10.refs_7_), channel_id=1, source_target_pairs={{0,4},{4,0},{8,12},{12,8},{16,20},{20,16},{24,28},{28,24},{1,5},{5... | collective-permute-start | bytes 1474568 | tf_op jit(solution)/shard_map/ppermute | solution.py:814
  49.2 2.8 %collective-permute-start.15 = (bf16[48,5120]{1,0:T(8,128)(2,1)S(1)}, bf16[48,5120]{1,0:T(8,128)(2,1)S(1)}, u32[]{:S(2)}, u32[]{:S(2)}) collective-permute-start(bf16[48,5120]{1,0:T(8,128)(2,1)S(1)} %collective-permute-done.11.refs_8_), channel_id=1, source_target_pairs={{0,4},{4,0},{8,12},{12,8},{16,20},{20,16},{24,28},{28,24},{1,5},{5... | collective-permute-start | bytes 1474568 | tf_op jit(solution)/shard_map/ppermute | solution.py:814
  79.4 5.9 %collective-permute-start.16 = (bf16[4,5,48,1152]{3,2,1,0:T(8,128)(2,1)S(1)}, bf16[4,5,48,1152]{3,2,1,0:T(8,128)(2,1)S(1)}, u32[]{:S(2)}, u32[]{:S(2)}) collective-permute-start(bf16[4,5,48,1152]{3,2,1,0:T(8,128)(2,1)S(1)} %get-tuple-element.120), channel_id=1, source_target_pairs={{0,4},{4,0},{8,12},{12,8},{16,20},{20,16},{24,28},{28,24},{1,5},{5... | collective-permute-start | bytes 6635528 | tf_op jit(solution)/shard_map/ppermute | solution.py:814
  86.0 29.6 %collective-permute-start.17 = (bf16[5,48,1152]{2,1,0:T(8,128)(2,1)S(1)}, bf16[5,48,1152]{2,1,0:T(8,128)(2,1)S(1)}, u32[]{:S(2)}, u32[]{:S(2)}) collective-permute-start(bf16[5,48,1152]{2,1,0:T(8,128)(2,1)S(1)} %get-tuple-element.192), channel_id=1, source_target_pairs={{0,8},{4,12},{8,0},{12,4},{16,24},{20,28},{24,16},{28,20},{1,9},{5... | collective-permute-start | bytes 1658888 | tf_op jit(solution)/shard_map/ppermute | solution.py:814
  87.6 28.1 %collective-permute-start.18 = (bf16[5,48,1152]{2,1,0:T(8,128)(2,1)S(1)}, bf16[5,48,1152]{2,1,0:T(8,128)(2,1)S(1)}, u32[]{:S(2)}, u32[]{:S(2)}) collective-permute-start(bf16[5,48,1152]{2,1,0:T(8,128)(2,1)S(1)} %get-tuple-element.191), channel_id=1, source_target_pairs={{0,16},{4,20},{8,24},{12,28},{16,0},{20,4},{24,8},{28,12},{1,17},{... | collective-permute-start | bytes 1658888 | tf_op jit(solution)/shard_map/ppermute | solution.py:814
  88.1 27.5 %collective-permute-start.19 = (bf16[5,48,1152]{2,1,0:T(8,128)(2,1)S(1)}, bf16[5,48,1152]{2,1,0:T(8,128)(2,1)S(1)}, u32[]{:S(2)}, u32[]{:S(2)}) collective-permute-start(bf16[5,48,1152]{2,1,0:T(8,128)(2,1)S(1)} %get-tuple-element.190), channel_id=1, source_target_pairs={{0,24},{4,28},{8,16},{12,20},{16,8},{20,12},{24,0},{28,4},{1,25},{... | collective-permute-start | bytes 1658888 | tf_op jit(solution)/shard_map/ppermute | solution.py:814
  115.6 2.6 %collective-permute-start.20 = (bf16[4,48,2432]{2,1,0:T(8,128)(2,1)S(1)}, bf16[4,48,2432]{2,1,0:T(8,128)(2,1)S(1)}, u32[]{:S(2)}, u32[]{:S(2)}) collective-permute-start(bf16[4,48,2432]{2,1,0:T(8,128)(2,1)S(1)} %get-tuple-element.135), channel_id=1, source_target_pairs={{0,4},{4,0},{8,12},{12,8},{16,20},{20,16},{24,28},{28,24},{1,5},{5... | collective-permute-start | bytes 2801672 | tf_op jit(solution)/shard_map/ppermute | solution.py:814
  118.4 16.5 %collective-permute-start.21 = (bf16[3,48,1152]{2,1,0:T(8,128)(2,1)S(1)}, bf16[3,48,1152]{2,1,0:T(8,128)(2,1)S(1)}, u32[]{:S(2)}, u32[]{:S(2)}) collective-permute-start(bf16[3,48,1152]{2,1,0:T(8,128)(2,1)S(1)} %pad_maximum_fusion), channel_id=1, source_target_pairs={{0,2},{1,3},{2,0},{3,1},{4,5},{5,4},{6,7},{7,6},{8,10},{9,11},{10,... | collective-permute-start | bytes 995336 | tf_op jit(solution)/shard_map/ppermute | solution.py:830
  120.8 14.1 %collective-permute-start.22 = (bf16[48,2432]{1,0:T(8,128)(2,1)S(1)}, bf16[48,2432]{1,0:T(8,128)(2,1)S(1)}, u32[]{:S(2)}, u32[]{:S(2)}) collective-permute-start(bf16[48,2432]{1,0:T(8,128)(2,1)S(1)} %get-tuple-element.197), channel_id=1, source_target_pairs={{0,8},{4,12},{8,0},{12,4},{16,24},{20,28},{24,16},{28,20},{1,9},{5... | collective-permute-start | bytes 700424 | tf_op jit(solution)/shard_map/ppermute | solution.py:814
  122.4 12.6 %collective-permute-start.23 = (bf16[48,2432]{1,0:T(8,128)(2,1)S(1)}, bf16[48,2432]{1,0:T(8,128)(2,1)S(1)}, u32[]{:S(2)}, u32[]{:S(2)}) collective-permute-start(bf16[48,2432]{1,0:T(8,128)(2,1)S(1)} %get-tuple-element.196), channel_id=1, source_target_pairs={{0,16},{4,20},{8,24},{12,28},{16,0},{20,4},{24,8},{28,12},{1,17},{... | collective-permute-start | bytes 700424 | tf_op jit(solution)/shard_map/ppermute | solution.py:814
  123.9 11.0 %collective-permute-start.24 = (bf16[48,2432]{1,0:T(8,128)(2,1)S(1)}, bf16[48,2432]{1,0:T(8,128)(2,1)S(1)}, u32[]{:S(2)}, u32[]{:S(2)}) collective-permute-start(bf16[48,2432]{1,0:T(8,128)(2,1)S(1)} %get-tuple-element.195), channel_id=1, source_target_pairs={{0,24},{4,28},{8,16},{12,20},{16,8},{20,12},{24,0},{28,4},{1,25},{... | collective-permute-start | bytes 700424 | tf_op jit(solution)/shard_map/ppermute | solution.py:814
  135.1 8.4 %collective-permute-start.26 = (bf16[48,2432]{1,0:T(8,128)(2,1)S(1)}, bf16[48,2432]{1,0:T(8,128)(2,1)S(1)}, u32[]{:S(2)}, u32[]{:S(2)}) collective-permute-start(bf16[48,2432]{1,0:T(8,128)(2,1)S(1)} %fusion.8), channel_id=1, source_target_pairs={{0,1},{1,0},{2,3},{3,2},{4,6},{5,7},{6,4},{7,5},{8,9},{9,8},{10,11... | collective-permute-start | bytes 700424 | tf_op jit(solution)/shard_map/ppermute | solution.py:830
  137.0 6.5 %collective-permute-start.27 = (bf16[48,896]{1,0:T(8,128)(2,1)S(1)}, bf16[48,896]{1,0:T(8,128)(2,1)S(1)}, u32[]{:S(2)}, u32[]{:S(2)}) collective-permute-start(bf16[48,896]{1,0:T(8,128)(2,1)S(1)} %get-tuple-element.202), channel_id=1, source_target_pairs={{0,8},{4,12},{8,0},{12,4},{16,24},{20,28},{24,16},{28,20},{1,9},{5... | collective-permute-start | bytes 258056 | tf_op jit(solution)/shard_map/ppermute | solution.py:814
  138.6 5.4 %collective-permute-start.28 = (bf16[48,896]{1,0:T(8,128)(2,1)S(1)}, bf16[48,896]{1,0:T(8,128)(2,1)S(1)}, u32[]{:S(2)}, u32[]{:S(2)}) collective-permute-start(bf16[48,896]{1,0:T(8,128)(2,1)S(1)} %get-tuple-element.201), channel_id=1, source_target_pairs={{0,16},{4,20},{8,24},{12,28},{16,0},{20,4},{24,8},{28,12},{1,17},{... | collective-permute-start | bytes 258056 | tf_op jit(solution)/shard_map/ppermute | solution.py:814
  140.2 5.4 %collective-permute-start.29 = (bf16[48,896]{1,0:T(8,128)(2,1)S(1)}, bf16[48,896]{1,0:T(8,128)(2,1)S(1)}, u32[]{:S(2)}, u32[]{:S(2)}) collective-permute-start(bf16[48,896]{1,0:T(8,128)(2,1)S(1)} %get-tuple-element.200), channel_id=1, source_target_pairs={{0,24},{4,28},{8,16},{12,20},{16,8},{20,12},{24,0},{28,4},{1,25},{... | collective-permute-start | bytes 258056 | tf_op jit(solution)/shard_map/ppermute | solution.py:814
  140.6 16.3 %collective-permute-start.33 = (bf16[48,2304]{1,0:T(8,128)(2,1)S(1)}, bf16[48,2304]{1,0:T(8,128)(2,1)S(1)}, u32[]{:S(2)}, u32[]{:S(2)}) collective-permute-start(bf16[48,2304]{1,0:T(8,128)(2,1)S(1)} %pad_maximum_fusion.2), channel_id=1, source_target_pairs={{0,1},{1,0},{2,3},{3,2},{4,6},{5,7},{6,4},{7,5},{8,9},{9,8},{10,11... | collective-permute-start | bytes 663560 | tf_op jit(solution)/shard_map/ppermute | solution.py:830
  145.8 7.0 %collective-permute-start.30 = (bf16[48,896]{1,0:T(8,128)(2,1)S(1)}, bf16[48,896]{1,0:T(8,128)(2,1)S(1)}, u32[]{:S(2)}, u32[]{:S(2)}) collective-permute-start(bf16[48,896]{1,0:T(8,128)(2,1)S(1)} %fusion.11), channel_id=1, source_target_pairs={{0,2},{1,3},{2,0},{3,1},{4,5},{5,4},{6,7},{7,6},{8,10},{9,11},{10,... | collective-permute-start | bytes 258056 | tf_op jit(solution)/shard_map/ppermute | solution.py:830
  150.7 10.5 %collective-permute-start.31 = (bf16[48,2432]{1,0:T(8,128)(2,1)S(1)}, bf16[48,2432]{1,0:T(8,128)(2,1)S(1)}, u32[]{:S(2)}, u32[]{:S(2)}) collective-permute-start(bf16[48,2432]{1,0:T(8,128)(2,1)S(1)} %get-tuple-element.165), channel_id=1, source_target_pairs={{0,2},{1,3},{2,0},{3,1},{4,5},{5,4},{6,7},{7,6},{8,10},{9,11},{10,... | collective-permute-start | bytes 700424 | tf_op jit(solution)/shard_map/ppermute | solution.py:830
  152.8 5.0 %collective-permute-start.32 = (bf16[48,896]{1,0:T(8,128)(2,1)S(1)}, bf16[48,896]{1,0:T(8,128)(2,1)S(1)}, u32[]{:S(2)}, u32[]{:S(2)}) collective-permute-start(bf16[48,896]{1,0:T(8,128)(2,1)S(1)} %get-tuple-element.166), channel_id=1, source_target_pairs={{0,1},{1,0},{2,3},{3,2},{4,6},{5,7},{6,4},{7,5},{8,9},{9,8},{10,11... | collective-permute-start | bytes 258056 | tf_op jit(solution)/shard_map/ppermute | solution.py:830
  (14 other events, 172.4 us)

commit v3 on v2

--- a/solution.py
+++ b/solution.py
@@ -254,7 +254,7 @@
         ],
         out_shape=[
             pltpu.HBM((seqs, ROWS, GROUPS * QKV), bf16),
-            pltpu.HBM((seqs, ROWS, INNER), bf16),
+            pltpu.VMEM((seqs, ROWS, INNER), bf16),
             pltpu.HBM((seqs, HEADS, KEYS, ROWS), bf16),
             pltpu.HBM((seqs, GROUPS, 8, ROWS), f32),
             pltpu.HBM((D, GROUPS * QKV), bf16),
@@ -437,7 +437,6 @@
         send_specs = [pl.BlockSpec((1, D, BLOCK), lambda c: (c, 0, 0))]
     rows3 = (seqs, ROWS, D)
     rows2 = (seqs * KEYS, D)
-    mixed = pltpu.with_memory_space_constraint(mixed, pltpu.HBM)
     return pl.pallas_call(
         functools.partial(forward_kernel, pieces, len(biases), chunk),
         grid=(5,),
@@ -455,10 +454,10 @@
         out_shape=[
             jax.ShapeDtypeStruct(tokens.shape, bf16),
             jax.ShapeDtypeStruct(rows3, f32),
-            jax.ShapeDtypeStruct(rows3, bf16),
-            jax.ShapeDtypeStruct((D, INNER), bf16),
+            pltpu.VMEM(rows3, bf16),
+            pltpu.VMEM((D, INNER), bf16),
         ]
-        + [jax.ShapeDtypeStruct(s, bf16) for s in send_shapes],
+        + [pltpu.VMEM(s, bf16) for s in send_shapes],
         scratch_shapes=[
             pltpu.VMEM((D, FF), bf16),
             pltpu.VMEM((D, FF), bf16),

time: 163 us -> 162 us (level)
  Pallas kernels: 104 us -> 102 us
    pallas_call x1, Pallas kernels: 27.4 us -> 25.7 us  [forward(): pl.pallas_call(functools.partial(forward_kernel, pieces, len(biases), chu...]
where the time goes in v3:
time: 162 us; the launch traced here: 161 us
  Pallas kernels  102 us (63%)
  starting transfers between devices  34.9 us (22%)
  waiting for transfers between devices  17.6 us (11%)
  local copies, waits for them, and re-layouts  2.82 us (2%)
  other arithmetic  2.78 us (2%)
    pallas_call x2, Pallas kernels, backward(): pl.pallas_call(functools.partial(backward_kernel, pieces), grid=(groups,...  36.6 us
    pallas_call x1, Pallas kernels, forward(): pl.pallas_call(functools.partial(forward_kernel, pieces, len(biases), chu...  25.7 us
    pallas_call x1, Pallas kernels, attend(): pl.pallas_call(functools.partial(attend_kernel, len(parts)), grid=(GROUPS...  23 us
    ppermute x23, starting transfers between devices, swap(): return lax.ppermute(values, 'tok', [(i, i ^ mask) for i in range(size)])  17 us
    ppermute x8, starting transfers between devices, swap_half_line(): return lax.ppermute(values.astype(bf16), ('tok', 'mlp'), pairs)  14.3 us
    ppermute x8, waiting for transfers between devices, swap_half_line(): return lax.ppermute(values.astype(bf16), ('tok', 'mlp'), pairs)  7.77 us
    ppermute x23, waiting for transfers between devices, swap(): return lax.ppermute(values, 'tok', [(i, i ^ mask) for i in range(size)])  7.01 us
    pallas_call x1, Pallas kernels, mixed_gradient(): pl.pallas_call(mixed_gradient_kernel, grid=(seqs, GROUPS // each), in_spe...  5.45 us
  transfers between devices with their start and end apart: 34, of which 13 were waited for; matrix products, arithmetic and copies ran while one was open for 2% of the time, Pallas kernels for 45%

profile of v3, /device:TPU:0, one launch (start us, length us, event | category | flops | bytes accessed | tf_op | source)
XLA Modules:
  0.0 161.4 jit_solution(6183999630359722655)
XLA Ops:
  0.7 1.9 %prepare.1 = (bf16[64,1024]{1,0:T(8,128)(2,1)}, bf16[48,1024]{1,0:T(8,128)(2,1)}, f32[8,384]{1,0:T(8,128)}, f32[384,8]{1,0:T(8,128)}, f32[1,2048]{1,0:T(1,128)}) custom-call(bf16[48,512]{1,0:T(8,128)(2,1)} %one_ref.1, bf16[48,512]{1,0:T(8,128)(2,1)} %bitcast.63, bf16[512]{0:T(512)(128)(2,1)} %hidden_bias_ref.1, bf16[128,384]{1,0:T(8,128)(2,1)} %out_ref.1, ...), custom_call_target="tpu_custom_call" | custom-call | flops 2200000000 | bytes 1024 | tf_op jit(solution)/shard_map/prepare/pallas_call | solution.py:107
  2.5 4.0 %collective-permute-start = (bf16[64,1024]{1,0:T(8,128)(2,1)}, bf16[64,1024]{1,0:T(8,128)(2,1)S(1)}, u32[]{:S(2)}, u32[]{:S(2)}) collective-permute-start(bf16[64,1024]{1,0:T(8,128)(2,1)} %get-tuple-element.100.refs_0_), channel_id=1, source_target_pairs={{0,2},{1,3},{2,0},{3,1},{4,5},{5,4},{6,7},{7,6},{8,10},{9,11},{10,... | collective-permute-start | bytes 393224 | tf_op jit(solution)/shard_map/ppermute | solution.py:829
  6.6 1.5 collective-permute-start.2
  8.1 1.5 collective-permute-start.3
  11.4 1.8 %collective-permute-start.1 = (bf16[2,64,1024]{2,1,0:T(8,128)(2,1)S(1)}, bf16[2,64,1024]{2,1,0:T(8,128)(2,1)S(1)}, u32[]{:S(2)}, u32[]{:S(2)}) collective-permute-start(bf16[2,64,1024]{2,1,0:T(8,128)(2,1)S(1)} %pad_maximum_fusion.1), channel_id=1, source_target_pairs={{0,1},{1,0},{2,3},{3,2},{4,6},{5,7},{6,4},{7,5},{8,9},{9,8},{10,11... | collective-permute-start | bytes 786440 | tf_op jit(solution)/shard_map/ppermute | solution.py:829
  14.2 1.1 collective-permute-done.2.refs_1_
  15.8 1.2 collective-permute-start.7
  18.6 1.7 %collective-permute-done.1 = bf16[2,64,1024]{2,1,0:T(8,128)(2,1)S(1)} collective-permute-done((bf16[2,64,1024]{2,1,0:T(8,128)(2,1)S(1)}, bf16[2,64,1024]{2,1,0:T(8,128)(2,1)S(1)}, u32[]{:S(2)}, u32[]{:S(2)}) %collective-permute-start.1) | collective-permute-done | bytes 262176 | tf_op jit(solution)/shard_map/ppermute | solution.py:829
  20.3 1.7 %collective-permute-done.4.refs_3_ = bf16[48,3072]{1,0:T(8,128)(2,1)S(1)} collective-permute-done((bf16[48,3072]{1,0:T(8,128)(2,1)S(1)}, bf16[48,3072]{1,0:T(8,128)(2,1)S(1)}, u32[]{:S(2)}, u32[]{:S(2)}) %collective-permute-start.4) | collective-permute-done | bytes 294944 | tf_op jit(solution)/shard_map/ppermute | solution.py:819
  22.0 1.6 collective-permute-start.9
  24.1 1.5 collective-permute-start.11
  25.7 23.0 %attend.1 = (bf16[2,640,3072]{2,1,0:T(8,128)(2,1)}, bf16[2,640,1024]{2,1,0:T(8,128)(2,1)S(1)}, bf16[2,16,592,640]{3,2,1,0:T(8,128)(2,1)}, f32[2,4,8,640]{3,2,1,0:T(8,128)}, bf16[384,3072]{1,0:T(8,128)(2,1)}) custom-call(s32[1]{0:T(128)} %bitcast.me_ref, bf16[2,640,384]{2,1,0:T(8,128)(2,1)S(1)} %get-tuple-element.104.normed_ref, f32[1,2048]{1,0:T(1,128)S(1)} %copy-done.10, ...), custom_call_target="tpu_custom_call" | custom-call | flops 24199999488 | bytes 1024 | tf_op jit(solution)/shard_map/attend/pallas_call | solution.py:238
  52.2 25.7 %forward.1 = (bf16[1176,384]{1,0:T(8,128)(2,1)}, f32[2,640,384]{2,1,0:T(8,128)S(1)}, bf16[2,640,384]{2,1,0:T(8,128)(2,1)S(1)}, bf16[384,1024]{1,0:T(8,128)(2,1)S...) custom-call(s32[1]{0:T(128)} %bitcast.me_ref, bf16[1176,384]{1,0:T(8,128)(2,1)S(1)} %copy-done.2, ...), custom_call_target="tpu_custom_call" | custom-call | flops 32999999488 | bytes 1024 | tf_op jit(solution)/shard_map/forward/pallas_call | solution.py:440
  78.3 5.4 %mixed_gradient.1 = (bf16[2,640,1024]{2,1,0:T(8,128)(2,1)}, f32[2,4,8,640]{3,2,1,0:T(8,128)}) custom-call(bf16[2,640,384]{2,1,0:T(8,128)(2,1)S(1)} %get-tuple-element.117.branch_ref, bf16[384,1024]{1,0:T(8,128)(2,1)S(1)} %get-tuple-element.118.out_wide_ref, bf16[2,640,1024]{2,1,0:T(8,128)(2,1)S(1)} %get-tuple-element.109.refs_4_.mixed_ref), custom_call_target="tpu_custom_call" | custom-call | flops 5500000256 | bytes 1024 | tf_op jit(solution)/shard_map/mixed_gradient/pallas_call | solution.py:501
  84.5 1.6 collective-permute-start.17
  86.7 1.4 collective-permute-start.19
  88.1 26.0 %backward.2 = (bf16[2,640,2304]{2,1,0:T(8,128)(2,1)S(1)}, bf16[4,48,2432]{2,1,0:T(8,128)(2,1)S(1)}, bf16[4,48,2432]{2,1,0:T(8,128)(2,1)S(1)}) custom-call(s32[1]{0:T(128)} %bitcast.me_ref, bf16[2,640,1024]{2,1,0:T(8,128)(2,1)} %get-tuple-element.123.refs_0_, f32[2,4,8,640]{3,2,1,0:T(8,128)} %get-tuple-element.124.refs_1_, bf16[2,640,384]{2,1,0:T(8,128)(2,1)} %copy-done.6, ...), custom_call_target="tpu_custom_call" | custom-call | flops 36300001280 | bytes 1024 | tf_op jit(solution)/shard_map/backward/pallas_call | solution.py:648
  114.6 2.1 %collective-permute-done.20 = bf16[4,48,2432]{2,1,0:T(8,128)(2,1)S(1)} collective-permute-done((bf16[4,48,2432]{2,1,0:T(8,128)(2,1)S(1)}, bf16[4,48,2432]{2,1,0:T(8,128)(2,1)S(1)}, u32[]{:S(2)}, u32[]{:S(2)}) %collective-permute-start.20) | collective-permute-done | bytes 933920 | tf_op jit(solution)/shard_map/ppermute | solution.py:813
  116.9 2.4 %collective-permute-start.21 = (bf16[3,48,1152]{2,1,0:T(8,128)(2,1)S(1)}, bf16[3,48,1152]{2,1,0:T(8,128)(2,1)S(1)}, u32[]{:S(2)}, u32[]{:S(2)}) collective-permute-start(bf16[3,48,1152]{2,1,0:T(8,128)(2,1)S(1)} %pad_maximum_fusion), channel_id=1, source_target_pairs={{0,2},{1,3},{2,0},{3,1},{4,5},{5,4},{6,7},{7,6},{8,10},{9,11},{10,... | collective-permute-start | bytes 995336 | tf_op jit(solution)/shard_map/ppermute | solution.py:829
  119.3 1.6 collective-permute-start.22
  120.9 1.5 collective-permute-start.23
  122.9 10.6 %backward.3 = (bf16[2,640,768]{2,1,0:T(8,128)(2,1)S(1)}, bf16[4,48,896]{2,1,0:T(8,128)(2,1)S(1)}, bf16[4,48,896]{2,1,0:T(8,128)(2,1)S(1)}) custom-call(s32[1]{0:T(128)} %bitcast.me_ref, bf16[2,640,1024]{2,1,0:T(8,128)(2,1)} %get-tuple-element.123.refs_0_, f32[2,4,8,640]{3,2,1,0:T(8,128)} %get-tuple-element.124.refs_1_, bf16[2,640,384]{2,1,0:T(8,128)(2,1)} %copy-done.6, ...), custom_call_target="tpu_custom_call" | custom-call | flops 12099999744 | bytes 1024 | tf_op jit(solution)/shard_map/backward/pallas_call | solution.py:648
  133.7 1.1 collective-permute-start.26
  135.6 1.6 collective-permute-start.27
  137.2 1.5 collective-permute-start.28
  139.2 1.1 collective-permute-start.33
  140.2 1.8 %collective-permute-done.26 = bf16[48,2432]{1,0:T(8,128)(2,1)S(1)} collective-permute-done((bf16[48,2432]{1,0:T(8,128)(2,1)S(1)}, bf16[48,2432]{1,0:T(8,128)(2,1)S(1)}, u32[]{:S(2)}, u32[]{:S(2)}) %collective-permute-start.26) | collective-permute-done | bytes 233504 | tf_op jit(solution)/shard_map/ppermute | solution.py:829
  142.6 1.5 collective-permute-done.29
  145.3 3.9 %early_gradient.1.early_ref = f32[2,592,384]{2,1,0:T(8,128)S(1)} custom-call(bf16[2,640,2304]{2,1,0:T(8,128)(2,1)S(1)} %get-tuple-element.159.back_ref, bf16[384,3072]{1,0:T(8,128)(2,1)S(1)} %copy-done.5), custom_call_target="tpu_custom_call" | custom-call | flops 5500000256 | bytes 1024 | tf_op jit(solution)/shard_map/early_gradient/pallas_call | solution.py:690
  149.2 2.1 %collective-permute-start.31 = (bf16[48,2432]{1,0:T(8,128)(2,1)S(1)}, bf16[48,2432]{1,0:T(8,128)(2,1)S(1)}, u32[]{:S(2)}, u32[]{:S(2)}) collective-permute-start(bf16[48,2432]{1,0:T(8,128)(2,1)S(1)} %get-tuple-element.165), channel_id=1, source_target_pairs={{0,2},{1,3},{2,0},{3,1},{4,5},{5,4},{6,7},{7,6},{8,10},{9,11},{10,... | collective-permute-start | bytes 700424 | tf_op jit(solution)/shard_map/ppermute | solution.py:829
  152.2 3.2 %input_gradient.1 = f32[1176,384]{1,0:T(8,128)} custom-call(bf16[1176,384]{1,0:T(8,128)(2,1)S(1)} %copy-done.2, f32[2,640,384]{2,1,0:T(8,128)S(1)} %get-tuple-element.115.middle_grad_ref, f32[8,384]{1,0:T(8,128)S(1)} %copy-done.9, f32[2,592,384]{2,1,0:T(8,128)S(1)} %early_gradient.1.early_ref, bf16[2,640,768]{2,1,0:T(8,128)(2,1)S(1)} %get-tuple-element.164.back_ref, ...), custom_call_target="tpu_custom_call" | custom-call | flops 4400000000 | bytes 1024 | tf_op jit(solution)/shard_map/input_gradient/pallas_call | solution.py:716
  156.4 3.2 %collective-permute-done.31.early_line_ref = bf16[48,2432]{1,0:T(8,128)(2,1)S(1)} collective-permute-done((bf16[48,2432]{1,0:T(8,128)(2,1)S(1)}, bf16[48,2432]{1,0:T(8,128)(2,1)S(1)}, u32[]{:S(2)}, u32[]{:S(2)}) %collective-permute-start.31) | collective-permute-done | bytes 233504 | tf_op jit(solution)/shard_map/ppermute | solution.py:829
  (93 shorter events, 18.6 us)
Async XLA Ops:
  2.5 8.0 %collective-permute-start = (bf16[64,1024]{1,0:T(8,128)(2,1)}, bf16[64,1024]{1,0:T(8,128)(2,1)S(1)}, u32[]{:S(2)}, u32[]{:S(2)}) collective-permute-start(bf16[64,1024]{1,0:T(8,128)(2,1)} %get-tuple-element.100.refs_0_), channel_id=1, source_target_pairs={{0,2},{1,3},{2,0},{3,1},{4,5},{5,4},{6,7},{7,6},{8,10},{9,11},{10,... | collective-permute-start | bytes 393224 | tf_op jit(solution)/shard_map/ppermute | solution.py:829
  6.6 8.7 %collective-permute-start.2 = (bf16[48,3072]{1,0:T(8,128)(2,1)S(1)}, bf16[48,3072]{1,0:T(8,128)(2,1)S(1)}, u32[]{:S(2)}, u32[]{:S(2)}) collective-permute-start(bf16[48,3072]{1,0:T(8,128)(2,1)S(1)} %copy-done.3), channel_id=1, source_target_pairs={{0,8},{4,20},{8,0},{12,28},{16,24},{20,4},{24,16},{28,12},{1,9},{5... | collective-permute-start | bytes 884744 | tf_op jit(solution)/shard_map/ppermute | solution.py:819
  8.1 7.7 %collective-permute-start.3 = (bf16[48,3072]{1,0:T(8,128)(2,1)S(1)}, bf16[48,3072]{1,0:T(8,128)(2,1)S(1)}, u32[]{:S(2)}, u32[]{:S(2)}) collective-permute-start(bf16[48,3072]{1,0:T(8,128)(2,1)S(1)} %copy-done.3), channel_id=1, source_target_pairs={{0,16},{4,12},{8,24},{12,4},{16,0},{20,28},{24,8},{28,20},{1,17},{... | collective-permute-start | bytes 884744 | tf_op jit(solution)/shard_map/ppermute | solution.py:819
  9.6 14.0 %collective-permute-start.5 = (bf16[48,3072]{1,0:T(8,128)(2,1)S(1)}, bf16[48,3072]{1,0:T(8,128)(2,1)S(1)}, u32[]{:S(2)}, u32[]{:S(2)}) collective-permute-start(bf16[48,3072]{1,0:T(8,128)(2,1)S(1)} %copy-done.3), channel_id=1, source_target_pairs={{0,4},{4,0},{8,12},{12,8},{16,20},{20,16},{24,28},{28,24},{1,5},{5... | collective-permute-start | bytes 884744 | tf_op jit(solution)/shard_map/ppermute | solution.py:813
  11.4 8.8 %collective-permute-start.1 = (bf16[2,64,1024]{2,1,0:T(8,128)(2,1)S(1)}, bf16[2,64,1024]{2,1,0:T(8,128)(2,1)S(1)}, u32[]{:S(2)}, u32[]{:S(2)}) collective-permute-start(bf16[2,64,1024]{2,1,0:T(8,128)(2,1)S(1)} %pad_maximum_fusion.1), channel_id=1, source_target_pairs={{0,1},{1,0},{2,3},{3,2},{4,6},{5,7},{6,4},{7,5},{8,9},{9,8},{10,11... | collective-permute-start | bytes 786440 | tf_op jit(solution)/shard_map/ppermute | solution.py:829
  15.3 8.9 %collective-permute-start.6 = (bf16[48,3072]{1,0:T(8,128)(2,1)S(1)}, bf16[48,3072]{1,0:T(8,128)(2,1)S(1)}, u32[]{:S(2)}, u32[]{:S(2)}) collective-permute-start(bf16[48,3072]{1,0:T(8,128)(2,1)S(1)} %collective-permute-done.2.refs_1_), channel_id=1, source_target_pairs={{0,4},{4,0},{8,12},{12,8},{16,20},{20,16},{24,28},{28,24},{1,5},{5... | collective-permute-start | bytes 884744 | tf_op jit(solution)/shard_map/ppermute | solution.py:813
  15.3 6.7 %collective-permute-start.4 = (bf16[48,3072]{1,0:T(8,128)(2,1)S(1)}, bf16[48,3072]{1,0:T(8,128)(2,1)S(1)}, u32[]{:S(2)}, u32[]{:S(2)}) collective-permute-start(bf16[48,3072]{1,0:T(8,128)(2,1)S(1)} %collective-permute-done.2.refs_1_), channel_id=1, source_target_pairs={{0,16},{4,12},{8,24},{12,4},{16,0},{20,28},{24,8},{28,20},{1,17},{... | collective-permute-start | bytes 884744 | tf_op jit(solution)/shard_map/ppermute | solution.py:819
  15.8 9.8 %collective-permute-start.7 = (bf16[48,3072]{1,0:T(8,128)(2,1)S(1)}, bf16[48,3072]{1,0:T(8,128)(2,1)S(1)}, u32[]{:S(2)}, u32[]{:S(2)}) collective-permute-start(bf16[48,3072]{1,0:T(8,128)(2,1)S(1)} %collective-permute-done.3.refs_2_), channel_id=1, source_target_pairs={{0,4},{4,0},{8,12},{12,8},{16,20},{20,16},{24,28},{28,24},{1,5},{5... | collective-permute-start | bytes 884744 | tf_op jit(solution)/shard_map/ppermute | solution.py:813
  22.0 3.6 %collective-permute-start.8 = (bf16[48,3072]{1,0:T(8,128)(2,1)S(1)}, bf16[48,3072]{1,0:T(8,128)(2,1)S(1)}, u32[]{:S(2)}, u32[]{:S(2)}) collective-permute-start(bf16[48,3072]{1,0:T(8,128)(2,1)S(1)} %collective-permute-done.4.refs_3_), channel_id=1, source_target_pairs={{0,4},{4,0},{8,12},{12,8},{16,20},{20,16},{24,28},{28,24},{1,5},{5... | collective-permute-start | bytes 884744 | tf_op jit(solution)/shard_map/ppermute | solution.py:813
  22.0 26.7 %collective-permute-start.9 = (bf16[48,5120]{1,0:T(8,128)(2,1)S(1)}, bf16[48,5120]{1,0:T(8,128)(2,1)S(1)}, u32[]{:S(2)}, u32[]{:S(2)}) collective-permute-start(bf16[48,5120]{1,0:T(8,128)(2,1)S(1)} %fusion.10.refs_5_), channel_id=1, source_target_pairs={{0,8},{4,12},{8,0},{12,4},{16,24},{20,28},{24,16},{28,20},{1,9},{5... | collective-permute-start | bytes 1474568 | tf_op jit(solution)/shard_map/ppermute | solution.py:813
  23.6 25.1 %collective-permute-start.10 = (bf16[48,5120]{1,0:T(8,128)(2,1)S(1)}, bf16[48,5120]{1,0:T(8,128)(2,1)S(1)}, u32[]{:S(2)}, u32[]{:S(2)}) collective-permute-start(bf16[48,5120]{1,0:T(8,128)(2,1)S(1)} %fusion.10.refs_5_), channel_id=1, source_target_pairs={{0,16},{4,20},{8,24},{12,28},{16,0},{20,4},{24,8},{28,12},{1,17},{... | collective-permute-start | bytes 1474568 | tf_op jit(solution)/shard_map/ppermute | solution.py:813
  24.1 24.6 %collective-permute-start.11 = (bf16[48,5120]{1,0:T(8,128)(2,1)S(1)}, bf16[48,5120]{1,0:T(8,128)(2,1)S(1)}, u32[]{:S(2)}, u32[]{:S(2)}) collective-permute-start(bf16[48,5120]{1,0:T(8,128)(2,1)S(1)} %fusion.10.refs_5_), channel_id=1, source_target_pairs={{0,24},{4,28},{8,16},{12,20},{16,8},{20,12},{24,0},{28,4},{1,25},{... | collective-permute-start | bytes 1474568 | tf_op jit(solution)/shard_map/ppermute | solution.py:813
  25.6 23.1 %collective-permute-start.12 = (bf16[48,5120]{1,0:T(8,128)(2,1)S(1)}, bf16[48,5120]{1,0:T(8,128)(2,1)S(1)}, u32[]{:S(2)}, u32[]{:S(2)}) collective-permute-start(bf16[48,5120]{1,0:T(8,128)(2,1)S(1)} %fusion.10.refs_5_), channel_id=1, source_target_pairs={{0,4},{4,0},{8,12},{12,8},{16,20},{20,16},{24,28},{28,24},{1,5},{5... | collective-permute-start | bytes 1474568 | tf_op jit(solution)/shard_map/ppermute | solution.py:813
  49.3 2.2 %collective-permute-start.14 = (bf16[48,5120]{1,0:T(8,128)(2,1)S(1)}, bf16[48,5120]{1,0:T(8,128)(2,1)S(1)}, u32[]{:S(2)}, u32[]{:S(2)}) collective-permute-start(bf16[48,5120]{1,0:T(8,128)(2,1)S(1)} %collective-permute-done.10.refs_7_), channel_id=1, source_target_pairs={{0,4},{4,0},{8,12},{12,8},{16,20},{20,16},{24,28},{28,24},{1,5},{5... | collective-permute-start | bytes 1474568 | tf_op jit(solution)/shard_map/ppermute | solution.py:813
  49.4 2.8 %collective-permute-start.15 = (bf16[48,5120]{1,0:T(8,128)(2,1)S(1)}, bf16[48,5120]{1,0:T(8,128)(2,1)S(1)}, u32[]{:S(2)}, u32[]{:S(2)}) collective-permute-start(bf16[48,5120]{1,0:T(8,128)(2,1)S(1)} %collective-permute-done.11.refs_8_), channel_id=1, source_target_pairs={{0,4},{4,0},{8,12},{12,8},{16,20},{20,16},{24,28},{28,24},{1,5},{5... | collective-permute-start | bytes 1474568 | tf_op jit(solution)/shard_map/ppermute | solution.py:813
  77.9 5.9 %collective-permute-start.16 = (bf16[4,5,48,1152]{3,2,1,0:T(8,128)(2,1)S(1)}, bf16[4,5,48,1152]{3,2,1,0:T(8,128)(2,1)S(1)}, u32[]{:S(2)}, u32[]{:S(2)}) collective-permute-start(bf16[4,5,48,1152]{3,2,1,0:T(8,128)(2,1)S(1)} %get-tuple-element.120), channel_id=1, source_target_pairs={{0,4},{4,0},{8,12},{12,8},{16,20},{20,16},{24,28},{28,24},{1,5},{5... | collective-permute-start | bytes 6635528 | tf_op jit(solution)/shard_map/ppermute | solution.py:813
  84.5 29.6 %collective-permute-start.17 = (bf16[5,48,1152]{2,1,0:T(8,128)(2,1)S(1)}, bf16[5,48,1152]{2,1,0:T(8,128)(2,1)S(1)}, u32[]{:S(2)}, u32[]{:S(2)}) collective-permute-start(bf16[5,48,1152]{2,1,0:T(8,128)(2,1)S(1)} %get-tuple-element.192), channel_id=1, source_target_pairs={{0,8},{4,12},{8,0},{12,4},{16,24},{20,28},{24,16},{28,20},{1,9},{5... | collective-permute-start | bytes 1658888 | tf_op jit(solution)/shard_map/ppermute | solution.py:813
  86.1 28.1 %collective-permute-start.18 = (bf16[5,48,1152]{2,1,0:T(8,128)(2,1)S(1)}, bf16[5,48,1152]{2,1,0:T(8,128)(2,1)S(1)}, u32[]{:S(2)}, u32[]{:S(2)}) collective-permute-start(bf16[5,48,1152]{2,1,0:T(8,128)(2,1)S(1)} %get-tuple-element.191), channel_id=1, source_target_pairs={{0,16},{4,20},{8,24},{12,28},{16,0},{20,4},{24,8},{28,12},{1,17},{... | collective-permute-start | bytes 1658888 | tf_op jit(solution)/shard_map/ppermute | solution.py:813
  86.7 27.5 %collective-permute-start.19 = (bf16[5,48,1152]{2,1,0:T(8,128)(2,1)S(1)}, bf16[5,48,1152]{2,1,0:T(8,128)(2,1)S(1)}, u32[]{:S(2)}, u32[]{:S(2)}) collective-permute-start(bf16[5,48,1152]{2,1,0:T(8,128)(2,1)S(1)} %get-tuple-element.190), channel_id=1, source_target_pairs={{0,24},{4,28},{8,16},{12,20},{16,8},{20,12},{24,0},{28,4},{1,25},{... | collective-permute-start | bytes 1658888 | tf_op jit(solution)/shard_map/ppermute | solution.py:813
  114.1 2.6 %collective-permute-start.20 = (bf16[4,48,2432]{2,1,0:T(8,128)(2,1)S(1)}, bf16[4,48,2432]{2,1,0:T(8,128)(2,1)S(1)}, u32[]{:S(2)}, u32[]{:S(2)}) collective-permute-start(bf16[4,48,2432]{2,1,0:T(8,128)(2,1)S(1)} %get-tuple-element.135), channel_id=1, source_target_pairs={{0,4},{4,0},{8,12},{12,8},{16,20},{20,16},{24,28},{28,24},{1,5},{5... | collective-permute-start | bytes 2801672 | tf_op jit(solution)/shard_map/ppermute | solution.py:813
  116.9 16.6 %collective-permute-start.21 = (bf16[3,48,1152]{2,1,0:T(8,128)(2,1)S(1)}, bf16[3,48,1152]{2,1,0:T(8,128)(2,1)S(1)}, u32[]{:S(2)}, u32[]{:S(2)}) collective-permute-start(bf16[3,48,1152]{2,1,0:T(8,128)(2,1)S(1)} %pad_maximum_fusion), channel_id=1, source_target_pairs={{0,2},{1,3},{2,0},{3,1},{4,5},{5,4},{6,7},{7,6},{8,10},{9,11},{10,... | collective-permute-start | bytes 995336 | tf_op jit(solution)/shard_map/ppermute | solution.py:829
  119.3 14.1 %collective-permute-start.22 = (bf16[48,2432]{1,0:T(8,128)(2,1)S(1)}, bf16[48,2432]{1,0:T(8,128)(2,1)S(1)}, u32[]{:S(2)}, u32[]{:S(2)}) collective-permute-start(bf16[48,2432]{1,0:T(8,128)(2,1)S(1)} %get-tuple-element.197), channel_id=1, source_target_pairs={{0,8},{4,12},{8,0},{12,4},{16,24},{20,28},{24,16},{28,20},{1,9},{5... | collective-permute-start | bytes 700424 | tf_op jit(solution)/shard_map/ppermute | solution.py:813
  120.9 12.6 %collective-permute-start.23 = (bf16[48,2432]{1,0:T(8,128)(2,1)S(1)}, bf16[48,2432]{1,0:T(8,128)(2,1)S(1)}, u32[]{:S(2)}, u32[]{:S(2)}) collective-permute-start(bf16[48,2432]{1,0:T(8,128)(2,1)S(1)} %get-tuple-element.196), channel_id=1, source_target_pairs={{0,16},{4,20},{8,24},{12,28},{16,0},{20,4},{24,8},{28,12},{1,17},{... | collective-permute-start | bytes 700424 | tf_op jit(solution)/shard_map/ppermute | solution.py:813
  122.4 11.0 %collective-permute-start.24 = (bf16[48,2432]{1,0:T(8,128)(2,1)S(1)}, bf16[48,2432]{1,0:T(8,128)(2,1)S(1)}, u32[]{:S(2)}, u32[]{:S(2)}) collective-permute-start(bf16[48,2432]{1,0:T(8,128)(2,1)S(1)} %get-tuple-element.195), channel_id=1, source_target_pairs={{0,24},{4,28},{8,16},{12,20},{16,8},{20,12},{24,0},{28,4},{1,25},{... | collective-permute-start | bytes 700424 | tf_op jit(solution)/shard_map/ppermute | solution.py:813
  133.7 8.3 %collective-permute-start.26 = (bf16[48,2432]{1,0:T(8,128)(2,1)S(1)}, bf16[48,2432]{1,0:T(8,128)(2,1)S(1)}, u32[]{:S(2)}, u32[]{:S(2)}) collective-permute-start(bf16[48,2432]{1,0:T(8,128)(2,1)S(1)} %fusion.8), channel_id=1, source_target_pairs={{0,1},{1,0},{2,3},{3,2},{4,6},{5,7},{6,4},{7,5},{8,9},{9,8},{10,11... | collective-permute-start | bytes 700424 | tf_op jit(solution)/shard_map/ppermute | solution.py:829
  135.6 6.5 %collective-permute-start.27 = (bf16[48,896]{1,0:T(8,128)(2,1)S(1)}, bf16[48,896]{1,0:T(8,128)(2,1)S(1)}, u32[]{:S(2)}, u32[]{:S(2)}) collective-permute-start(bf16[48,896]{1,0:T(8,128)(2,1)S(1)} %get-tuple-element.202), channel_id=1, source_target_pairs={{0,8},{4,12},{8,0},{12,4},{16,24},{20,28},{24,16},{28,20},{1,9},{5... | collective-permute-start | bytes 258056 | tf_op jit(solution)/shard_map/ppermute | solution.py:813
  137.2 5.4 %collective-permute-start.28 = (bf16[48,896]{1,0:T(8,128)(2,1)S(1)}, bf16[48,896]{1,0:T(8,128)(2,1)S(1)}, u32[]{:S(2)}, u32[]{:S(2)}) collective-permute-start(bf16[48,896]{1,0:T(8,128)(2,1)S(1)} %get-tuple-element.201), channel_id=1, source_target_pairs={{0,16},{4,20},{8,24},{12,28},{16,0},{20,4},{24,8},{28,12},{1,17},{... | collective-permute-start | bytes 258056 | tf_op jit(solution)/shard_map/ppermute | solution.py:813
  138.7 5.4 %collective-permute-start.29 = (bf16[48,896]{1,0:T(8,128)(2,1)S(1)}, bf16[48,896]{1,0:T(8,128)(2,1)S(1)}, u32[]{:S(2)}, u32[]{:S(2)}) collective-permute-start(bf16[48,896]{1,0:T(8,128)(2,1)S(1)} %get-tuple-element.200), channel_id=1, source_target_pairs={{0,24},{4,28},{8,16},{12,20},{16,8},{20,12},{24,0},{28,4},{1,25},{... | collective-permute-start | bytes 258056 | tf_op jit(solution)/shard_map/ppermute | solution.py:813
  139.2 16.2 %collective-permute-start.33 = (bf16[48,2304]{1,0:T(8,128)(2,1)S(1)}, bf16[48,2304]{1,0:T(8,128)(2,1)S(1)}, u32[]{:S(2)}, u32[]{:S(2)}) collective-permute-start(bf16[48,2304]{1,0:T(8,128)(2,1)S(1)} %pad_maximum_fusion.2), channel_id=1, source_target_pairs={{0,1},{1,0},{2,3},{3,2},{4,6},{5,7},{6,4},{7,5},{8,9},{9,8},{10,11... | collective-permute-start | bytes 663560 | tf_op jit(solution)/shard_map/ppermute | solution.py:829
  144.3 7.0 %collective-permute-start.30 = (bf16[48,896]{1,0:T(8,128)(2,1)S(1)}, bf16[48,896]{1,0:T(8,128)(2,1)S(1)}, u32[]{:S(2)}, u32[]{:S(2)}) collective-permute-start(bf16[48,896]{1,0:T(8,128)(2,1)S(1)} %fusion.11), channel_id=1, source_target_pairs={{0,2},{1,3},{2,0},{3,1},{4,5},{5,4},{6,7},{7,6},{8,10},{9,11},{10,... | collective-permute-start | bytes 258056 | tf_op jit(solution)/shard_map/ppermute | solution.py:829
  149.2 10.5 %collective-permute-start.31 = (bf16[48,2432]{1,0:T(8,128)(2,1)S(1)}, bf16[48,2432]{1,0:T(8,128)(2,1)S(1)}, u32[]{:S(2)}, u32[]{:S(2)}) collective-permute-start(bf16[48,2432]{1,0:T(8,128)(2,1)S(1)} %get-tuple-element.165), channel_id=1, source_target_pairs={{0,2},{1,3},{2,0},{3,1},{4,5},{5,4},{6,7},{7,6},{8,10},{9,11},{10,... | collective-permute-start | bytes 700424 | tf_op jit(solution)/shard_map/ppermute | solution.py:829
  151.4 5.1 %collective-permute-start.32 = (bf16[48,896]{1,0:T(8,128)(2,1)S(1)}, bf16[48,896]{1,0:T(8,128)(2,1)S(1)}, u32[]{:S(2)}, u32[]{:S(2)}) collective-permute-start(bf16[48,896]{1,0:T(8,128)(2,1)S(1)} %get-tuple-element.166), channel_id=1, source_target_pairs={{0,1},{1,0},{2,3},{3,2},{4,6},{5,7},{6,4},{7,5},{8,9},{9,8},{10,11... | collective-permute-start | bytes 258056 | tf_op jit(solution)/shard_map/ppermute | solution.py:829
  (13 other events, 142.8 us)

commit v4 on v3

--- a/solution.py
+++ b/solution.py
@@ -537,44 +537,55 @@
     lane = lax.broadcasted_iota(jnp.int32, (1, 128), 1)
     low = lane < 64
     kept = {}
-    for pair in range(GROUP // 2):
-        columns = slice(pair * 128, pair * 128 + 128)
-        grad = grad_ref[0, :, columns]
+    turned_keys = {}
+
+    def parts(head):
+        columns = slice(head // 2 * 128, head // 2 * 128 + 128)
+        return columns, head % 2, grad_ref[0, :, columns]
+
+    def score_gradients(head):
+        columns, half, grad = parts(head)
+        mine = low if half == 0 else jnp.logical_not(low)
+        value = projected_ref[0, :KEYS, 2 * WIDE + columns.start : 2 * WIDE + columns.stop]
+        own_value = jnp.where(mine, value, bf16(0))
+        inverse = inverse_ref[0, 0, head : head + 1].astype(bf16)
+        delta = delta_ref[0, 0, head : head + 1]
+        for start, width, keys in QUERY_BLOCKS:
+            block = slice(start, start + width)
+            change = dot(own_value[:keys], grad[block], NT) - delta[:, block]
+            probability = exp_ref[0, head, :keys, block] * inverse[:, block]
+            prob_scr[half, :keys, block] = probability
+            grad_scr[half, :keys, block] = probability * change.astype(bf16)
+
+    def input_gradients(head):
+        columns, half, grad = parts(head)
+        pair = head // 2
         query = projected_ref[0, :, columns]
-        value = projected_ref[0, :KEYS, 2 * WIDE + pair * 128 : 2 * WIDE + pair * 128 + 128]
-        turned = projected_ref[0, :KEYS, WIDE + pair * 128 : WIDE + pair * 128 + 128].T
-        for half in range(2):
-            head = 2 * pair + half
-            mine = low if half == 0 else jnp.logical_not(low)
-            own_value = jnp.where(mine, value, bf16(0))
-            inverse = inverse_ref[0, 0, head : head + 1].astype(bf16)
-            delta = delta_ref[0, 0, head : head + 1]
-            side = slice(64 * half, 64 * half + 64)
-            for start, width, keys in QUERY_BLOCKS:
-                block = slice(start, start + width)
-                change = dot(own_value[:keys], grad[block], NT) - delta[:, block]
-                probability = exp_ref[0, head, :keys, block] * inverse[:, block]
-                prob_scr[half, :keys, block] = probability
-                grad_scr[half, :keys, block] = probability * change.astype(bf16)
-            for start, width, keys in QUERY_BLOCKS:
-                block = slice(start, start + width)
-                turned_scr[head * 64 : (head + 1) * 64, block] = dot(
-                    turned[side, :keys], grad_scr[half, :keys, block], NN
-                ) * (HEAD_DIM**-0.5)
-            for start, stop, seen in KEY_RANGES:
-                value_grad = dot(prob_scr[half, start:stop, seen:], grad[seen:], NN)
-                key_grad = dot(grad_scr[half, start:stop, seen:], query[seen:], NN)
-                if half == 0:
-                    kept[start] = (value_grad, key_grad)
-                else:
-                    at = slice(WIDE + pair * 128, WIDE + pair * 128 + 128)
-                    back_ref[0, start:stop, at] = jnp.where(low, kept[start][1], key_grad).astype(
-                        bf16
-                    )
-                    at = slice(2 * WIDE + pair * 128, 2 * WIDE + pair * 128 + 128)
-                    back_ref[0, start:stop, at] = jnp.where(low, kept[start][0], value_grad).astype(
-                        bf16
-                    )
+        if half == 0:
+            turned_keys[pair] = projected_ref[0, :KEYS, WIDE + columns.start : WIDE + columns.stop].T
+        turned = turned_keys[pair]
+        side = slice(64 * half, 64 * half + 64)
+        for start, width, keys in QUERY_BLOCKS:
+            block = slice(start, start + width)
+            turned_scr[head * 64 : (head + 1) * 64, block] = dot(
+                turned[side, :keys], grad_scr[half, :keys, block], NN
+            ) * (HEAD_DIM**-0.5)
+        for start, stop, seen in KEY_RANGES:
+            value_grad = dot(prob_scr[half, start:stop, seen:], grad[seen:], NN)
+            key_grad = dot(grad_scr[half, start:stop, seen:], query[seen:], NN)
+            if half == 0:
+                kept[start] = (value_grad, key_grad)
+            else:
+                at = slice(WIDE + columns.start, WIDE + columns.stop)
+                back_ref[0, start:stop, at] = jnp.where(low, kept[start][1], key_grad).astype(bf16)
+                at = slice(2 * WIDE + columns.start, 2 * WIDE + columns.stop)
+                back_ref[0, start:stop, at] = jnp.where(low, kept[start][0], value_grad).astype(bf16)
+
+    score_gradients(0)
+    for head in range(GROUP):
+        if head + 1 < GROUP:
+            score_gradients(head + 1)
+        input_gradients(head)
     back_ref[0, :KEYS, :WIDE] = turned_scr[...].T[:KEYS].astype(bf16)
 
     back = back_ref[0, :KEYS]

time: 162 us -> 159 us (0.981)
  Pallas kernels: 102 us -> 99.5 us
    pallas_call x2, Pallas kernels: 36.6 us -> 33.8 us  [backward(): pl.pallas_call(functools.partial(backward_kernel, pieces), grid=(groups,...]
  transfers between devices with their start and end apart: 34 -> 34, of which waited for: 13 -> 14; matrix products, arithmetic and copies ran while one was open for 2% -> 2% of each run, Pallas kernels for 45% -> 44%
where the time goes in v4:
time: 159 us
  Pallas kernels  99.5 us (63%)
  starting transfers between devices  34.9 us (22%)
  waiting for transfers between devices  17.6 us (11%)
  local copies, waits for them, and re-layouts  2.82 us (2%)
  other arithmetic  2.78 us (2%)
    pallas_call x2, Pallas kernels, backward(): pl.pallas_call(functools.partial(backward_kernel, pieces), grid=(groups,...  33.8 us
    pallas_call x1, Pallas kernels, forward(): pl.pallas_call(functools.partial(forward_kernel, pieces, len(biases), chu...  25.7 us
    pallas_call x1, Pallas kernels, attend(): pl.pallas_call(functools.partial(attend_kernel, len(parts)), grid=(GROUPS...  23 us
    ppermute x23, starting transfers between devices, swap(): return lax.ppermute(values, 'tok', [(i, i ^ mask) for i in range(size)])  17 us
    ppermute x8, starting transfers between devices, swap_half_line(): return lax.ppermute(values.astype(bf16), ('tok', 'mlp'), pairs)  14.3 us
    ppermute x8, waiting for transfers between devices, swap_half_line(): return lax.ppermute(values.astype(bf16), ('tok', 'mlp'), pairs)  8.1 us
    ppermute x23, waiting for transfers between devices, swap(): return lax.ppermute(values, 'tok', [(i, i ^ mask) for i in range(size)])  6.68 us
    pallas_call x1, Pallas kernels, mixed_gradient(): pl.pallas_call(mixed_gradient_kernel, grid=(seqs, GROUPS // each), in_spe...  5.45 us
  transfers between devices with their start and end apart: 34, of which 14 were waited for; matrix products, arithmetic and copies ran while one was open for 2% of the time, Pallas kernels for 44%

profile of v4, /device:TPU:0, one launch (start us, length us, event | category | flops | bytes accessed | tf_op | source)
XLA Modules:
  0.0 158.7 jit_solution(596105250817443265)
XLA Ops:
  0.7 1.9 %prepare.1 = (bf16[64,1024]{1,0:T(8,128)(2,1)}, bf16[48,1024]{1,0:T(8,128)(2,1)}, f32[8,384]{1,0:T(8,128)}, f32[384,8]{1,0:T(8,128)}, f32[1,2048]{1,0:T(1,128)}) custom-call(bf16[48,512]{1,0:T(8,128)(2,1)} %one_ref.1, bf16[48,512]{1,0:T(8,128)(2,1)} %bitcast.63, bf16[512]{0:T(512)(128)(2,1)} %hidden_bias_ref.1, bf16[128,384]{1,0:T(8,128)(2,1)} %out_ref.1, ...), custom_call_target="tpu_custom_call" | custom-call | flops 2200000000 | bytes 1024 | tf_op jit(solution)/shard_map/prepare/pallas_call | solution.py:107
  2.5 4.0 %collective-permute-start = (bf16[64,1024]{1,0:T(8,128)(2,1)}, bf16[64,1024]{1,0:T(8,128)(2,1)S(1)}, u32[]{:S(2)}, u32[]{:S(2)}) collective-permute-start(bf16[64,1024]{1,0:T(8,128)(2,1)} %get-tuple-element.100.refs_0_), channel_id=1, source_target_pairs={{0,2},{1,3},{2,0},{3,1},{4,5},{5,4},{6,7},{7,6},{8,10},{9,11},{10,... | collective-permute-start | bytes 393224 | tf_op jit(solution)/shard_map/ppermute | solution.py:840
  6.6 1.5 collective-permute-start.2
  8.1 1.5 collective-permute-start.3
  11.4 1.8 %collective-permute-start.1 = (bf16[2,64,1024]{2,1,0:T(8,128)(2,1)S(1)}, bf16[2,64,1024]{2,1,0:T(8,128)(2,1)S(1)}, u32[]{:S(2)}, u32[]{:S(2)}) collective-permute-start(bf16[2,64,1024]{2,1,0:T(8,128)(2,1)S(1)} %pad_maximum_fusion.1), channel_id=1, source_target_pairs={{0,1},{1,0},{2,3},{3,2},{4,6},{5,7},{6,4},{7,5},{8,9},{9,8},{10,11... | collective-permute-start | bytes 786440 | tf_op jit(solution)/shard_map/ppermute | solution.py:840
  14.2 1.1 collective-permute-done.2.refs_1_
  15.8 1.2 collective-permute-start.7
  18.6 1.7 %collective-permute-done.1 = bf16[2,64,1024]{2,1,0:T(8,128)(2,1)S(1)} collective-permute-done((bf16[2,64,1024]{2,1,0:T(8,128)(2,1)S(1)}, bf16[2,64,1024]{2,1,0:T(8,128)(2,1)S(1)}, u32[]{:S(2)}, u32[]{:S(2)}) %collective-permute-start.1) | collective-permute-done | bytes 262176 | tf_op jit(solution)/shard_map/ppermute | solution.py:840
  20.3 1.7 %collective-permute-done.4.refs_3_ = bf16[48,3072]{1,0:T(8,128)(2,1)S(1)} collective-permute-done((bf16[48,3072]{1,0:T(8,128)(2,1)S(1)}, bf16[48,3072]{1,0:T(8,128)(2,1)S(1)}, u32[]{:S(2)}, u32[]{:S(2)}) %collective-permute-start.4) | collective-permute-done | bytes 294944 | tf_op jit(solution)/shard_map/ppermute | solution.py:830
  22.0 1.6 collective-permute-start.9
  24.1 1.5 collective-permute-start.11
  25.7 23.0 %attend.1 = (bf16[2,640,3072]{2,1,0:T(8,128)(2,1)}, bf16[2,640,1024]{2,1,0:T(8,128)(2,1)S(1)}, bf16[2,16,592,640]{3,2,1,0:T(8,128)(2,1)}, f32[2,4,8,640]{3,2,1,0:T(8,128)}, bf16[384,3072]{1,0:T(8,128)(2,1)}) custom-call(s32[1]{0:T(128)} %bitcast.me_ref, bf16[2,640,384]{2,1,0:T(8,128)(2,1)S(1)} %get-tuple-element.104.normed_ref, f32[1,2048]{1,0:T(1,128)S(1)} %copy-done.10, ...), custom_call_target="tpu_custom_call" | custom-call | flops 24199999488 | bytes 1024 | tf_op jit(solution)/shard_map/attend/pallas_call | solution.py:238
  52.2 25.7 %forward.1 = (bf16[1176,384]{1,0:T(8,128)(2,1)}, f32[2,640,384]{2,1,0:T(8,128)S(1)}, bf16[2,640,384]{2,1,0:T(8,128)(2,1)S(1)}, bf16[384,1024]{1,0:T(8,128)(2,1)S...) custom-call(s32[1]{0:T(128)} %bitcast.me_ref, bf16[1176,384]{1,0:T(8,128)(2,1)S(1)} %copy-done.2, ...), custom_call_target="tpu_custom_call" | custom-call | flops 32999999488 | bytes 1024 | tf_op jit(solution)/shard_map/forward/pallas_call | solution.py:440
  78.3 5.4 %mixed_gradient.1 = (bf16[2,640,1024]{2,1,0:T(8,128)(2,1)}, f32[2,4,8,640]{3,2,1,0:T(8,128)}) custom-call(bf16[2,640,384]{2,1,0:T(8,128)(2,1)S(1)} %get-tuple-element.117.branch_ref, bf16[384,1024]{1,0:T(8,128)(2,1)S(1)} %get-tuple-element.118.out_wide_ref, bf16[2,640,1024]{2,1,0:T(8,128)(2,1)S(1)} %get-tuple-element.109.refs_4_.mixed_ref), custom_call_target="tpu_custom_call" | custom-call | flops 5500000256 | bytes 1024 | tf_op jit(solution)/shard_map/mixed_gradient/pallas_call | solution.py:501
  84.5 1.6 collective-permute-start.17
  86.7 1.4 collective-permute-start.19
  88.1 24.0 %backward.2 = (bf16[2,640,2304]{2,1,0:T(8,128)(2,1)S(1)}, bf16[4,48,2432]{2,1,0:T(8,128)(2,1)S(1)}, bf16[4,48,2432]{2,1,0:T(8,128)(2,1)S(1)}) custom-call(s32[1]{0:T(128)} %bitcast.me_ref, bf16[2,640,1024]{2,1,0:T(8,128)(2,1)} %get-tuple-element.123.refs_0_, f32[2,4,8,640]{3,2,1,0:T(8,128)} %get-tuple-element.124.refs_1_, bf16[2,640,384]{2,1,0:T(8,128)(2,1)} %copy-done.6, ...), custom_call_target="tpu_custom_call" | custom-call | flops 36300001280 | bytes 1024 | tf_op jit(solution)/shard_map/backward/pallas_call | solution.py:659
  112.6 2.0 %collective-permute-done.20 = bf16[4,48,2432]{2,1,0:T(8,128)(2,1)S(1)} collective-permute-done((bf16[4,48,2432]{2,1,0:T(8,128)(2,1)S(1)}, bf16[4,48,2432]{2,1,0:T(8,128)(2,1)S(1)}, u32[]{:S(2)}, u32[]{:S(2)}) %collective-permute-start.20) | collective-permute-done | bytes 933920 | tf_op jit(solution)/shard_map/ppermute | solution.py:824
  114.9 2.4 %collective-permute-start.21 = (bf16[3,48,1152]{2,1,0:T(8,128)(2,1)S(1)}, bf16[3,48,1152]{2,1,0:T(8,128)(2,1)S(1)}, u32[]{:S(2)}, u32[]{:S(2)}) collective-permute-start(bf16[3,48,1152]{2,1,0:T(8,128)(2,1)S(1)} %pad_maximum_fusion), channel_id=1, source_target_pairs={{0,2},{1,3},{2,0},{3,1},{4,5},{5,4},{6,7},{7,6},{8,10},{9,11},{10,... | collective-permute-start | bytes 995336 | tf_op jit(solution)/shard_map/ppermute | solution.py:840
  117.3 1.6 collective-permute-start.22
  118.9 1.6 collective-permute-start.23
  120.9 9.9 %backward.3 = (bf16[2,640,768]{2,1,0:T(8,128)(2,1)S(1)}, bf16[4,48,896]{2,1,0:T(8,128)(2,1)S(1)}, bf16[4,48,896]{2,1,0:T(8,128)(2,1)S(1)}) custom-call(s32[1]{0:T(128)} %bitcast.me_ref, bf16[2,640,1024]{2,1,0:T(8,128)(2,1)} %get-tuple-element.123.refs_0_, f32[2,4,8,640]{3,2,1,0:T(8,128)} %get-tuple-element.124.refs_1_, bf16[2,640,384]{2,1,0:T(8,128)(2,1)} %copy-done.6, ...), custom_call_target="tpu_custom_call" | custom-call | flops 12099999744 | bytes 1024 | tf_op jit(solution)/shard_map/backward/pallas_call | solution.py:659
  131.0 1.1 collective-permute-start.26
  132.9 1.6 collective-permute-start.27
  134.4 1.6 collective-permute-start.28
  136.4 1.1 collective-permute-start.33
  137.5 2.2 %collective-permute-done.26 = bf16[48,2432]{1,0:T(8,128)(2,1)S(1)} collective-permute-done((bf16[48,2432]{1,0:T(8,128)(2,1)S(1)}, bf16[48,2432]{1,0:T(8,128)(2,1)S(1)}, u32[]{:S(2)}, u32[]{:S(2)}) %collective-permute-start.26) | collective-permute-done | bytes 233504 | tf_op jit(solution)/shard_map/ppermute | solution.py:840
  139.9 1.5 collective-permute-done.29
  142.6 3.9 %early_gradient.1.early_ref = f32[2,592,384]{2,1,0:T(8,128)S(1)} custom-call(bf16[2,640,2304]{2,1,0:T(8,128)(2,1)S(1)} %get-tuple-element.159.back_ref, bf16[384,3072]{1,0:T(8,128)(2,1)S(1)} %copy-done.5), custom_call_target="tpu_custom_call" | custom-call | flops 5500000256 | bytes 1024 | tf_op jit(solution)/shard_map/early_gradient/pallas_call | solution.py:701
  146.5 2.1 %collective-permute-start.31 = (bf16[48,2432]{1,0:T(8,128)(2,1)S(1)}, bf16[48,2432]{1,0:T(8,128)(2,1)S(1)}, u32[]{:S(2)}, u32[]{:S(2)}) collective-permute-start(bf16[48,2432]{1,0:T(8,128)(2,1)S(1)} %get-tuple-element.165), channel_id=1, source_target_pairs={{0,2},{1,3},{2,0},{3,1},{4,5},{5,4},{6,7},{7,6},{8,10},{9,11},{10,... | collective-permute-start | bytes 700424 | tf_op jit(solution)/shard_map/ppermute | solution.py:840
  149.5 3.2 %input_gradient.1 = f32[1176,384]{1,0:T(8,128)} custom-call(bf16[1176,384]{1,0:T(8,128)(2,1)S(1)} %copy-done.2, f32[2,640,384]{2,1,0:T(8,128)S(1)} %get-tuple-element.115.middle_grad_ref, f32[8,384]{1,0:T(8,128)S(1)} %copy-done.9, f32[2,592,384]{2,1,0:T(8,128)S(1)} %early_gradient.1.early_ref, bf16[2,640,768]{2,1,0:T(8,128)(2,1)S(1)} %get-tuple-element.164.back_ref, ...), custom_call_target="tpu_custom_call" | custom-call | flops 4400000000 | bytes 1024 | tf_op jit(solution)/shard_map/input_gradient/pallas_call | solution.py:727
  153.2 3.7 %collective-permute-done.31.early_line_ref = bf16[48,2432]{1,0:T(8,128)(2,1)S(1)} collective-permute-done((bf16[48,2432]{1,0:T(8,128)(2,1)S(1)}, bf16[48,2432]{1,0:T(8,128)(2,1)S(1)}, u32[]{:S(2)}, u32[]{:S(2)}) %collective-permute-start.31) | collective-permute-done | bytes 233504 | tf_op jit(solution)/shard_map/ppermute | solution.py:840
  (93 shorter events, 17.8 us)
Async XLA Ops:
  2.5 8.0 %collective-permute-start = (bf16[64,1024]{1,0:T(8,128)(2,1)}, bf16[64,1024]{1,0:T(8,128)(2,1)S(1)}, u32[]{:S(2)}, u32[]{:S(2)}) collective-permute-start(bf16[64,1024]{1,0:T(8,128)(2,1)} %get-tuple-element.100.refs_0_), channel_id=1, source_target_pairs={{0,2},{1,3},{2,0},{3,1},{4,5},{5,4},{6,7},{7,6},{8,10},{9,11},{10,... | collective-permute-start | bytes 393224 | tf_op jit(solution)/shard_map/ppermute | solution.py:840
  6.6 8.7 %collective-permute-start.2 = (bf16[48,3072]{1,0:T(8,128)(2,1)S(1)}, bf16[48,3072]{1,0:T(8,128)(2,1)S(1)}, u32[]{:S(2)}, u32[]{:S(2)}) collective-permute-start(bf16[48,3072]{1,0:T(8,128)(2,1)S(1)} %copy-done.3), channel_id=1, source_target_pairs={{0,8},{4,20},{8,0},{12,28},{16,24},{20,4},{24,16},{28,12},{1,9},{5... | collective-permute-start | bytes 884744 | tf_op jit(solution)/shard_map/ppermute | solution.py:830
  8.1 7.7 %collective-permute-start.3 = (bf16[48,3072]{1,0:T(8,128)(2,1)S(1)}, bf16[48,3072]{1,0:T(8,128)(2,1)S(1)}, u32[]{:S(2)}, u32[]{:S(2)}) collective-permute-start(bf16[48,3072]{1,0:T(8,128)(2,1)S(1)} %copy-done.3), channel_id=1, source_target_pairs={{0,16},{4,12},{8,24},{12,4},{16,0},{20,28},{24,8},{28,20},{1,17},{... | collective-permute-start | bytes 884744 | tf_op jit(solution)/shard_map/ppermute | solution.py:830
  9.6 14.0 %collective-permute-start.5 = (bf16[48,3072]{1,0:T(8,128)(2,1)S(1)}, bf16[48,3072]{1,0:T(8,128)(2,1)S(1)}, u32[]{:S(2)}, u32[]{:S(2)}) collective-permute-start(bf16[48,3072]{1,0:T(8,128)(2,1)S(1)} %copy-done.3), channel_id=1, source_target_pairs={{0,4},{4,0},{8,12},{12,8},{16,20},{20,16},{24,28},{28,24},{1,5},{5... | collective-permute-start | bytes 884744 | tf_op jit(solution)/shard_map/ppermute | solution.py:824
  11.4 8.8 %collective-permute-start.1 = (bf16[2,64,1024]{2,1,0:T(8,128)(2,1)S(1)}, bf16[2,64,1024]{2,1,0:T(8,128)(2,1)S(1)}, u32[]{:S(2)}, u32[]{:S(2)}) collective-permute-start(bf16[2,64,1024]{2,1,0:T(8,128)(2,1)S(1)} %pad_maximum_fusion.1), channel_id=1, source_target_pairs={{0,1},{1,0},{2,3},{3,2},{4,6},{5,7},{6,4},{7,5},{8,9},{9,8},{10,11... | collective-permute-start | bytes 786440 | tf_op jit(solution)/shard_map/ppermute | solution.py:840
  15.3 8.9 %collective-permute-start.6 = (bf16[48,3072]{1,0:T(8,128)(2,1)S(1)}, bf16[48,3072]{1,0:T(8,128)(2,1)S(1)}, u32[]{:S(2)}, u32[]{:S(2)}) collective-permute-start(bf16[48,3072]{1,0:T(8,128)(2,1)S(1)} %collective-permute-done.2.refs_1_), channel_id=1, source_target_pairs={{0,4},{4,0},{8,12},{12,8},{16,20},{20,16},{24,28},{28,24},{1,5},{5... | collective-permute-start | bytes 884744 | tf_op jit(solution)/shard_map/ppermute | solution.py:824
  15.3 6.7 %collective-permute-start.4 = (bf16[48,3072]{1,0:T(8,128)(2,1)S(1)}, bf16[48,3072]{1,0:T(8,128)(2,1)S(1)}, u32[]{:S(2)}, u32[]{:S(2)}) collective-permute-start(bf16[48,3072]{1,0:T(8,128)(2,1)S(1)} %collective-permute-done.2.refs_1_), channel_id=1, source_target_pairs={{0,16},{4,12},{8,24},{12,4},{16,0},{20,28},{24,8},{28,20},{1,17},{... | collective-permute-start | bytes 884744 | tf_op jit(solution)/shard_map/ppermute | solution.py:830
  15.8 9.8 %collective-permute-start.7 = (bf16[48,3072]{1,0:T(8,128)(2,1)S(1)}, bf16[48,3072]{1,0:T(8,128)(2,1)S(1)}, u32[]{:S(2)}, u32[]{:S(2)}) collective-permute-start(bf16[48,3072]{1,0:T(8,128)(2,1)S(1)} %collective-permute-done.3.refs_2_), channel_id=1, source_target_pairs={{0,4},{4,0},{8,12},{12,8},{16,20},{20,16},{24,28},{28,24},{1,5},{5... | collective-permute-start | bytes 884744 | tf_op jit(solution)/shard_map/ppermute | solution.py:824
  22.0 3.6 %collective-permute-start.8 = (bf16[48,3072]{1,0:T(8,128)(2,1)S(1)}, bf16[48,3072]{1,0:T(8,128)(2,1)S(1)}, u32[]{:S(2)}, u32[]{:S(2)}) collective-permute-start(bf16[48,3072]{1,0:T(8,128)(2,1)S(1)} %collective-permute-done.4.refs_3_), channel_id=1, source_target_pairs={{0,4},{4,0},{8,12},{12,8},{16,20},{20,16},{24,28},{28,24},{1,5},{5... | collective-permute-start | bytes 884744 | tf_op jit(solution)/shard_map/ppermute | solution.py:824
  22.0 26.7 %collective-permute-start.9 = (bf16[48,5120]{1,0:T(8,128)(2,1)S(1)}, bf16[48,5120]{1,0:T(8,128)(2,1)S(1)}, u32[]{:S(2)}, u32[]{:S(2)}) collective-permute-start(bf16[48,5120]{1,0:T(8,128)(2,1)S(1)} %fusion.10.refs_5_), channel_id=1, source_target_pairs={{0,8},{4,12},{8,0},{12,4},{16,24},{20,28},{24,16},{28,20},{1,9},{5... | collective-permute-start | bytes 1474568 | tf_op jit(solution)/shard_map/ppermute | solution.py:824
  23.6 25.1 %collective-permute-start.10 = (bf16[48,5120]{1,0:T(8,128)(2,1)S(1)}, bf16[48,5120]{1,0:T(8,128)(2,1)S(1)}, u32[]{:S(2)}, u32[]{:S(2)}) collective-permute-start(bf16[48,5120]{1,0:T(8,128)(2,1)S(1)} %fusion.10.refs_5_), channel_id=1, source_target_pairs={{0,16},{4,20},{8,24},{12,28},{16,0},{20,4},{24,8},{28,12},{1,17},{... | collective-permute-start | bytes 1474568 | tf_op jit(solution)/shard_map/ppermute | solution.py:824
  24.1 24.6 %collective-permute-start.11 = (bf16[48,5120]{1,0:T(8,128)(2,1)S(1)}, bf16[48,5120]{1,0:T(8,128)(2,1)S(1)}, u32[]{:S(2)}, u32[]{:S(2)}) collective-permute-start(bf16[48,5120]{1,0:T(8,128)(2,1)S(1)} %fusion.10.refs_5_), channel_id=1, source_target_pairs={{0,24},{4,28},{8,16},{12,20},{16,8},{20,12},{24,0},{28,4},{1,25},{... | collective-permute-start | bytes 1474568 | tf_op jit(solution)/shard_map/ppermute | solution.py:824
  25.6 23.1 %collective-permute-start.12 = (bf16[48,5120]{1,0:T(8,128)(2,1)S(1)}, bf16[48,5120]{1,0:T(8,128)(2,1)S(1)}, u32[]{:S(2)}, u32[]{:S(2)}) collective-permute-start(bf16[48,5120]{1,0:T(8,128)(2,1)S(1)} %fusion.10.refs_5_), channel_id=1, source_target_pairs={{0,4},{4,0},{8,12},{12,8},{16,20},{20,16},{24,28},{28,24},{1,5},{5... | collective-permute-start | bytes 1474568 | tf_op jit(solution)/shard_map/ppermute | solution.py:824
  49.3 2.2 %collective-permute-start.14 = (bf16[48,5120]{1,0:T(8,128)(2,1)S(1)}, bf16[48,5120]{1,0:T(8,128)(2,1)S(1)}, u32[]{:S(2)}, u32[]{:S(2)}) collective-permute-start(bf16[48,5120]{1,0:T(8,128)(2,1)S(1)} %collective-permute-done.10.refs_7_), channel_id=1, source_target_pairs={{0,4},{4,0},{8,12},{12,8},{16,20},{20,16},{24,28},{28,24},{1,5},{5... | collective-permute-start | bytes 1474568 | tf_op jit(solution)/shard_map/ppermute | solution.py:824
  49.4 2.8 %collective-permute-start.15 = (bf16[48,5120]{1,0:T(8,128)(2,1)S(1)}, bf16[48,5120]{1,0:T(8,128)(2,1)S(1)}, u32[]{:S(2)}, u32[]{:S(2)}) collective-permute-start(bf16[48,5120]{1,0:T(8,128)(2,1)S(1)} %collective-permute-done.11.refs_8_), channel_id=1, source_target_pairs={{0,4},{4,0},{8,12},{12,8},{16,20},{20,16},{24,28},{28,24},{1,5},{5... | collective-permute-start | bytes 1474568 | tf_op jit(solution)/shard_map/ppermute | solution.py:824
  77.9 5.9 %collective-permute-start.16 = (bf16[4,5,48,1152]{3,2,1,0:T(8,128)(2,1)S(1)}, bf16[4,5,48,1152]{3,2,1,0:T(8,128)(2,1)S(1)}, u32[]{:S(2)}, u32[]{:S(2)}) collective-permute-start(bf16[4,5,48,1152]{3,2,1,0:T(8,128)(2,1)S(1)} %get-tuple-element.120), channel_id=1, source_target_pairs={{0,4},{4,0},{8,12},{12,8},{16,20},{20,16},{24,28},{28,24},{1,5},{5... | collective-permute-start | bytes 6635528 | tf_op jit(solution)/shard_map/ppermute | solution.py:824
  84.5 27.6 %collective-permute-start.17 = (bf16[5,48,1152]{2,1,0:T(8,128)(2,1)S(1)}, bf16[5,48,1152]{2,1,0:T(8,128)(2,1)S(1)}, u32[]{:S(2)}, u32[]{:S(2)}) collective-permute-start(bf16[5,48,1152]{2,1,0:T(8,128)(2,1)S(1)} %get-tuple-element.192), channel_id=1, source_target_pairs={{0,8},{4,12},{8,0},{12,4},{16,24},{20,28},{24,16},{28,20},{1,9},{5... | collective-permute-start | bytes 1658888 | tf_op jit(solution)/shard_map/ppermute | solution.py:824
  86.1 26.1 %collective-permute-start.18 = (bf16[5,48,1152]{2,1,0:T(8,128)(2,1)S(1)}, bf16[5,48,1152]{2,1,0:T(8,128)(2,1)S(1)}, u32[]{:S(2)}, u32[]{:S(2)}) collective-permute-start(bf16[5,48,1152]{2,1,0:T(8,128)(2,1)S(1)} %get-tuple-element.191), channel_id=1, source_target_pairs={{0,16},{4,20},{8,24},{12,28},{16,0},{20,4},{24,8},{28,12},{1,17},{... | collective-permute-start | bytes 1658888 | tf_op jit(solution)/shard_map/ppermute | solution.py:824
  86.7 25.6 %collective-permute-start.19 = (bf16[5,48,1152]{2,1,0:T(8,128)(2,1)S(1)}, bf16[5,48,1152]{2,1,0:T(8,128)(2,1)S(1)}, u32[]{:S(2)}, u32[]{:S(2)}) collective-permute-start(bf16[5,48,1152]{2,1,0:T(8,128)(2,1)S(1)} %get-tuple-element.190), channel_id=1, source_target_pairs={{0,24},{4,28},{8,16},{12,20},{16,8},{20,12},{24,0},{28,4},{1,25},{... | collective-permute-start | bytes 1658888 | tf_op jit(solution)/shard_map/ppermute | solution.py:824
  112.1 2.6 %collective-permute-start.20 = (bf16[4,48,2432]{2,1,0:T(8,128)(2,1)S(1)}, bf16[4,48,2432]{2,1,0:T(8,128)(2,1)S(1)}, u32[]{:S(2)}, u32[]{:S(2)}) collective-permute-start(bf16[4,48,2432]{2,1,0:T(8,128)(2,1)S(1)} %get-tuple-element.135), channel_id=1, source_target_pairs={{0,4},{4,0},{8,12},{12,8},{16,20},{20,16},{24,28},{28,24},{1,5},{5... | collective-permute-start | bytes 2801672 | tf_op jit(solution)/shard_map/ppermute | solution.py:824
  114.9 15.9 %collective-permute-start.21 = (bf16[3,48,1152]{2,1,0:T(8,128)(2,1)S(1)}, bf16[3,48,1152]{2,1,0:T(8,128)(2,1)S(1)}, u32[]{:S(2)}, u32[]{:S(2)}) collective-permute-start(bf16[3,48,1152]{2,1,0:T(8,128)(2,1)S(1)} %pad_maximum_fusion), channel_id=1, source_target_pairs={{0,2},{1,3},{2,0},{3,1},{4,5},{5,4},{6,7},{7,6},{8,10},{9,11},{10,... | collective-permute-start | bytes 995336 | tf_op jit(solution)/shard_map/ppermute | solution.py:840
  117.3 13.4 %collective-permute-start.22 = (bf16[48,2432]{1,0:T(8,128)(2,1)S(1)}, bf16[48,2432]{1,0:T(8,128)(2,1)S(1)}, u32[]{:S(2)}, u32[]{:S(2)}) collective-permute-start(bf16[48,2432]{1,0:T(8,128)(2,1)S(1)} %get-tuple-element.197), channel_id=1, source_target_pairs={{0,8},{4,12},{8,0},{12,4},{16,24},{20,28},{24,16},{28,20},{1,9},{5... | collective-permute-start | bytes 700424 | tf_op jit(solution)/shard_map/ppermute | solution.py:824
  118.9 11.9 %collective-permute-start.23 = (bf16[48,2432]{1,0:T(8,128)(2,1)S(1)}, bf16[48,2432]{1,0:T(8,128)(2,1)S(1)}, u32[]{:S(2)}, u32[]{:S(2)}) collective-permute-start(bf16[48,2432]{1,0:T(8,128)(2,1)S(1)} %get-tuple-element.196), channel_id=1, source_target_pairs={{0,16},{4,20},{8,24},{12,28},{16,0},{20,4},{24,8},{28,12},{1,17},{... | collective-permute-start | bytes 700424 | tf_op jit(solution)/shard_map/ppermute | solution.py:824
  120.4 10.3 %collective-permute-start.24 = (bf16[48,2432]{1,0:T(8,128)(2,1)S(1)}, bf16[48,2432]{1,0:T(8,128)(2,1)S(1)}, u32[]{:S(2)}, u32[]{:S(2)}) collective-permute-start(bf16[48,2432]{1,0:T(8,128)(2,1)S(1)} %get-tuple-element.195), channel_id=1, source_target_pairs={{0,24},{4,28},{8,16},{12,20},{16,8},{20,12},{24,0},{28,4},{1,25},{... | collective-permute-start | bytes 700424 | tf_op jit(solution)/shard_map/ppermute | solution.py:824
  131.0 8.7 %collective-permute-start.26 = (bf16[48,2432]{1,0:T(8,128)(2,1)S(1)}, bf16[48,2432]{1,0:T(8,128)(2,1)S(1)}, u32[]{:S(2)}, u32[]{:S(2)}) collective-permute-start(bf16[48,2432]{1,0:T(8,128)(2,1)S(1)} %fusion.8), channel_id=1, source_target_pairs={{0,1},{1,0},{2,3},{3,2},{4,6},{5,7},{6,4},{7,5},{8,9},{9,8},{10,11... | collective-permute-start | bytes 700424 | tf_op jit(solution)/shard_map/ppermute | solution.py:840
  132.9 6.8 %collective-permute-start.27 = (bf16[48,896]{1,0:T(8,128)(2,1)S(1)}, bf16[48,896]{1,0:T(8,128)(2,1)S(1)}, u32[]{:S(2)}, u32[]{:S(2)}) collective-permute-start(bf16[48,896]{1,0:T(8,128)(2,1)S(1)} %get-tuple-element.202), channel_id=1, source_target_pairs={{0,8},{4,12},{8,0},{12,4},{16,24},{20,28},{24,16},{28,20},{1,9},{5... | collective-permute-start | bytes 258056 | tf_op jit(solution)/shard_map/ppermute | solution.py:824
  134.4 5.4 %collective-permute-start.28 = (bf16[48,896]{1,0:T(8,128)(2,1)S(1)}, bf16[48,896]{1,0:T(8,128)(2,1)S(1)}, u32[]{:S(2)}, u32[]{:S(2)}) collective-permute-start(bf16[48,896]{1,0:T(8,128)(2,1)S(1)} %get-tuple-element.201), channel_id=1, source_target_pairs={{0,16},{4,20},{8,24},{12,28},{16,0},{20,4},{24,8},{28,12},{1,17},{... | collective-permute-start | bytes 258056 | tf_op jit(solution)/shard_map/ppermute | solution.py:824
  136.0 5.4 %collective-permute-start.29 = (bf16[48,896]{1,0:T(8,128)(2,1)S(1)}, bf16[48,896]{1,0:T(8,128)(2,1)S(1)}, u32[]{:S(2)}, u32[]{:S(2)}) collective-permute-start(bf16[48,896]{1,0:T(8,128)(2,1)S(1)} %get-tuple-element.200), channel_id=1, source_target_pairs={{0,24},{4,28},{8,16},{12,20},{16,8},{20,12},{24,0},{28,4},{1,25},{... | collective-permute-start | bytes 258056 | tf_op jit(solution)/shard_map/ppermute | solution.py:824
  136.4 16.2 %collective-permute-start.33 = (bf16[48,2304]{1,0:T(8,128)(2,1)S(1)}, bf16[48,2304]{1,0:T(8,128)(2,1)S(1)}, u32[]{:S(2)}, u32[]{:S(2)}) collective-permute-start(bf16[48,2304]{1,0:T(8,128)(2,1)S(1)} %pad_maximum_fusion.2), channel_id=1, source_target_pairs={{0,1},{1,0},{2,3},{3,2},{4,6},{5,7},{6,4},{7,5},{8,9},{9,8},{10,11... | collective-permute-start | bytes 663560 | tf_op jit(solution)/shard_map/ppermute | solution.py:840
  141.6 7.0 %collective-permute-start.30 = (bf16[48,896]{1,0:T(8,128)(2,1)S(1)}, bf16[48,896]{1,0:T(8,128)(2,1)S(1)}, u32[]{:S(2)}, u32[]{:S(2)}) collective-permute-start(bf16[48,896]{1,0:T(8,128)(2,1)S(1)} %fusion.11), channel_id=1, source_target_pairs={{0,2},{1,3},{2,0},{3,1},{4,5},{5,4},{6,7},{7,6},{8,10},{9,11},{10,... | collective-permute-start | bytes 258056 | tf_op jit(solution)/shard_map/ppermute | solution.py:840
  146.5 10.5 %collective-permute-start.31 = (bf16[48,2432]{1,0:T(8,128)(2,1)S(1)}, bf16[48,2432]{1,0:T(8,128)(2,1)S(1)}, u32[]{:S(2)}, u32[]{:S(2)}) collective-permute-start(bf16[48,2432]{1,0:T(8,128)(2,1)S(1)} %get-tuple-element.165), channel_id=1, source_target_pairs={{0,2},{1,3},{2,0},{3,1},{4,5},{5,4},{6,7},{7,6},{8,10},{9,11},{10,... | collective-permute-start | bytes 700424 | tf_op jit(solution)/shard_map/ppermute | solution.py:840
  148.7 4.6 %collective-permute-start.32 = (bf16[48,896]{1,0:T(8,128)(2,1)S(1)}, bf16[48,896]{1,0:T(8,128)(2,1)S(1)}, u32[]{:S(2)}, u32[]{:S(2)}) collective-permute-start(bf16[48,896]{1,0:T(8,128)(2,1)S(1)} %get-tuple-element.166), channel_id=1, source_target_pairs={{0,1},{1,0},{2,3},{3,2},{4,6},{5,7},{6,4},{7,5},{8,9},{9,8},{10,11... | collective-permute-start | bytes 258056 | tf_op jit(solution)/shard_map/ppermute | solution.py:840
  (13 other events, 142.8 us)

commit v5 on v4

--- a/solution.py
+++ b/solution.py
@@ -89,8 +89,10 @@
     rows, slot = one_ref.shape
     pack_ref[:rows, :slot] = one_ref[...]
     pack_ref[:rows, slot:] = two_ref[...]
-    pack_ref[rows:] = jnp.zeros_like(pack_ref[rows:])
-    pack_ref[rows : rows + 1, :slot] = hidden_bias_ref[...].reshape(1, slot)
+    first_row = lax.broadcasted_iota(jnp.int32, (16, 1), 0) == 0
+    hidden_bias = hidden_bias_ref[...].astype(f32).reshape(1, slot)
+    pack_ref[rows:, :slot] = jnp.where(first_row, hidden_bias, 0.0).astype(bf16)
+    pack_ref[rows:, slot:] = jnp.zeros((16, slot), bf16)
     turned = out_ref[...].T
     width = turned.shape[1]
     for r in range(D // rows):
@@ -118,14 +120,23 @@
     )(w_fc1, w_fc2.T, bias_fc1, w_out, bias_qv, *vectors)
 
 
-def norm_kernel(tokens_ref, rows_ref, out_ref, scaled_ref):
+def sequence_rows(scr_ref, s):
+    values = scr_ref[s * LEN : s * LEN + KEYS]
+    row = lax.broadcasted_iota(jnp.int32, (KEYS, 1), 0)
+    return jnp.where(row < LEN, values, 0.0)
+
+
+def norm_kernel(tokens_ref, rows_ref, out_ref, scaled_ref, rows_scr):
+    count = tokens_ref.shape[0]
+    rows_scr[:count] = tokens_ref[...].astype(f32)
+    rows_scr[count:] = jnp.zeros_like(rows_scr[count:])
+    row = lax.broadcasted_iota(jnp.int32, (KEYS, 1), 0)
     for s in range(out_ref.shape[0]):
-        values = tokens_ref[s * LEN : (s + 1) * LEN].astype(f32)
-        scaled, _ = normalize(values)
+        scaled, _ = normalize(sequence_rows(rows_scr, s))
         normed = scaled * rows_ref[GAIN_ONE] + rows_ref[SHIFT_ONE]
         for ref, rows in ((scaled_ref, scaled), (out_ref, normed)):
-            ref[s, :LEN] = rows.astype(bf16)
-            ref[s, LEN:] = jnp.zeros((ROWS - LEN, D), bf16)
+            ref[s, :KEYS] = jnp.where(row < LEN, rows, 0.0).astype(bf16)
+            ref[s, KEYS:] = jnp.zeros((ROWS - KEYS, D), bf16)
 
 
 def first_norm(tokens, rows_in):
@@ -134,7 +145,8 @@
     return pl.pallas_call(
         norm_kernel,
         out_shape=[shape, shape],
-        compiler_params=pltpu.CompilerParams(vmem_limit_bytes=10 * 1024 * 1024),
+        scratch_shapes=[pltpu.VMEM((seqs * KEYS, D), f32)],
+        compiler_params=pltpu.CompilerParams(vmem_limit_bytes=14 * 1024 * 1024),
         cost_estimate=cost(2.5),
         name="first_norm",
     )(tokens, rows_in)
@@ -354,18 +366,17 @@
             bias_scr[...] = bias_refs[0][...].astype(f32)
         else:
             for z in range(4):
-                row = bias_refs[z][rows : rows + 1, :per_slot]
-                bias_scr[:, z * per_slot : (z + 1) * per_slot] = row.astype(f32)
+                row = bias_refs[z][rows:, :per_slot].astype(f32)[0:1]
+                bias_scr[:, z * per_slot : (z + 1) * per_slot] = row
+        count = tokens_ref.shape[0]
+        for scr, ref in ((total_scr, tokens_ref), (back_scr, grad_ref)):
+            scr[:count] = ref[...].astype(f32)
+            scr[count:] = jnp.zeros_like(scr[count:])
         for s in range(seqs):
             block = slice(s * KEYS, (s + 1) * KEYS)
-            real = slice(s * KEYS, s * KEYS + LEN)
-            spare = slice(s * KEYS + LEN, (s + 1) * KEYS)
-            given = slice(s * LEN, (s + 1) * LEN)
-            grad_scr[real] = grad_ref[given]
-            grad_scr[spare] = jnp.zeros((KEYS - LEN, D), bf16)
-            middle_scr[real] = tokens_ref[given].astype(f32) + rows_ref[BIAS_OUT]
-            middle_scr[spare] = jnp.zeros((KEYS - LEN, D), f32)
-            middle = middle_scr[block] + dot(mixed_ref[s, :KEYS], out_wide_ref[...], NT)
+            grad_scr[block] = sequence_rows(back_scr, s).astype(bf16)
+            middle = sequence_rows(total_scr, s) + rows_ref[BIAS_OUT]
+            middle = middle + dot(mixed_ref[s, :KEYS], out_wide_ref[...], NT)
             middle_scr[block] = middle
             scaled, inverse = normalize(middle)
             scaled_scr[block] = scaled
@@ -391,9 +402,11 @@
         sums = [jnp.zeros((1, D), f32) for _ in range(2)]
         for s in range(seqs):
             block = slice(s * KEYS, (s + 1) * KEYS)
-            given = slice(s * LEN, (s + 1) * LEN)
-            output = (middle_scr[block] + total_scr[block] + rows_ref[BIAS_TWO]).astype(bf16)
-            out_ref[given] = output[:LEN]
+            output = middle_scr[block] + total_scr[block] + rows_ref[BIAS_TWO]
+            total_scr[s * LEN : (s + 1) * LEN] = output[:LEN]
+        out_ref[...] = total_scr[: seqs * LEN].astype(bf16)
+        for s in range(seqs):
+            block = slice(s * KEYS, (s + 1) * KEYS)
             scaled, inverse = scaled_scr[block], inverse_scr[block]
             grad_second = back_scr[block]
             grad_middle = grad_scr[block].astype(f32) + normalize_back(
@@ -714,10 +727,11 @@
 
 
 def input_kernel(tokens_ref, middle_grad_ref, rows_ref, early_ref, back_ref, wide_ref, out_ref):
+    out_ref[...] = tokens_ref[...].astype(f32)
     for s in range(middle_grad_ref.shape[0]):
         grad_first = early_ref[s] + dot(back_ref[s, :KEYS], wide_ref[...], NT)
         given = slice(s * LEN, (s + 1) * LEN)
-        scaled, inverse = normalize(tokens_ref[given].astype(f32))
+        scaled, inverse = normalize(out_ref[given])
         out_ref[given] = middle_grad_ref[s, :LEN] + normalize_back(
             grad_first[:LEN], rows_ref[GAIN_ONE], scaled, inverse
         )

time: 159 us -> 159 us (level)
  no operation moved by 1% of the time
where the time goes in v5:
time: 159 us
  Pallas kernels  99.4 us (63%)
  starting transfers between devices  34.9 us (22%)
  waiting for transfers between devices  17.7 us (11%)
  local copies, waits for them, and re-layouts  2.82 us (2%)
  other arithmetic  2.78 us (2%)
    pallas_call x2, Pallas kernels, backward(): pl.pallas_call(functools.partial(backward_kernel, pieces), grid=(groups,...  33.8 us
    pallas_call x1, Pallas kernels, forward(): pl.pallas_call(functools.partial(forward_kernel, pieces, len(biases), chu...  25.7 us
    pallas_call x1, Pallas kernels, attend(): pl.pallas_call(functools.partial(attend_kernel, len(parts)), grid=(GROUPS...  23 us
    ppermute x23, starting transfers between devices, swap(): return lax.ppermute(values, 'tok', [(i, i ^ mask) for i in range(size)])  17 us
    ppermute x8, starting transfers between devices, swap_half_line(): return lax.ppermute(values.astype(bf16), ('tok', 'mlp'), pairs)  14.4 us
    ppermute x8, waiting for transfers between devices, swap_half_line(): return lax.ppermute(values.astype(bf16), ('tok', 'mlp'), pairs)  8.21 us
    ppermute x23, waiting for transfers between devices, swap(): return lax.ppermute(values, 'tok', [(i, i ^ mask) for i in range(size)])  6.66 us
    pallas_call x1, Pallas kernels, mixed_gradient(): pl.pallas_call(mixed_gradient_kernel, grid=(seqs, GROUPS // each), in_spe...  5.45 us
  transfers between devices with their start and end apart: 34, of which 14 were waited for; matrix products, arithmetic and copies ran while one was open for 2% of the time, Pallas kernels for 44%

profile of v5, /device:TPU:0, one launch (start us, length us, event | category | flops | bytes accessed | tf_op | source)
XLA Modules:
  0.0 158.7 jit_solution(17089861691103684496)
XLA Ops:
  0.7 1.9 %prepare.1 = (bf16[64,1024]{1,0:T(8,128)(2,1)}, bf16[48,1024]{1,0:T(8,128)(2,1)}, f32[8,384]{1,0:T(8,128)}, f32[384,8]{1,0:T(8,128)}, f32[1,2048]{1,0:T(1,128)}) custom-call(bf16[48,512]{1,0:T(8,128)(2,1)} %one_ref.1, bf16[48,512]{1,0:T(8,128)(2,1)} %bitcast.63, bf16[512]{0:T(512)(128)(2,1)} %hidden_bias_ref.1, bf16[128,384]{1,0:T(8,128)(2,1)} %out_ref.1, ...), custom_call_target="tpu_custom_call" | custom-call | flops 2200000000 | bytes 1024 | tf_op jit(solution)/shard_map/prepare/pallas_call | solution.py:109
  2.5 4.0 %collective-permute-start = (bf16[64,1024]{1,0:T(8,128)(2,1)}, bf16[64,1024]{1,0:T(8,128)(2,1)S(1)}, u32[]{:S(2)}, u32[]{:S(2)}) collective-permute-start(bf16[64,1024]{1,0:T(8,128)(2,1)} %get-tuple-element.100.refs_0_), channel_id=1, source_target_pairs={{0,2},{1,3},{2,0},{3,1},{4,5},{5,4},{6,7},{7,6},{8,10},{9,11},{10,... | collective-permute-start | bytes 393224 | tf_op jit(solution)/shard_map/ppermute | solution.py:854
  6.6 1.5 collective-permute-start.2
  8.1 1.5 collective-permute-start.3
  11.4 1.8 %collective-permute-start.1 = (bf16[2,64,1024]{2,1,0:T(8,128)(2,1)S(1)}, bf16[2,64,1024]{2,1,0:T(8,128)(2,1)S(1)}, u32[]{:S(2)}, u32[]{:S(2)}) collective-permute-start(bf16[2,64,1024]{2,1,0:T(8,128)(2,1)S(1)} %pad_maximum_fusion.1), channel_id=1, source_target_pairs={{0,1},{1,0},{2,3},{3,2},{4,6},{5,7},{6,4},{7,5},{8,9},{9,8},{10,11... | collective-permute-start | bytes 786440 | tf_op jit(solution)/shard_map/ppermute | solution.py:854
  14.2 1.1 collective-permute-done.2.refs_1_
  15.8 1.2 collective-permute-start.7
  18.5 1.8 %collective-permute-done.1 = bf16[2,64,1024]{2,1,0:T(8,128)(2,1)S(1)} collective-permute-done((bf16[2,64,1024]{2,1,0:T(8,128)(2,1)S(1)}, bf16[2,64,1024]{2,1,0:T(8,128)(2,1)S(1)}, u32[]{:S(2)}, u32[]{:S(2)}) %collective-permute-start.1) | collective-permute-done | bytes 262176 | tf_op jit(solution)/shard_map/ppermute | solution.py:854
  20.3 1.7 %collective-permute-done.4.refs_3_ = bf16[48,3072]{1,0:T(8,128)(2,1)S(1)} collective-permute-done((bf16[48,3072]{1,0:T(8,128)(2,1)S(1)}, bf16[48,3072]{1,0:T(8,128)(2,1)S(1)}, u32[]{:S(2)}, u32[]{:S(2)}) %collective-permute-start.4) | collective-permute-done | bytes 294944 | tf_op jit(solution)/shard_map/ppermute | solution.py:844
  22.0 1.6 collective-permute-start.9
  24.1 1.5 collective-permute-start.11
  25.7 23.0 %attend.1 = (bf16[2,640,3072]{2,1,0:T(8,128)(2,1)}, bf16[2,640,1024]{2,1,0:T(8,128)(2,1)S(1)}, bf16[2,16,592,640]{3,2,1,0:T(8,128)(2,1)}, f32[2,4,8,640]{3,2,1,0:T(8,128)}, bf16[384,3072]{1,0:T(8,128)(2,1)}) custom-call(s32[1]{0:T(128)} %bitcast.me_ref, bf16[2,640,384]{2,1,0:T(8,128)(2,1)S(1)} %get-tuple-element.104.normed_ref, f32[1,2048]{1,0:T(1,128)S(1)} %copy-done.10, ...), custom_call_target="tpu_custom_call" | custom-call | flops 24199999488 | bytes 1024 | tf_op jit(solution)/shard_map/attend/pallas_call | solution.py:250
  52.2 25.7 %forward.1 = (bf16[1176,384]{1,0:T(8,128)(2,1)}, f32[2,640,384]{2,1,0:T(8,128)S(1)}, bf16[2,640,384]{2,1,0:T(8,128)(2,1)S(1)}, bf16[384,1024]{1,0:T(8,128)(2,1)S...) custom-call(s32[1]{0:T(128)} %bitcast.me_ref, bf16[1176,384]{1,0:T(8,128)(2,1)S(1)} %copy-done.2, ...), custom_call_target="tpu_custom_call" | custom-call | flops 32999999488 | bytes 1024 | tf_op jit(solution)/shard_map/forward/pallas_call | solution.py:453
  78.3 5.5 %mixed_gradient.1 = (bf16[2,640,1024]{2,1,0:T(8,128)(2,1)}, f32[2,4,8,640]{3,2,1,0:T(8,128)}) custom-call(bf16[2,640,384]{2,1,0:T(8,128)(2,1)S(1)} %get-tuple-element.117.branch_ref, bf16[384,1024]{1,0:T(8,128)(2,1)S(1)} %get-tuple-element.118.out_wide_ref, bf16[2,640,1024]{2,1,0:T(8,128)(2,1)S(1)} %get-tuple-element.109.refs_4_.mixed_ref), custom_call_target="tpu_custom_call" | custom-call | flops 5500000256 | bytes 1024 | tf_op jit(solution)/shard_map/mixed_gradient/pallas_call | solution.py:514
  84.5 1.6 collective-permute-start.17
  86.7 1.4 collective-permute-start.19
  88.1 24.0 %backward.2 = (bf16[2,640,2304]{2,1,0:T(8,128)(2,1)S(1)}, bf16[4,48,2432]{2,1,0:T(8,128)(2,1)S(1)}, bf16[4,48,2432]{2,1,0:T(8,128)(2,1)S(1)}) custom-call(s32[1]{0:T(128)} %bitcast.me_ref, bf16[2,640,1024]{2,1,0:T(8,128)(2,1)} %get-tuple-element.123.refs_0_, f32[2,4,8,640]{3,2,1,0:T(8,128)} %get-tuple-element.124.refs_1_, bf16[2,640,384]{2,1,0:T(8,128)(2,1)} %copy-done.6, ...), custom_call_target="tpu_custom_call" | custom-call | flops 36300001280 | bytes 1024 | tf_op jit(solution)/shard_map/backward/pallas_call | solution.py:672
  112.6 2.0 %collective-permute-done.20 = bf16[4,48,2432]{2,1,0:T(8,128)(2,1)S(1)} collective-permute-done((bf16[4,48,2432]{2,1,0:T(8,128)(2,1)S(1)}, bf16[4,48,2432]{2,1,0:T(8,128)(2,1)S(1)}, u32[]{:S(2)}, u32[]{:S(2)}) %collective-permute-start.20) | collective-permute-done | bytes 933920 | tf_op jit(solution)/shard_map/ppermute | solution.py:838
  114.9 2.4 %collective-permute-start.21 = (bf16[3,48,1152]{2,1,0:T(8,128)(2,1)S(1)}, bf16[3,48,1152]{2,1,0:T(8,128)(2,1)S(1)}, u32[]{:S(2)}, u32[]{:S(2)}) collective-permute-start(bf16[3,48,1152]{2,1,0:T(8,128)(2,1)S(1)} %pad_maximum_fusion), channel_id=1, source_target_pairs={{0,2},{1,3},{2,0},{3,1},{4,5},{5,4},{6,7},{7,6},{8,10},{9,11},{10,... | collective-permute-start | bytes 995336 | tf_op jit(solution)/shard_map/ppermute | solution.py:854
  117.3 1.6 collective-permute-start.22
  118.9 1.6 collective-permute-start.23
  120.9 9.9 %backward.3 = (bf16[2,640,768]{2,1,0:T(8,128)(2,1)S(1)}, bf16[4,48,896]{2,1,0:T(8,128)(2,1)S(1)}, bf16[4,48,896]{2,1,0:T(8,128)(2,1)S(1)}) custom-call(s32[1]{0:T(128)} %bitcast.me_ref, bf16[2,640,1024]{2,1,0:T(8,128)(2,1)} %get-tuple-element.123.refs_0_, f32[2,4,8,640]{3,2,1,0:T(8,128)} %get-tuple-element.124.refs_1_, bf16[2,640,384]{2,1,0:T(8,128)(2,1)} %copy-done.6, ...), custom_call_target="tpu_custom_call" | custom-call | flops 12099999744 | bytes 1024 | tf_op jit(solution)/shard_map/backward/pallas_call | solution.py:672
  131.0 1.2 collective-permute-start.26
  132.9 1.6 collective-permute-start.27
  134.4 1.6 collective-permute-start.28
  136.4 1.1 collective-permute-start.33
  137.5 2.2 %collective-permute-done.26 = bf16[48,2432]{1,0:T(8,128)(2,1)S(1)} collective-permute-done((bf16[48,2432]{1,0:T(8,128)(2,1)S(1)}, bf16[48,2432]{1,0:T(8,128)(2,1)S(1)}, u32[]{:S(2)}, u32[]{:S(2)}) %collective-permute-start.26) | collective-permute-done | bytes 233504 | tf_op jit(solution)/shard_map/ppermute | solution.py:854
  139.9 1.5 collective-permute-done.29
  142.6 3.9 %early_gradient.1.early_ref = f32[2,592,384]{2,1,0:T(8,128)S(1)} custom-call(bf16[2,640,2304]{2,1,0:T(8,128)(2,1)S(1)} %get-tuple-element.159.back_ref, bf16[384,3072]{1,0:T(8,128)(2,1)S(1)} %copy-done.5), custom_call_target="tpu_custom_call" | custom-call | flops 5500000256 | bytes 1024 | tf_op jit(solution)/shard_map/early_gradient/pallas_call | solution.py:714
  146.5 2.1 %collective-permute-start.31 = (bf16[48,2432]{1,0:T(8,128)(2,1)S(1)}, bf16[48,2432]{1,0:T(8,128)(2,1)S(1)}, u32[]{:S(2)}, u32[]{:S(2)}) collective-permute-start(bf16[48,2432]{1,0:T(8,128)(2,1)S(1)} %get-tuple-element.165), channel_id=1, source_target_pairs={{0,2},{1,3},{2,0},{3,1},{4,5},{5,4},{6,7},{7,6},{8,10},{9,11},{10,... | collective-permute-start | bytes 700424 | tf_op jit(solution)/shard_map/ppermute | solution.py:854
  149.5 3.2 %input_gradient.1 = f32[1176,384]{1,0:T(8,128)} custom-call(bf16[1176,384]{1,0:T(8,128)(2,1)S(1)} %copy-done.2, f32[2,640,384]{2,1,0:T(8,128)S(1)} %get-tuple-element.115.middle_grad_ref, f32[8,384]{1,0:T(8,128)S(1)} %copy-done.9, f32[2,592,384]{2,1,0:T(8,128)S(1)} %early_gradient.1.early_ref, bf16[2,640,768]{2,1,0:T(8,128)(2,1)S(1)} %get-tuple-element.164.back_ref, ...), custom_call_target="tpu_custom_call" | custom-call | flops 4400000000 | bytes 1024 | tf_op jit(solution)/shard_map/input_gradient/pallas_call | solution.py:741
  153.2 3.7 %collective-permute-done.31.early_line_ref = bf16[48,2432]{1,0:T(8,128)(2,1)S(1)} collective-permute-done((bf16[48,2432]{1,0:T(8,128)(2,1)S(1)}, bf16[48,2432]{1,0:T(8,128)(2,1)S(1)}, u32[]{:S(2)}, u32[]{:S(2)}) %collective-permute-start.31) | collective-permute-done | bytes 233504 | tf_op jit(solution)/shard_map/ppermute | solution.py:854
  (93 shorter events, 17.6 us)
Async XLA Ops:
  2.5 8.0 %collective-permute-start = (bf16[64,1024]{1,0:T(8,128)(2,1)}, bf16[64,1024]{1,0:T(8,128)(2,1)S(1)}, u32[]{:S(2)}, u32[]{:S(2)}) collective-permute-start(bf16[64,1024]{1,0:T(8,128)(2,1)} %get-tuple-element.100.refs_0_), channel_id=1, source_target_pairs={{0,2},{1,3},{2,0},{3,1},{4,5},{5,4},{6,7},{7,6},{8,10},{9,11},{10,... | collective-permute-start | bytes 393224 | tf_op jit(solution)/shard_map/ppermute | solution.py:854
  6.6 8.7 %collective-permute-start.2 = (bf16[48,3072]{1,0:T(8,128)(2,1)S(1)}, bf16[48,3072]{1,0:T(8,128)(2,1)S(1)}, u32[]{:S(2)}, u32[]{:S(2)}) collective-permute-start(bf16[48,3072]{1,0:T(8,128)(2,1)S(1)} %copy-done.3), channel_id=1, source_target_pairs={{0,8},{4,20},{8,0},{12,28},{16,24},{20,4},{24,16},{28,12},{1,9},{5... | collective-permute-start | bytes 884744 | tf_op jit(solution)/shard_map/ppermute | solution.py:844
  8.1 7.7 %collective-permute-start.3 = (bf16[48,3072]{1,0:T(8,128)(2,1)S(1)}, bf16[48,3072]{1,0:T(8,128)(2,1)S(1)}, u32[]{:S(2)}, u32[]{:S(2)}) collective-permute-start(bf16[48,3072]{1,0:T(8,128)(2,1)S(1)} %copy-done.3), channel_id=1, source_target_pairs={{0,16},{4,12},{8,24},{12,4},{16,0},{20,28},{24,8},{28,20},{1,17},{... | collective-permute-start | bytes 884744 | tf_op jit(solution)/shard_map/ppermute | solution.py:844
  9.6 14.0 %collective-permute-start.5 = (bf16[48,3072]{1,0:T(8,128)(2,1)S(1)}, bf16[48,3072]{1,0:T(8,128)(2,1)S(1)}, u32[]{:S(2)}, u32[]{:S(2)}) collective-permute-start(bf16[48,3072]{1,0:T(8,128)(2,1)S(1)} %copy-done.3), channel_id=1, source_target_pairs={{0,4},{4,0},{8,12},{12,8},{16,20},{20,16},{24,28},{28,24},{1,5},{5... | collective-permute-start | bytes 884744 | tf_op jit(solution)/shard_map/ppermute | solution.py:838
  11.4 8.8 %collective-permute-start.1 = (bf16[2,64,1024]{2,1,0:T(8,128)(2,1)S(1)}, bf16[2,64,1024]{2,1,0:T(8,128)(2,1)S(1)}, u32[]{:S(2)}, u32[]{:S(2)}) collective-permute-start(bf16[2,64,1024]{2,1,0:T(8,128)(2,1)S(1)} %pad_maximum_fusion.1), channel_id=1, source_target_pairs={{0,1},{1,0},{2,3},{3,2},{4,6},{5,7},{6,4},{7,5},{8,9},{9,8},{10,11... | collective-permute-start | bytes 786440 | tf_op jit(solution)/shard_map/ppermute | solution.py:854
  15.3 8.9 %collective-permute-start.6 = (bf16[48,3072]{1,0:T(8,128)(2,1)S(1)}, bf16[48,3072]{1,0:T(8,128)(2,1)S(1)}, u32[]{:S(2)}, u32[]{:S(2)}) collective-permute-start(bf16[48,3072]{1,0:T(8,128)(2,1)S(1)} %collective-permute-done.2.refs_1_), channel_id=1, source_target_pairs={{0,4},{4,0},{8,12},{12,8},{16,20},{20,16},{24,28},{28,24},{1,5},{5... | collective-permute-start | bytes 884744 | tf_op jit(solution)/shard_map/ppermute | solution.py:838
  15.3 6.7 %collective-permute-start.4 = (bf16[48,3072]{1,0:T(8,128)(2,1)S(1)}, bf16[48,3072]{1,0:T(8,128)(2,1)S(1)}, u32[]{:S(2)}, u32[]{:S(2)}) collective-permute-start(bf16[48,3072]{1,0:T(8,128)(2,1)S(1)} %collective-permute-done.2.refs_1_), channel_id=1, source_target_pairs={{0,16},{4,12},{8,24},{12,4},{16,0},{20,28},{24,8},{28,20},{1,17},{... | collective-permute-start | bytes 884744 | tf_op jit(solution)/shard_map/ppermute | solution.py:844
  15.8 9.8 %collective-permute-start.7 = (bf16[48,3072]{1,0:T(8,128)(2,1)S(1)}, bf16[48,3072]{1,0:T(8,128)(2,1)S(1)}, u32[]{:S(2)}, u32[]{:S(2)}) collective-permute-start(bf16[48,3072]{1,0:T(8,128)(2,1)S(1)} %collective-permute-done.3.refs_2_), channel_id=1, source_target_pairs={{0,4},{4,0},{8,12},{12,8},{16,20},{20,16},{24,28},{28,24},{1,5},{5... | collective-permute-start | bytes 884744 | tf_op jit(solution)/shard_map/ppermute | solution.py:838
  22.0 3.6 %collective-permute-start.8 = (bf16[48,3072]{1,0:T(8,128)(2,1)S(1)}, bf16[48,3072]{1,0:T(8,128)(2,1)S(1)}, u32[]{:S(2)}, u32[]{:S(2)}) collective-permute-start(bf16[48,3072]{1,0:T(8,128)(2,1)S(1)} %collective-permute-done.4.refs_3_), channel_id=1, source_target_pairs={{0,4},{4,0},{8,12},{12,8},{16,20},{20,16},{24,28},{28,24},{1,5},{5... | collective-permute-start | bytes 884744 | tf_op jit(solution)/shard_map/ppermute | solution.py:838
  22.0 26.7 %collective-permute-start.9 = (bf16[48,5120]{1,0:T(8,128)(2,1)S(1)}, bf16[48,5120]{1,0:T(8,128)(2,1)S(1)}, u32[]{:S(2)}, u32[]{:S(2)}) collective-permute-start(bf16[48,5120]{1,0:T(8,128)(2,1)S(1)} %fusion.10.refs_5_), channel_id=1, source_target_pairs={{0,8},{4,12},{8,0},{12,4},{16,24},{20,28},{24,16},{28,20},{1,9},{5... | collective-permute-start | bytes 1474568 | tf_op jit(solution)/shard_map/ppermute | solution.py:838
  23.6 25.1 %collective-permute-start.10 = (bf16[48,5120]{1,0:T(8,128)(2,1)S(1)}, bf16[48,5120]{1,0:T(8,128)(2,1)S(1)}, u32[]{:S(2)}, u32[]{:S(2)}) collective-permute-start(bf16[48,5120]{1,0:T(8,128)(2,1)S(1)} %fusion.10.refs_5_), channel_id=1, source_target_pairs={{0,16},{4,20},{8,24},{12,28},{16,0},{20,4},{24,8},{28,12},{1,17},{... | collective-permute-start | bytes 1474568 | tf_op jit(solution)/shard_map/ppermute | solution.py:838
  24.1 24.6 %collective-permute-start.11 = (bf16[48,5120]{1,0:T(8,128)(2,1)S(1)}, bf16[48,5120]{1,0:T(8,128)(2,1)S(1)}, u32[]{:S(2)}, u32[]{:S(2)}) collective-permute-start(bf16[48,5120]{1,0:T(8,128)(2,1)S(1)} %fusion.10.refs_5_), channel_id=1, source_target_pairs={{0,24},{4,28},{8,16},{12,20},{16,8},{20,12},{24,0},{28,4},{1,25},{... | collective-permute-start | bytes 1474568 | tf_op jit(solution)/shard_map/ppermute | solution.py:838
  25.6 23.1 %collective-permute-start.12 = (bf16[48,5120]{1,0:T(8,128)(2,1)S(1)}, bf16[48,5120]{1,0:T(8,128)(2,1)S(1)}, u32[]{:S(2)}, u32[]{:S(2)}) collective-permute-start(bf16[48,5120]{1,0:T(8,128)(2,1)S(1)} %fusion.10.refs_5_), channel_id=1, source_target_pairs={{0,4},{4,0},{8,12},{12,8},{16,20},{20,16},{24,28},{28,24},{1,5},{5... | collective-permute-start | bytes 1474568 | tf_op jit(solution)/shard_map/ppermute | solution.py:838
  49.3 2.2 %collective-permute-start.14 = (bf16[48,5120]{1,0:T(8,128)(2,1)S(1)}, bf16[48,5120]{1,0:T(8,128)(2,1)S(1)}, u32[]{:S(2)}, u32[]{:S(2)}) collective-permute-start(bf16[48,5120]{1,0:T(8,128)(2,1)S(1)} %collective-permute-done.10.refs_7_), channel_id=1, source_target_pairs={{0,4},{4,0},{8,12},{12,8},{16,20},{20,16},{24,28},{28,24},{1,5},{5... | collective-permute-start | bytes 1474568 | tf_op jit(solution)/shard_map/ppermute | solution.py:838
  49.4 2.8 %collective-permute-start.15 = (bf16[48,5120]{1,0:T(8,128)(2,1)S(1)}, bf16[48,5120]{1,0:T(8,128)(2,1)S(1)}, u32[]{:S(2)}, u32[]{:S(2)}) collective-permute-start(bf16[48,5120]{1,0:T(8,128)(2,1)S(1)} %collective-permute-done.11.refs_8_), channel_id=1, source_target_pairs={{0,4},{4,0},{8,12},{12,8},{16,20},{20,16},{24,28},{28,24},{1,5},{5... | collective-permute-start | bytes 1474568 | tf_op jit(solution)/shard_map/ppermute | solution.py:838
  77.9 5.9 %collective-permute-start.16 = (bf16[4,5,48,1152]{3,2,1,0:T(8,128)(2,1)S(1)}, bf16[4,5,48,1152]{3,2,1,0:T(8,128)(2,1)S(1)}, u32[]{:S(2)}, u32[]{:S(2)}) collective-permute-start(bf16[4,5,48,1152]{3,2,1,0:T(8,128)(2,1)S(1)} %get-tuple-element.120), channel_id=1, source_target_pairs={{0,4},{4,0},{8,12},{12,8},{16,20},{20,16},{24,28},{28,24},{1,5},{5... | collective-permute-start | bytes 6635528 | tf_op jit(solution)/shard_map/ppermute | solution.py:838
  84.5 27.6 %collective-permute-start.17 = (bf16[5,48,1152]{2,1,0:T(8,128)(2,1)S(1)}, bf16[5,48,1152]{2,1,0:T(8,128)(2,1)S(1)}, u32[]{:S(2)}, u32[]{:S(2)}) collective-permute-start(bf16[5,48,1152]{2,1,0:T(8,128)(2,1)S(1)} %get-tuple-element.192), channel_id=1, source_target_pairs={{0,8},{4,12},{8,0},{12,4},{16,24},{20,28},{24,16},{28,20},{1,9},{5... | collective-permute-start | bytes 1658888 | tf_op jit(solution)/shard_map/ppermute | solution.py:838
  86.1 26.1 %collective-permute-start.18 = (bf16[5,48,1152]{2,1,0:T(8,128)(2,1)S(1)}, bf16[5,48,1152]{2,1,0:T(8,128)(2,1)S(1)}, u32[]{:S(2)}, u32[]{:S(2)}) collective-permute-start(bf16[5,48,1152]{2,1,0:T(8,128)(2,1)S(1)} %get-tuple-element.191), channel_id=1, source_target_pairs={{0,16},{4,20},{8,24},{12,28},{16,0},{20,4},{24,8},{28,12},{1,17},{... | collective-permute-start | bytes 1658888 | tf_op jit(solution)/shard_map/ppermute | solution.py:838
  86.7 25.6 %collective-permute-start.19 = (bf16[5,48,1152]{2,1,0:T(8,128)(2,1)S(1)}, bf16[5,48,1152]{2,1,0:T(8,128)(2,1)S(1)}, u32[]{:S(2)}, u32[]{:S(2)}) collective-permute-start(bf16[5,48,1152]{2,1,0:T(8,128)(2,1)S(1)} %get-tuple-element.190), channel_id=1, source_target_pairs={{0,24},{4,28},{8,16},{12,20},{16,8},{20,12},{24,0},{28,4},{1,25},{... | collective-permute-start | bytes 1658888 | tf_op jit(solution)/shard_map/ppermute | solution.py:838
  112.1 2.6 %collective-permute-start.20 = (bf16[4,48,2432]{2,1,0:T(8,128)(2,1)S(1)}, bf16[4,48,2432]{2,1,0:T(8,128)(2,1)S(1)}, u32[]{:S(2)}, u32[]{:S(2)}) collective-permute-start(bf16[4,48,2432]{2,1,0:T(8,128)(2,1)S(1)} %get-tuple-element.135), channel_id=1, source_target_pairs={{0,4},{4,0},{8,12},{12,8},{16,20},{20,16},{24,28},{28,24},{1,5},{5... | collective-permute-start | bytes 2801672 | tf_op jit(solution)/shard_map/ppermute | solution.py:838
  114.9 15.9 %collective-permute-start.21 = (bf16[3,48,1152]{2,1,0:T(8,128)(2,1)S(1)}, bf16[3,48,1152]{2,1,0:T(8,128)(2,1)S(1)}, u32[]{:S(2)}, u32[]{:S(2)}) collective-permute-start(bf16[3,48,1152]{2,1,0:T(8,128)(2,1)S(1)} %pad_maximum_fusion), channel_id=1, source_target_pairs={{0,2},{1,3},{2,0},{3,1},{4,5},{5,4},{6,7},{7,6},{8,10},{9,11},{10,... | collective-permute-start | bytes 995336 | tf_op jit(solution)/shard_map/ppermute | solution.py:854
  117.3 13.4 %collective-permute-start.22 = (bf16[48,2432]{1,0:T(8,128)(2,1)S(1)}, bf16[48,2432]{1,0:T(8,128)(2,1)S(1)}, u32[]{:S(2)}, u32[]{:S(2)}) collective-permute-start(bf16[48,2432]{1,0:T(8,128)(2,1)S(1)} %get-tuple-element.197), channel_id=1, source_target_pairs={{0,8},{4,12},{8,0},{12,4},{16,24},{20,28},{24,16},{28,20},{1,9},{5... | collective-permute-start | bytes 700424 | tf_op jit(solution)/shard_map/ppermute | solution.py:838
  118.9 11.9 %collective-permute-start.23 = (bf16[48,2432]{1,0:T(8,128)(2,1)S(1)}, bf16[48,2432]{1,0:T(8,128)(2,1)S(1)}, u32[]{:S(2)}, u32[]{:S(2)}) collective-permute-start(bf16[48,2432]{1,0:T(8,128)(2,1)S(1)} %get-tuple-element.196), channel_id=1, source_target_pairs={{0,16},{4,20},{8,24},{12,28},{16,0},{20,4},{24,8},{28,12},{1,17},{... | collective-permute-start | bytes 700424 | tf_op jit(solution)/shard_map/ppermute | solution.py:838
  120.4 10.3 %collective-permute-start.24 = (bf16[48,2432]{1,0:T(8,128)(2,1)S(1)}, bf16[48,2432]{1,0:T(8,128)(2,1)S(1)}, u32[]{:S(2)}, u32[]{:S(2)}) collective-permute-start(bf16[48,2432]{1,0:T(8,128)(2,1)S(1)} %get-tuple-element.195), channel_id=1, source_target_pairs={{0,24},{4,28},{8,16},{12,20},{16,8},{20,12},{24,0},{28,4},{1,25},{... | collective-permute-start | bytes 700424 | tf_op jit(solution)/shard_map/ppermute | solution.py:838
  131.0 8.7 %collective-permute-start.26 = (bf16[48,2432]{1,0:T(8,128)(2,1)S(1)}, bf16[48,2432]{1,0:T(8,128)(2,1)S(1)}, u32[]{:S(2)}, u32[]{:S(2)}) collective-permute-start(bf16[48,2432]{1,0:T(8,128)(2,1)S(1)} %fusion.8), channel_id=1, source_target_pairs={{0,1},{1,0},{2,3},{3,2},{4,6},{5,7},{6,4},{7,5},{8,9},{9,8},{10,11... | collective-permute-start | bytes 700424 | tf_op jit(solution)/shard_map/ppermute | solution.py:854
  132.9 6.8 %collective-permute-start.27 = (bf16[48,896]{1,0:T(8,128)(2,1)S(1)}, bf16[48,896]{1,0:T(8,128)(2,1)S(1)}, u32[]{:S(2)}, u32[]{:S(2)}) collective-permute-start(bf16[48,896]{1,0:T(8,128)(2,1)S(1)} %get-tuple-element.202), channel_id=1, source_target_pairs={{0,8},{4,12},{8,0},{12,4},{16,24},{20,28},{24,16},{28,20},{1,9},{5... | collective-permute-start | bytes 258056 | tf_op jit(solution)/shard_map/ppermute | solution.py:838
  134.4 5.4 %collective-permute-start.28 = (bf16[48,896]{1,0:T(8,128)(2,1)S(1)}, bf16[48,896]{1,0:T(8,128)(2,1)S(1)}, u32[]{:S(2)}, u32[]{:S(2)}) collective-permute-start(bf16[48,896]{1,0:T(8,128)(2,1)S(1)} %get-tuple-element.201), channel_id=1, source_target_pairs={{0,16},{4,20},{8,24},{12,28},{16,0},{20,4},{24,8},{28,12},{1,17},{... | collective-permute-start | bytes 258056 | tf_op jit(solution)/shard_map/ppermute | solution.py:838
  136.0 5.4 %collective-permute-start.29 = (bf16[48,896]{1,0:T(8,128)(2,1)S(1)}, bf16[48,896]{1,0:T(8,128)(2,1)S(1)}, u32[]{:S(2)}, u32[]{:S(2)}) collective-permute-start(bf16[48,896]{1,0:T(8,128)(2,1)S(1)} %get-tuple-element.200), channel_id=1, source_target_pairs={{0,24},{4,28},{8,16},{12,20},{16,8},{20,12},{24,0},{28,4},{1,25},{... | collective-permute-start | bytes 258056 | tf_op jit(solution)/shard_map/ppermute | solution.py:838
  136.4 16.3 %collective-permute-start.33 = (bf16[48,2304]{1,0:T(8,128)(2,1)S(1)}, bf16[48,2304]{1,0:T(8,128)(2,1)S(1)}, u32[]{:S(2)}, u32[]{:S(2)}) collective-permute-start(bf16[48,2304]{1,0:T(8,128)(2,1)S(1)} %pad_maximum_fusion.2), channel_id=1, source_target_pairs={{0,1},{1,0},{2,3},{3,2},{4,6},{5,7},{6,4},{7,5},{8,9},{9,8},{10,11... | collective-permute-start | bytes 663560 | tf_op jit(solution)/shard_map/ppermute | solution.py:854
  141.6 7.0 %collective-permute-start.30 = (bf16[48,896]{1,0:T(8,128)(2,1)S(1)}, bf16[48,896]{1,0:T(8,128)(2,1)S(1)}, u32[]{:S(2)}, u32[]{:S(2)}) collective-permute-start(bf16[48,896]{1,0:T(8,128)(2,1)S(1)} %fusion.11), channel_id=1, source_target_pairs={{0,2},{1,3},{2,0},{3,1},{4,5},{5,4},{6,7},{7,6},{8,10},{9,11},{10,... | collective-permute-start | bytes 258056 | tf_op jit(solution)/shard_map/ppermute | solution.py:854
  146.5 10.5 %collective-permute-start.31 = (bf16[48,2432]{1,0:T(8,128)(2,1)S(1)}, bf16[48,2432]{1,0:T(8,128)(2,1)S(1)}, u32[]{:S(2)}, u32[]{:S(2)}) collective-permute-start(bf16[48,2432]{1,0:T(8,128)(2,1)S(1)} %get-tuple-element.165), channel_id=1, source_target_pairs={{0,2},{1,3},{2,0},{3,1},{4,5},{5,4},{6,7},{7,6},{8,10},{9,11},{10,... | collective-permute-start | bytes 700424 | tf_op jit(solution)/shard_map/ppermute | solution.py:854
  148.7 4.6 %collective-permute-start.32 = (bf16[48,896]{1,0:T(8,128)(2,1)S(1)}, bf16[48,896]{1,0:T(8,128)(2,1)S(1)}, u32[]{:S(2)}, u32[]{:S(2)}) collective-permute-start(bf16[48,896]{1,0:T(8,128)(2,1)S(1)} %get-tuple-element.166), channel_id=1, source_target_pairs={{0,1},{1,0},{2,3},{3,2},{4,6},{5,7},{6,4},{7,5},{8,9},{9,8},{10,11... | collective-permute-start | bytes 258056 | tf_op jit(solution)/shard_map/ppermute | solution.py:854
  (13 other events, 143.0 us)

commit v6 on v5

--- a/solution.py
+++ b/solution.py
@@ -726,15 +726,19 @@
     )(back, weights)
 
 
-def input_kernel(tokens_ref, middle_grad_ref, rows_ref, early_ref, back_ref, wide_ref, out_ref):
-    out_ref[...] = tokens_ref[...].astype(f32)
+def input_kernel(
+    tokens_ref, middle_grad_ref, rows_ref, early_ref, back_ref, wide_ref, out_ref, rows_scr
+):
+    count = tokens_ref.shape[0]
+    rows_scr[:count] = tokens_ref[...].astype(f32)
     for s in range(middle_grad_ref.shape[0]):
         grad_first = early_ref[s] + dot(back_ref[s, :KEYS], wide_ref[...], NT)
         given = slice(s * LEN, (s + 1) * LEN)
-        scaled, inverse = normalize(out_ref[given])
-        out_ref[given] = middle_grad_ref[s, :LEN] + normalize_back(
+        scaled, inverse = normalize(rows_scr[given])
+        rows_scr[given] = middle_grad_ref[s, :LEN] + normalize_back(
             grad_first[:LEN], rows_ref[GAIN_ONE], scaled, inverse
         )
+    out_ref[...] = rows_scr[:count]
 
 
 def input_gradient(tokens, middle_grad, rows_in, early, back, weights):
@@ -751,6 +755,7 @@
         ],
         out_specs=whole(tokens.shape),
         out_shape=jax.ShapeDtypeStruct(tokens.shape, f32),
+        scratch_shapes=[pltpu.VMEM((middle_grad.shape[0] * KEYS, D), f32)],
         compiler_params=pltpu.CompilerParams(vmem_limit_bytes=16 * 1024 * 1024),
         cost_estimate=cost(4),
         name="input_gradient",

time: 159 us -> 159 us (level)
  no operation moved by 1% of the time
where the time goes in v6:
time: 159 us
  Pallas kernels  99.4 us (63%)
  starting transfers between devices  34.9 us (22%)
  waiting for transfers between devices  17.7 us (11%)
  local copies, waits for them, and re-layouts  2.82 us (2%)
  other arithmetic  2.78 us (2%)
    pallas_call x2, Pallas kernels, backward(): pl.pallas_call(functools.partial(backward_kernel, pieces), grid=(groups,...  33.8 us
    pallas_call x1, Pallas kernels, forward(): pl.pallas_call(functools.partial(forward_kernel, pieces, len(biases), chu...  25.7 us
    pallas_call x1, Pallas kernels, attend(): pl.pallas_call(functools.partial(attend_kernel, len(parts)), grid=(GROUPS...  23 us
    ppermute x23, starting transfers between devices, swap(): return lax.ppermute(values, 'tok', [(i, i ^ mask) for i in range(size)])  17 us
    ppermute x8, starting transfers between devices, swap_half_line(): return lax.ppermute(values.astype(bf16), ('tok', 'mlp'), pairs)  14.4 us
    ppermute x8, waiting for transfers between devices, swap_half_line(): return lax.ppermute(values.astype(bf16), ('tok', 'mlp'), pairs)  8.22 us
    ppermute x23, waiting for transfers between devices, swap(): return lax.ppermute(values, 'tok', [(i, i ^ mask) for i in range(size)])  6.66 us
    pallas_call x1, Pallas kernels, mixed_gradient(): pl.pallas_call(mixed_gradient_kernel, grid=(seqs, GROUPS // each), in_spe...  5.45 us
  transfers between devices with their start and end apart: 34, of which 14 were waited for; matrix products, arithmetic and copies ran while one was open for 2% of the time, Pallas kernels for 44%

profile of v6, /device:TPU:0, one launch (start us, length us, event | category | flops | bytes accessed | tf_op | source)
XLA Modules:
  0.0 158.7 jit_solution(6587686554620349593)
XLA Ops:
  0.7 1.9 %prepare.1 = (bf16[64,1024]{1,0:T(8,128)(2,1)}, bf16[48,1024]{1,0:T(8,128)(2,1)}, f32[8,384]{1,0:T(8,128)}, f32[384,8]{1,0:T(8,128)}, f32[1,2048]{1,0:T(1,128)}) custom-call(bf16[48,512]{1,0:T(8,128)(2,1)} %one_ref.1, bf16[48,512]{1,0:T(8,128)(2,1)} %bitcast.63, bf16[512]{0:T(512)(128)(2,1)} %hidden_bias_ref.1, bf16[128,384]{1,0:T(8,128)(2,1)} %out_ref.1, ...), custom_call_target="tpu_custom_call" | custom-call | flops 2200000000 | bytes 1024 | tf_op jit(solution)/shard_map/prepare/pallas_call | solution.py:109
  2.5 4.0 %collective-permute-start = (bf16[64,1024]{1,0:T(8,128)(2,1)}, bf16[64,1024]{1,0:T(8,128)(2,1)S(1)}, u32[]{:S(2)}, u32[]{:S(2)}) collective-permute-start(bf16[64,1024]{1,0:T(8,128)(2,1)} %get-tuple-element.100.refs_0_), channel_id=1, source_target_pairs={{0,2},{1,3},{2,0},{3,1},{4,5},{5,4},{6,7},{7,6},{8,10},{9,11},{10,... | collective-permute-start | bytes 393224 | tf_op jit(solution)/shard_map/ppermute | solution.py:859
  6.6 1.5 collective-permute-start.2
  8.1 1.5 collective-permute-start.3
  11.4 1.8 %collective-permute-start.1 = (bf16[2,64,1024]{2,1,0:T(8,128)(2,1)S(1)}, bf16[2,64,1024]{2,1,0:T(8,128)(2,1)S(1)}, u32[]{:S(2)}, u32[]{:S(2)}) collective-permute-start(bf16[2,64,1024]{2,1,0:T(8,128)(2,1)S(1)} %pad_maximum_fusion.1), channel_id=1, source_target_pairs={{0,1},{1,0},{2,3},{3,2},{4,6},{5,7},{6,4},{7,5},{8,9},{9,8},{10,11... | collective-permute-start | bytes 786440 | tf_op jit(solution)/shard_map/ppermute | solution.py:859
  14.2 1.1 collective-permute-done.2.refs_1_
  15.8 1.2 collective-permute-start.7
  18.5 1.8 %collective-permute-done.1 = bf16[2,64,1024]{2,1,0:T(8,128)(2,1)S(1)} collective-permute-done((bf16[2,64,1024]{2,1,0:T(8,128)(2,1)S(1)}, bf16[2,64,1024]{2,1,0:T(8,128)(2,1)S(1)}, u32[]{:S(2)}, u32[]{:S(2)}) %collective-permute-start.1) | collective-permute-done | bytes 262176 | tf_op jit(solution)/shard_map/ppermute | solution.py:859
  20.3 1.7 %collective-permute-done.4.refs_3_ = bf16[48,3072]{1,0:T(8,128)(2,1)S(1)} collective-permute-done((bf16[48,3072]{1,0:T(8,128)(2,1)S(1)}, bf16[48,3072]{1,0:T(8,128)(2,1)S(1)}, u32[]{:S(2)}, u32[]{:S(2)}) %collective-permute-start.4) | collective-permute-done | bytes 294944 | tf_op jit(solution)/shard_map/ppermute | solution.py:849
  22.0 1.6 collective-permute-start.9
  24.1 1.5 collective-permute-start.11
  25.7 23.0 %attend.1 = (bf16[2,640,3072]{2,1,0:T(8,128)(2,1)}, bf16[2,640,1024]{2,1,0:T(8,128)(2,1)S(1)}, bf16[2,16,592,640]{3,2,1,0:T(8,128)(2,1)}, f32[2,4,8,640]{3,2,1,0:T(8,128)}, bf16[384,3072]{1,0:T(8,128)(2,1)}) custom-call(s32[1]{0:T(128)} %bitcast.me_ref, bf16[2,640,384]{2,1,0:T(8,128)(2,1)S(1)} %get-tuple-element.104.normed_ref, f32[1,2048]{1,0:T(1,128)S(1)} %copy-done.10, ...), custom_call_target="tpu_custom_call" | custom-call | flops 24199999488 | bytes 1024 | tf_op jit(solution)/shard_map/attend/pallas_call | solution.py:250
  52.2 25.7 %forward.1 = (bf16[1176,384]{1,0:T(8,128)(2,1)}, f32[2,640,384]{2,1,0:T(8,128)S(1)}, bf16[2,640,384]{2,1,0:T(8,128)(2,1)S(1)}, bf16[384,1024]{1,0:T(8,128)(2,1)S...) custom-call(s32[1]{0:T(128)} %bitcast.me_ref, bf16[1176,384]{1,0:T(8,128)(2,1)S(1)} %copy-done.2, ...), custom_call_target="tpu_custom_call" | custom-call | flops 32999999488 | bytes 1024 | tf_op jit(solution)/shard_map/forward/pallas_call | solution.py:453
  78.3 5.5 %mixed_gradient.1 = (bf16[2,640,1024]{2,1,0:T(8,128)(2,1)}, f32[2,4,8,640]{3,2,1,0:T(8,128)}) custom-call(bf16[2,640,384]{2,1,0:T(8,128)(2,1)S(1)} %get-tuple-element.117.branch_ref, bf16[384,1024]{1,0:T(8,128)(2,1)S(1)} %get-tuple-element.118.out_wide_ref, bf16[2,640,1024]{2,1,0:T(8,128)(2,1)S(1)} %get-tuple-element.109.refs_4_.mixed_ref), custom_call_target="tpu_custom_call" | custom-call | flops 5500000256 | bytes 1024 | tf_op jit(solution)/shard_map/mixed_gradient/pallas_call | solution.py:514
  84.5 1.6 collective-permute-start.17
  86.7 1.4 collective-permute-start.19
  88.1 24.0 %backward.2 = (bf16[2,640,2304]{2,1,0:T(8,128)(2,1)S(1)}, bf16[4,48,2432]{2,1,0:T(8,128)(2,1)S(1)}, bf16[4,48,2432]{2,1,0:T(8,128)(2,1)S(1)}) custom-call(s32[1]{0:T(128)} %bitcast.me_ref, bf16[2,640,1024]{2,1,0:T(8,128)(2,1)} %get-tuple-element.123.refs_0_, f32[2,4,8,640]{3,2,1,0:T(8,128)} %get-tuple-element.124.refs_1_, bf16[2,640,384]{2,1,0:T(8,128)(2,1)} %copy-done.6, ...), custom_call_target="tpu_custom_call" | custom-call | flops 36300001280 | bytes 1024 | tf_op jit(solution)/shard_map/backward/pallas_call | solution.py:672
  112.6 2.0 %collective-permute-done.20 = bf16[4,48,2432]{2,1,0:T(8,128)(2,1)S(1)} collective-permute-done((bf16[4,48,2432]{2,1,0:T(8,128)(2,1)S(1)}, bf16[4,48,2432]{2,1,0:T(8,128)(2,1)S(1)}, u32[]{:S(2)}, u32[]{:S(2)}) %collective-permute-start.20) | collective-permute-done | bytes 933920 | tf_op jit(solution)/shard_map/ppermute | solution.py:843
  114.9 2.4 %collective-permute-start.21 = (bf16[3,48,1152]{2,1,0:T(8,128)(2,1)S(1)}, bf16[3,48,1152]{2,1,0:T(8,128)(2,1)S(1)}, u32[]{:S(2)}, u32[]{:S(2)}) collective-permute-start(bf16[3,48,1152]{2,1,0:T(8,128)(2,1)S(1)} %pad_maximum_fusion), channel_id=1, source_target_pairs={{0,2},{1,3},{2,0},{3,1},{4,5},{5,4},{6,7},{7,6},{8,10},{9,11},{10,... | collective-permute-start | bytes 995336 | tf_op jit(solution)/shard_map/ppermute | solution.py:859
  117.3 1.6 collective-permute-start.22
  118.9 1.6 collective-permute-start.23
  120.9 9.9 %backward.3 = (bf16[2,640,768]{2,1,0:T(8,128)(2,1)S(1)}, bf16[4,48,896]{2,1,0:T(8,128)(2,1)S(1)}, bf16[4,48,896]{2,1,0:T(8,128)(2,1)S(1)}) custom-call(s32[1]{0:T(128)} %bitcast.me_ref, bf16[2,640,1024]{2,1,0:T(8,128)(2,1)} %get-tuple-element.123.refs_0_, f32[2,4,8,640]{3,2,1,0:T(8,128)} %get-tuple-element.124.refs_1_, bf16[2,640,384]{2,1,0:T(8,128)(2,1)} %copy-done.6, ...), custom_call_target="tpu_custom_call" | custom-call | flops 12099999744 | bytes 1024 | tf_op jit(solution)/shard_map/backward/pallas_call | solution.py:672
  131.0 1.2 collective-permute-start.26
  132.9 1.6 collective-permute-start.27
  134.4 1.6 collective-permute-start.28
  136.4 1.1 collective-permute-start.33
  137.5 2.2 %collective-permute-done.26 = bf16[48,2432]{1,0:T(8,128)(2,1)S(1)} collective-permute-done((bf16[48,2432]{1,0:T(8,128)(2,1)S(1)}, bf16[48,2432]{1,0:T(8,128)(2,1)S(1)}, u32[]{:S(2)}, u32[]{:S(2)}) %collective-permute-start.26) | collective-permute-done | bytes 233504 | tf_op jit(solution)/shard_map/ppermute | solution.py:859
  139.9 1.5 collective-permute-done.29
  142.6 3.9 %early_gradient.1.early_ref = f32[2,592,384]{2,1,0:T(8,128)S(1)} custom-call(bf16[2,640,2304]{2,1,0:T(8,128)(2,1)S(1)} %get-tuple-element.159.back_ref, bf16[384,3072]{1,0:T(8,128)(2,1)S(1)} %copy-done.5), custom_call_target="tpu_custom_call" | custom-call | flops 5500000256 | bytes 1024 | tf_op jit(solution)/shard_map/early_gradient/pallas_call | solution.py:714
  146.5 2.1 %collective-permute-start.31 = (bf16[48,2432]{1,0:T(8,128)(2,1)S(1)}, bf16[48,2432]{1,0:T(8,128)(2,1)S(1)}, u32[]{:S(2)}, u32[]{:S(2)}) collective-permute-start(bf16[48,2432]{1,0:T(8,128)(2,1)S(1)} %get-tuple-element.165), channel_id=1, source_target_pairs={{0,2},{1,3},{2,0},{3,1},{4,5},{5,4},{6,7},{7,6},{8,10},{9,11},{10,... | collective-permute-start | bytes 700424 | tf_op jit(solution)/shard_map/ppermute | solution.py:859
  149.5 3.2 %input_gradient.1 = f32[1176,384]{1,0:T(8,128)} custom-call(bf16[1176,384]{1,0:T(8,128)(2,1)S(1)} %copy-done.2, f32[2,640,384]{2,1,0:T(8,128)S(1)} %get-tuple-element.115.middle_grad_ref, f32[8,384]{1,0:T(8,128)S(1)} %copy-done.9, f32[2,592,384]{2,1,0:T(8,128)S(1)} %early_gradient.1.early_ref, bf16[2,640,768]{2,1,0:T(8,128)(2,1)S(1)} %get-tuple-element.164.back_ref, ...), custom_call_target="tpu_custom_call" | custom-call | flops 4400000000 | bytes 1024 | tf_op jit(solution)/shard_map/input_gradient/pallas_call | solution.py:745
  153.2 3.7 %collective-permute-done.31.early_line_ref = bf16[48,2432]{1,0:T(8,128)(2,1)S(1)} collective-permute-done((bf16[48,2432]{1,0:T(8,128)(2,1)S(1)}, bf16[48,2432]{1,0:T(8,128)(2,1)S(1)}, u32[]{:S(2)}, u32[]{:S(2)}) %collective-permute-start.31) | collective-permute-done | bytes 233504 | tf_op jit(solution)/shard_map/ppermute | solution.py:859
  (93 shorter events, 17.6 us)
Async XLA Ops:
  2.5 8.0 %collective-permute-start = (bf16[64,1024]{1,0:T(8,128)(2,1)}, bf16[64,1024]{1,0:T(8,128)(2,1)S(1)}, u32[]{:S(2)}, u32[]{:S(2)}) collective-permute-start(bf16[64,1024]{1,0:T(8,128)(2,1)} %get-tuple-element.100.refs_0_), channel_id=1, source_target_pairs={{0,2},{1,3},{2,0},{3,1},{4,5},{5,4},{6,7},{7,6},{8,10},{9,11},{10,... | collective-permute-start | bytes 393224 | tf_op jit(solution)/shard_map/ppermute | solution.py:859
  6.6 8.7 %collective-permute-start.2 = (bf16[48,3072]{1,0:T(8,128)(2,1)S(1)}, bf16[48,3072]{1,0:T(8,128)(2,1)S(1)}, u32[]{:S(2)}, u32[]{:S(2)}) collective-permute-start(bf16[48,3072]{1,0:T(8,128)(2,1)S(1)} %copy-done.3), channel_id=1, source_target_pairs={{0,8},{4,20},{8,0},{12,28},{16,24},{20,4},{24,16},{28,12},{1,9},{5... | collective-permute-start | bytes 884744 | tf_op jit(solution)/shard_map/ppermute | solution.py:849
  8.1 7.7 %collective-permute-start.3 = (bf16[48,3072]{1,0:T(8,128)(2,1)S(1)}, bf16[48,3072]{1,0:T(8,128)(2,1)S(1)}, u32[]{:S(2)}, u32[]{:S(2)}) collective-permute-start(bf16[48,3072]{1,0:T(8,128)(2,1)S(1)} %copy-done.3), channel_id=1, source_target_pairs={{0,16},{4,12},{8,24},{12,4},{16,0},{20,28},{24,8},{28,20},{1,17},{... | collective-permute-start | bytes 884744 | tf_op jit(solution)/shard_map/ppermute | solution.py:849
  9.6 14.0 %collective-permute-start.5 = (bf16[48,3072]{1,0:T(8,128)(2,1)S(1)}, bf16[48,3072]{1,0:T(8,128)(2,1)S(1)}, u32[]{:S(2)}, u32[]{:S(2)}) collective-permute-start(bf16[48,3072]{1,0:T(8,128)(2,1)S(1)} %copy-done.3), channel_id=1, source_target_pairs={{0,4},{4,0},{8,12},{12,8},{16,20},{20,16},{24,28},{28,24},{1,5},{5... | collective-permute-start | bytes 884744 | tf_op jit(solution)/shard_map/ppermute | solution.py:843
  11.4 8.8 %collective-permute-start.1 = (bf16[2,64,1024]{2,1,0:T(8,128)(2,1)S(1)}, bf16[2,64,1024]{2,1,0:T(8,128)(2,1)S(1)}, u32[]{:S(2)}, u32[]{:S(2)}) collective-permute-start(bf16[2,64,1024]{2,1,0:T(8,128)(2,1)S(1)} %pad_maximum_fusion.1), channel_id=1, source_target_pairs={{0,1},{1,0},{2,3},{3,2},{4,6},{5,7},{6,4},{7,5},{8,9},{9,8},{10,11... | collective-permute-start | bytes 786440 | tf_op jit(solution)/shard_map/ppermute | solution.py:859
  15.3 8.9 %collective-permute-start.6 = (bf16[48,3072]{1,0:T(8,128)(2,1)S(1)}, bf16[48,3072]{1,0:T(8,128)(2,1)S(1)}, u32[]{:S(2)}, u32[]{:S(2)}) collective-permute-start(bf16[48,3072]{1,0:T(8,128)(2,1)S(1)} %collective-permute-done.2.refs_1_), channel_id=1, source_target_pairs={{0,4},{4,0},{8,12},{12,8},{16,20},{20,16},{24,28},{28,24},{1,5},{5... | collective-permute-start | bytes 884744 | tf_op jit(solution)/shard_map/ppermute | solution.py:843
  15.3 6.7 %collective-permute-start.4 = (bf16[48,3072]{1,0:T(8,128)(2,1)S(1)}, bf16[48,3072]{1,0:T(8,128)(2,1)S(1)}, u32[]{:S(2)}, u32[]{:S(2)}) collective-permute-start(bf16[48,3072]{1,0:T(8,128)(2,1)S(1)} %collective-permute-done.2.refs_1_), channel_id=1, source_target_pairs={{0,16},{4,12},{8,24},{12,4},{16,0},{20,28},{24,8},{28,20},{1,17},{... | collective-permute-start | bytes 884744 | tf_op jit(solution)/shard_map/ppermute | solution.py:849
  15.8 9.8 %collective-permute-start.7 = (bf16[48,3072]{1,0:T(8,128)(2,1)S(1)}, bf16[48,3072]{1,0:T(8,128)(2,1)S(1)}, u32[]{:S(2)}, u32[]{:S(2)}) collective-permute-start(bf16[48,3072]{1,0:T(8,128)(2,1)S(1)} %collective-permute-done.3.refs_2_), channel_id=1, source_target_pairs={{0,4},{4,0},{8,12},{12,8},{16,20},{20,16},{24,28},{28,24},{1,5},{5... | collective-permute-start | bytes 884744 | tf_op jit(solution)/shard_map/ppermute | solution.py:843
  22.0 3.6 %collective-permute-start.8 = (bf16[48,3072]{1,0:T(8,128)(2,1)S(1)}, bf16[48,3072]{1,0:T(8,128)(2,1)S(1)}, u32[]{:S(2)}, u32[]{:S(2)}) collective-permute-start(bf16[48,3072]{1,0:T(8,128)(2,1)S(1)} %collective-permute-done.4.refs_3_), channel_id=1, source_target_pairs={{0,4},{4,0},{8,12},{12,8},{16,20},{20,16},{24,28},{28,24},{1,5},{5... | collective-permute-start | bytes 884744 | tf_op jit(solution)/shard_map/ppermute | solution.py:843
  22.0 26.7 %collective-permute-start.9 = (bf16[48,5120]{1,0:T(8,128)(2,1)S(1)}, bf16[48,5120]{1,0:T(8,128)(2,1)S(1)}, u32[]{:S(2)}, u32[]{:S(2)}) collective-permute-start(bf16[48,5120]{1,0:T(8,128)(2,1)S(1)} %fusion.10.refs_5_), channel_id=1, source_target_pairs={{0,8},{4,12},{8,0},{12,4},{16,24},{20,28},{24,16},{28,20},{1,9},{5... | collective-permute-start | bytes 1474568 | tf_op jit(solution)/shard_map/ppermute | solution.py:843
  23.6 25.1 %collective-permute-start.10 = (bf16[48,5120]{1,0:T(8,128)(2,1)S(1)}, bf16[48,5120]{1,0:T(8,128)(2,1)S(1)}, u32[]{:S(2)}, u32[]{:S(2)}) collective-permute-start(bf16[48,5120]{1,0:T(8,128)(2,1)S(1)} %fusion.10.refs_5_), channel_id=1, source_target_pairs={{0,16},{4,20},{8,24},{12,28},{16,0},{20,4},{24,8},{28,12},{1,17},{... | collective-permute-start | bytes 1474568 | tf_op jit(solution)/shard_map/ppermute | solution.py:843
  24.1 24.6 %collective-permute-start.11 = (bf16[48,5120]{1,0:T(8,128)(2,1)S(1)}, bf16[48,5120]{1,0:T(8,128)(2,1)S(1)}, u32[]{:S(2)}, u32[]{:S(2)}) collective-permute-start(bf16[48,5120]{1,0:T(8,128)(2,1)S(1)} %fusion.10.refs_5_), channel_id=1, source_target_pairs={{0,24},{4,28},{8,16},{12,20},{16,8},{20,12},{24,0},{28,4},{1,25},{... | collective-permute-start | bytes 1474568 | tf_op jit(solution)/shard_map/ppermute | solution.py:843
  25.6 23.1 %collective-permute-start.12 = (bf16[48,5120]{1,0:T(8,128)(2,1)S(1)}, bf16[48,5120]{1,0:T(8,128)(2,1)S(1)}, u32[]{:S(2)}, u32[]{:S(2)}) collective-permute-start(bf16[48,5120]{1,0:T(8,128)(2,1)S(1)} %fusion.10.refs_5_), channel_id=1, source_target_pairs={{0,4},{4,0},{8,12},{12,8},{16,20},{20,16},{24,28},{28,24},{1,5},{5... | collective-permute-start | bytes 1474568 | tf_op jit(solution)/shard_map/ppermute | solution.py:843
  49.3 2.2 %collective-permute-start.14 = (bf16[48,5120]{1,0:T(8,128)(2,1)S(1)}, bf16[48,5120]{1,0:T(8,128)(2,1)S(1)}, u32[]{:S(2)}, u32[]{:S(2)}) collective-permute-start(bf16[48,5120]{1,0:T(8,128)(2,1)S(1)} %collective-permute-done.10.refs_7_), channel_id=1, source_target_pairs={{0,4},{4,0},{8,12},{12,8},{16,20},{20,16},{24,28},{28,24},{1,5},{5... | collective-permute-start | bytes 1474568 | tf_op jit(solution)/shard_map/ppermute | solution.py:843
  49.4 2.8 %collective-permute-start.15 = (bf16[48,5120]{1,0:T(8,128)(2,1)S(1)}, bf16[48,5120]{1,0:T(8,128)(2,1)S(1)}, u32[]{:S(2)}, u32[]{:S(2)}) collective-permute-start(bf16[48,5120]{1,0:T(8,128)(2,1)S(1)} %collective-permute-done.11.refs_8_), channel_id=1, source_target_pairs={{0,4},{4,0},{8,12},{12,8},{16,20},{20,16},{24,28},{28,24},{1,5},{5... | collective-permute-start | bytes 1474568 | tf_op jit(solution)/shard_map/ppermute | solution.py:843
  77.9 5.9 %collective-permute-start.16 = (bf16[4,5,48,1152]{3,2,1,0:T(8,128)(2,1)S(1)}, bf16[4,5,48,1152]{3,2,1,0:T(8,128)(2,1)S(1)}, u32[]{:S(2)}, u32[]{:S(2)}) collective-permute-start(bf16[4,5,48,1152]{3,2,1,0:T(8,128)(2,1)S(1)} %get-tuple-element.120), channel_id=1, source_target_pairs={{0,4},{4,0},{8,12},{12,8},{16,20},{20,16},{24,28},{28,24},{1,5},{5... | collective-permute-start | bytes 6635528 | tf_op jit(solution)/shard_map/ppermute | solution.py:843
  84.5 27.6 %collective-permute-start.17 = (bf16[5,48,1152]{2,1,0:T(8,128)(2,1)S(1)}, bf16[5,48,1152]{2,1,0:T(8,128)(2,1)S(1)}, u32[]{:S(2)}, u32[]{:S(2)}) collective-permute-start(bf16[5,48,1152]{2,1,0:T(8,128)(2,1)S(1)} %get-tuple-element.192), channel_id=1, source_target_pairs={{0,8},{4,12},{8,0},{12,4},{16,24},{20,28},{24,16},{28,20},{1,9},{5... | collective-permute-start | bytes 1658888 | tf_op jit(solution)/shard_map/ppermute | solution.py:843
  86.1 26.1 %collective-permute-start.18 = (bf16[5,48,1152]{2,1,0:T(8,128)(2,1)S(1)}, bf16[5,48,1152]{2,1,0:T(8,128)(2,1)S(1)}, u32[]{:S(2)}, u32[]{:S(2)}) collective-permute-start(bf16[5,48,1152]{2,1,0:T(8,128)(2,1)S(1)} %get-tuple-element.191), channel_id=1, source_target_pairs={{0,16},{4,20},{8,24},{12,28},{16,0},{20,4},{24,8},{28,12},{1,17},{... | collective-permute-start | bytes 1658888 | tf_op jit(solution)/shard_map/ppermute | solution.py:843
  86.7 25.6 %collective-permute-start.19 = (bf16[5,48,1152]{2,1,0:T(8,128)(2,1)S(1)}, bf16[5,48,1152]{2,1,0:T(8,128)(2,1)S(1)}, u32[]{:S(2)}, u32[]{:S(2)}) collective-permute-start(bf16[5,48,1152]{2,1,0:T(8,128)(2,1)S(1)} %get-tuple-element.190), channel_id=1, source_target_pairs={{0,24},{4,28},{8,16},{12,20},{16,8},{20,12},{24,0},{28,4},{1,25},{... | collective-permute-start | bytes 1658888 | tf_op jit(solution)/shard_map/ppermute | solution.py:843
  112.1 2.6 %collective-permute-start.20 = (bf16[4,48,2432]{2,1,0:T(8,128)(2,1)S(1)}, bf16[4,48,2432]{2,1,0:T(8,128)(2,1)S(1)}, u32[]{:S(2)}, u32[]{:S(2)}) collective-permute-start(bf16[4,48,2432]{2,1,0:T(8,128)(2,1)S(1)} %get-tuple-element.135), channel_id=1, source_target_pairs={{0,4},{4,0},{8,12},{12,8},{16,20},{20,16},{24,28},{28,24},{1,5},{5... | collective-permute-start | bytes 2801672 | tf_op jit(solution)/shard_map/ppermute | solution.py:843
  114.9 15.9 %collective-permute-start.21 = (bf16[3,48,1152]{2,1,0:T(8,128)(2,1)S(1)}, bf16[3,48,1152]{2,1,0:T(8,128)(2,1)S(1)}, u32[]{:S(2)}, u32[]{:S(2)}) collective-permute-start(bf16[3,48,1152]{2,1,0:T(8,128)(2,1)S(1)} %pad_maximum_fusion), channel_id=1, source_target_pairs={{0,2},{1,3},{2,0},{3,1},{4,5},{5,4},{6,7},{7,6},{8,10},{9,11},{10,... | collective-permute-start | bytes 995336 | tf_op jit(solution)/shard_map/ppermute | solution.py:859
  117.3 13.4 %collective-permute-start.22 = (bf16[48,2432]{1,0:T(8,128)(2,1)S(1)}, bf16[48,2432]{1,0:T(8,128)(2,1)S(1)}, u32[]{:S(2)}, u32[]{:S(2)}) collective-permute-start(bf16[48,2432]{1,0:T(8,128)(2,1)S(1)} %get-tuple-element.197), channel_id=1, source_target_pairs={{0,8},{4,12},{8,0},{12,4},{16,24},{20,28},{24,16},{28,20},{1,9},{5... | collective-permute-start | bytes 700424 | tf_op jit(solution)/shard_map/ppermute | solution.py:843
  118.9 11.9 %collective-permute-start.23 = (bf16[48,2432]{1,0:T(8,128)(2,1)S(1)}, bf16[48,2432]{1,0:T(8,128)(2,1)S(1)}, u32[]{:S(2)}, u32[]{:S(2)}) collective-permute-start(bf16[48,2432]{1,0:T(8,128)(2,1)S(1)} %get-tuple-element.196), channel_id=1, source_target_pairs={{0,16},{4,20},{8,24},{12,28},{16,0},{20,4},{24,8},{28,12},{1,17},{... | collective-permute-start | bytes 700424 | tf_op jit(solution)/shard_map/ppermute | solution.py:843
  120.4 10.3 %collective-permute-start.24 = (bf16[48,2432]{1,0:T(8,128)(2,1)S(1)}, bf16[48,2432]{1,0:T(8,128)(2,1)S(1)}, u32[]{:S(2)}, u32[]{:S(2)}) collective-permute-start(bf16[48,2432]{1,0:T(8,128)(2,1)S(1)} %get-tuple-element.195), channel_id=1, source_target_pairs={{0,24},{4,28},{8,16},{12,20},{16,8},{20,12},{24,0},{28,4},{1,25},{... | collective-permute-start | bytes 700424 | tf_op jit(solution)/shard_map/ppermute | solution.py:843
  131.0 8.7 %collective-permute-start.26 = (bf16[48,2432]{1,0:T(8,128)(2,1)S(1)}, bf16[48,2432]{1,0:T(8,128)(2,1)S(1)}, u32[]{:S(2)}, u32[]{:S(2)}) collective-permute-start(bf16[48,2432]{1,0:T(8,128)(2,1)S(1)} %fusion.8), channel_id=1, source_target_pairs={{0,1},{1,0},{2,3},{3,2},{4,6},{5,7},{6,4},{7,5},{8,9},{9,8},{10,11... | collective-permute-start | bytes 700424 | tf_op jit(solution)/shard_map/ppermute | solution.py:859
  132.9 6.8 %collective-permute-start.27 = (bf16[48,896]{1,0:T(8,128)(2,1)S(1)}, bf16[48,896]{1,0:T(8,128)(2,1)S(1)}, u32[]{:S(2)}, u32[]{:S(2)}) collective-permute-start(bf16[48,896]{1,0:T(8,128)(2,1)S(1)} %get-tuple-element.202), channel_id=1, source_target_pairs={{0,8},{4,12},{8,0},{12,4},{16,24},{20,28},{24,16},{28,20},{1,9},{5... | collective-permute-start | bytes 258056 | tf_op jit(solution)/shard_map/ppermute | solution.py:843
  134.4 5.4 %collective-permute-start.28 = (bf16[48,896]{1,0:T(8,128)(2,1)S(1)}, bf16[48,896]{1,0:T(8,128)(2,1)S(1)}, u32[]{:S(2)}, u32[]{:S(2)}) collective-permute-start(bf16[48,896]{1,0:T(8,128)(2,1)S(1)} %get-tuple-element.201), channel_id=1, source_target_pairs={{0,16},{4,20},{8,24},{12,28},{16,0},{20,4},{24,8},{28,12},{1,17},{... | collective-permute-start | bytes 258056 | tf_op jit(solution)/shard_map/ppermute | solution.py:843
  136.0 5.4 %collective-permute-start.29 = (bf16[48,896]{1,0:T(8,128)(2,1)S(1)}, bf16[48,896]{1,0:T(8,128)(2,1)S(1)}, u32[]{:S(2)}, u32[]{:S(2)}) collective-permute-start(bf16[48,896]{1,0:T(8,128)(2,1)S(1)} %get-tuple-element.200), channel_id=1, source_target_pairs={{0,24},{4,28},{8,16},{12,20},{16,8},{20,12},{24,0},{28,4},{1,25},{... | collective-permute-start | bytes 258056 | tf_op jit(solution)/shard_map/ppermute | solution.py:843
  136.4 16.3 %collective-permute-start.33 = (bf16[48,2304]{1,0:T(8,128)(2,1)S(1)}, bf16[48,2304]{1,0:T(8,128)(2,1)S(1)}, u32[]{:S(2)}, u32[]{:S(2)}) collective-permute-start(bf16[48,2304]{1,0:T(8,128)(2,1)S(1)} %pad_maximum_fusion.2), channel_id=1, source_target_pairs={{0,1},{1,0},{2,3},{3,2},{4,6},{5,7},{6,4},{7,5},{8,9},{9,8},{10,11... | collective-permute-start | bytes 663560 | tf_op jit(solution)/shard_map/ppermute | solution.py:859
  141.6 7.0 %collective-permute-start.30 = (bf16[48,896]{1,0:T(8,128)(2,1)S(1)}, bf16[48,896]{1,0:T(8,128)(2,1)S(1)}, u32[]{:S(2)}, u32[]{:S(2)}) collective-permute-start(bf16[48,896]{1,0:T(8,128)(2,1)S(1)} %fusion.11), channel_id=1, source_target_pairs={{0,2},{1,3},{2,0},{3,1},{4,5},{5,4},{6,7},{7,6},{8,10},{9,11},{10,... | collective-permute-start | bytes 258056 | tf_op jit(solution)/shard_map/ppermute | solution.py:859
  146.5 10.5 %collective-permute-start.31 = (bf16[48,2432]{1,0:T(8,128)(2,1)S(1)}, bf16[48,2432]{1,0:T(8,128)(2,1)S(1)}, u32[]{:S(2)}, u32[]{:S(2)}) collective-permute-start(bf16[48,2432]{1,0:T(8,128)(2,1)S(1)} %get-tuple-element.165), channel_id=1, source_target_pairs={{0,2},{1,3},{2,0},{3,1},{4,5},{5,4},{6,7},{7,6},{8,10},{9,11},{10,... | collective-permute-start | bytes 700424 | tf_op jit(solution)/shard_map/ppermute | solution.py:859
  148.7 4.6 %collective-permute-start.32 = (bf16[48,896]{1,0:T(8,128)(2,1)S(1)}, bf16[48,896]{1,0:T(8,128)(2,1)S(1)}, u32[]{:S(2)}, u32[]{:S(2)}) collective-permute-start(bf16[48,896]{1,0:T(8,128)(2,1)S(1)} %get-tuple-element.166), channel_id=1, source_target_pairs={{0,1},{1,0},{2,3},{3,2},{4,6},{5,7},{6,4},{7,5},{8,9},{9,8},{10,11... | collective-permute-start | bytes 258056 | tf_op jit(solution)/shard_map/ppermute | solution.py:859
  (13 other events, 143.0 us)

commit v7 on v6

--- a/solution.py
+++ b/solution.py
@@ -1000,9 +1000,9 @@
     line_b = swap_half_line(sent, 1)
     input_grad = input_gradient(tokens, middle_grad, rows_in, early, back_b, weights)
 
-    input_grad, line_a, line_b, line_2 = after(input_grad, line_a, line_b, line_2)
+    input_grad, line_2 = after(input_grad, line_2)
     hidden_grads = hidden_end(block, rest, line_2, slot)
-    one_grad = hidden_grads[0]
+    one_grad, line_a, line_b = after(hidden_grads[0], line_a, line_b)
     qkv_grad, bias_grad, gain_grad, shift_grad = heads_end(total_a, line_a, total_b, line_b)
     _, two_grad, hidden_bias_grad, out_rows, *vector_grads = hidden_grads
     return (

time: 159 us -> 158 us (level)
  transfers between devices with their start and end apart: 34 -> 34, of which waited for: 14 -> 13; matrix products, arithmetic and copies ran while one was open for 2% -> 2% of each run, Pallas kernels for 44% -> 45%
where the time goes in v7:
time: 158 us
  Pallas kernels  99.4 us (63%)
  starting transfers between devices  34.9 us (22%)
  waiting for transfers between devices  16.9 us (11%)
  local copies, waits for them, and re-layouts  2.82 us (2%)
  other arithmetic  2.78 us (2%)
    pallas_call x2, Pallas kernels, backward(): pl.pallas_call(functools.partial(backward_kernel, pieces), grid=(groups,...  33.8 us
    pallas_call x1, Pallas kernels, forward(): pl.pallas_call(functools.partial(forward_kernel, pieces, len(biases), chu...  25.7 us
    pallas_call x1, Pallas kernels, attend(): pl.pallas_call(functools.partial(attend_kernel, len(parts)), grid=(GROUPS...  23 us
    ppermute x23, starting transfers between devices, swap(): return lax.ppermute(values, 'tok', [(i, i ^ mask) for i in range(size)])  17 us
    ppermute x8, starting transfers between devices, swap_half_line(): return lax.ppermute(values.astype(bf16), ('tok', 'mlp'), pairs)  14.4 us
    ppermute x8, waiting for transfers between devices, swap_half_line(): return lax.ppermute(values.astype(bf16), ('tok', 'mlp'), pairs)  7.39 us
    ppermute x23, waiting for transfers between devices, swap(): return lax.ppermute(values, 'tok', [(i, i ^ mask) for i in range(size)])  6.66 us
    pallas_call x1, Pallas kernels, mixed_gradient(): pl.pallas_call(mixed_gradient_kernel, grid=(seqs, GROUPS // each), in_spe...  5.45 us
  transfers between devices with their start and end apart: 34, of which 13 were waited for; matrix products, arithmetic and copies ran while one was open for 2% of the time, Pallas kernels for 45%

profile of v7, /device:TPU:0, one launch (start us, length us, event | category | flops | bytes accessed | tf_op | source)
XLA Modules:
  0.0 157.8 jit_solution(11857830840849645627)
XLA Ops:
  0.7 1.9 %prepare.1 = (bf16[64,1024]{1,0:T(8,128)(2,1)}, bf16[48,1024]{1,0:T(8,128)(2,1)}, f32[8,384]{1,0:T(8,128)}, f32[384,8]{1,0:T(8,128)}, f32[1,2048]{1,0:T(1,128)}) custom-call(bf16[48,512]{1,0:T(8,128)(2,1)} %one_ref.1, bf16[48,512]{1,0:T(8,128)(2,1)} %bitcast.63, bf16[512]{0:T(512)(128)(2,1)} %hidden_bias_ref.1, bf16[128,384]{1,0:T(8,128)(2,1)} %out_ref.1, ...), custom_call_target="tpu_custom_call" | custom-call | flops 2200000000 | bytes 1024 | tf_op jit(solution)/shard_map/prepare/pallas_call | solution.py:109
  2.5 4.0 %collective-permute-start = (bf16[64,1024]{1,0:T(8,128)(2,1)}, bf16[64,1024]{1,0:T(8,128)(2,1)S(1)}, u32[]{:S(2)}, u32[]{:S(2)}) collective-permute-start(bf16[64,1024]{1,0:T(8,128)(2,1)} %get-tuple-element.101.refs_0_), channel_id=1, source_target_pairs={{0,2},{1,3},{2,0},{3,1},{4,5},{5,4},{6,7},{7,6},{8,10},{9,11},{10,... | collective-permute-start | bytes 393224 | tf_op jit(solution)/shard_map/ppermute | solution.py:859
  6.6 1.5 collective-permute-start.2
  8.1 1.5 collective-permute-start.3
  11.4 1.8 %collective-permute-start.1 = (bf16[2,64,1024]{2,1,0:T(8,128)(2,1)S(1)}, bf16[2,64,1024]{2,1,0:T(8,128)(2,1)S(1)}, u32[]{:S(2)}, u32[]{:S(2)}) collective-permute-start(bf16[2,64,1024]{2,1,0:T(8,128)(2,1)S(1)} %pad_maximum_fusion.1), channel_id=1, source_target_pairs={{0,1},{1,0},{2,3},{3,2},{4,6},{5,7},{6,4},{7,5},{8,9},{9,8},{10,11... | collective-permute-start | bytes 786440 | tf_op jit(solution)/shard_map/ppermute | solution.py:859
  14.2 1.1 collective-permute-done.2.refs_1_
  15.8 1.2 collective-permute-start.7
  18.5 1.8 %collective-permute-done.1 = bf16[2,64,1024]{2,1,0:T(8,128)(2,1)S(1)} collective-permute-done((bf16[2,64,1024]{2,1,0:T(8,128)(2,1)S(1)}, bf16[2,64,1024]{2,1,0:T(8,128)(2,1)S(1)}, u32[]{:S(2)}, u32[]{:S(2)}) %collective-permute-start.1) | collective-permute-done | bytes 262176 | tf_op jit(solution)/shard_map/ppermute | solution.py:859
  20.3 1.7 %collective-permute-done.4.refs_3_ = bf16[48,3072]{1,0:T(8,128)(2,1)S(1)} collective-permute-done((bf16[48,3072]{1,0:T(8,128)(2,1)S(1)}, bf16[48,3072]{1,0:T(8,128)(2,1)S(1)}, u32[]{:S(2)}, u32[]{:S(2)}) %collective-permute-start.4) | collective-permute-done | bytes 294944 | tf_op jit(solution)/shard_map/ppermute | solution.py:849
  22.0 1.6 collective-permute-start.9
  24.1 1.5 collective-permute-start.11
  25.7 23.0 %attend.1 = (bf16[2,640,3072]{2,1,0:T(8,128)(2,1)}, bf16[2,640,1024]{2,1,0:T(8,128)(2,1)S(1)}, bf16[2,16,592,640]{3,2,1,0:T(8,128)(2,1)}, f32[2,4,8,640]{3,2,1,0:T(8,128)}, bf16[384,3072]{1,0:T(8,128)(2,1)}) custom-call(s32[1]{0:T(128)} %bitcast.me_ref, bf16[2,640,384]{2,1,0:T(8,128)(2,1)S(1)} %get-tuple-element.105.normed_ref, f32[1,2048]{1,0:T(1,128)S(1)} %copy-done.10, ...), custom_call_target="tpu_custom_call" | custom-call | flops 24199999488 | bytes 1024 | tf_op jit(solution)/shard_map/attend/pallas_call | solution.py:250
  52.2 25.7 %forward.1 = (bf16[1176,384]{1,0:T(8,128)(2,1)}, f32[2,640,384]{2,1,0:T(8,128)S(1)}, bf16[2,640,384]{2,1,0:T(8,128)(2,1)S(1)}, bf16[384,1024]{1,0:T(8,128)(2,1)S...) custom-call(s32[1]{0:T(128)} %bitcast.me_ref, bf16[1176,384]{1,0:T(8,128)(2,1)S(1)} %copy-done.2, ...), custom_call_target="tpu_custom_call" | custom-call | flops 32999999488 | bytes 1024 | tf_op jit(solution)/shard_map/forward/pallas_call | solution.py:453
  78.3 5.5 %mixed_gradient.1 = (bf16[2,640,1024]{2,1,0:T(8,128)(2,1)}, f32[2,4,8,640]{3,2,1,0:T(8,128)}) custom-call(bf16[2,640,384]{2,1,0:T(8,128)(2,1)S(1)} %get-tuple-element.118.branch_ref, bf16[384,1024]{1,0:T(8,128)(2,1)S(1)} %get-tuple-element.119.out_wide_ref, bf16[2,640,1024]{2,1,0:T(8,128)(2,1)S(1)} %get-tuple-element.110.refs_4_.mixed_ref), custom_call_target="tpu_custom_call" | custom-call | flops 5500000256 | bytes 1024 | tf_op jit(solution)/shard_map/mixed_gradient/pallas_call | solution.py:514
  84.5 1.6 collective-permute-start.17
  86.7 1.4 collective-permute-start.19
  88.1 24.0 %backward.2 = (bf16[2,640,2304]{2,1,0:T(8,128)(2,1)S(1)}, bf16[4,48,2432]{2,1,0:T(8,128)(2,1)S(1)}, bf16[4,48,2432]{2,1,0:T(8,128)(2,1)S(1)}) custom-call(s32[1]{0:T(128)} %bitcast.me_ref, bf16[2,640,1024]{2,1,0:T(8,128)(2,1)} %get-tuple-element.124.refs_0_, f32[2,4,8,640]{3,2,1,0:T(8,128)} %get-tuple-element.125.refs_1_, bf16[2,640,384]{2,1,0:T(8,128)(2,1)} %copy-done.6, ...), custom_call_target="tpu_custom_call" | custom-call | flops 36300001280 | bytes 1024 | tf_op jit(solution)/shard_map/backward/pallas_call | solution.py:672
  112.6 2.0 %collective-permute-done.20 = bf16[4,48,2432]{2,1,0:T(8,128)(2,1)S(1)} collective-permute-done((bf16[4,48,2432]{2,1,0:T(8,128)(2,1)S(1)}, bf16[4,48,2432]{2,1,0:T(8,128)(2,1)S(1)}, u32[]{:S(2)}, u32[]{:S(2)}) %collective-permute-start.20) | collective-permute-done | bytes 933920 | tf_op jit(solution)/shard_map/ppermute | solution.py:843
  114.9 2.4 %collective-permute-start.21 = (bf16[3,48,1152]{2,1,0:T(8,128)(2,1)S(1)}, bf16[3,48,1152]{2,1,0:T(8,128)(2,1)S(1)}, u32[]{:S(2)}, u32[]{:S(2)}) collective-permute-start(bf16[3,48,1152]{2,1,0:T(8,128)(2,1)S(1)} %pad_maximum_fusion), channel_id=1, source_target_pairs={{0,2},{1,3},{2,0},{3,1},{4,5},{5,4},{6,7},{7,6},{8,10},{9,11},{10,... | collective-permute-start | bytes 995336 | tf_op jit(solution)/shard_map/ppermute | solution.py:859
  117.3 1.6 collective-permute-start.22
  118.9 1.6 collective-permute-start.23
  120.9 9.9 %backward.3 = (bf16[2,640,768]{2,1,0:T(8,128)(2,1)S(1)}, bf16[4,48,896]{2,1,0:T(8,128)(2,1)S(1)}, bf16[4,48,896]{2,1,0:T(8,128)(2,1)S(1)}) custom-call(s32[1]{0:T(128)} %bitcast.me_ref, bf16[2,640,1024]{2,1,0:T(8,128)(2,1)} %get-tuple-element.124.refs_0_, f32[2,4,8,640]{3,2,1,0:T(8,128)} %get-tuple-element.125.refs_1_, bf16[2,640,384]{2,1,0:T(8,128)(2,1)} %copy-done.6, ...), custom_call_target="tpu_custom_call" | custom-call | flops 12099999744 | bytes 1024 | tf_op jit(solution)/shard_map/backward/pallas_call | solution.py:672
  131.0 1.2 collective-permute-start.26
  132.9 1.6 collective-permute-start.27
  134.4 1.6 collective-permute-start.28
  136.4 1.1 collective-permute-start.31
  137.5 2.2 %collective-permute-done.26 = bf16[48,2432]{1,0:T(8,128)(2,1)S(1)} collective-permute-done((bf16[48,2432]{1,0:T(8,128)(2,1)S(1)}, bf16[48,2432]{1,0:T(8,128)(2,1)S(1)}, u32[]{:S(2)}, u32[]{:S(2)}) %collective-permute-start.26) | collective-permute-done | bytes 233504 | tf_op jit(solution)/shard_map/ppermute | solution.py:859
  139.9 1.5 collective-permute-done.29
  142.6 3.9 %early_gradient.1.early_ref = f32[2,592,384]{2,1,0:T(8,128)S(1)} custom-call(bf16[2,640,2304]{2,1,0:T(8,128)(2,1)S(1)} %get-tuple-element.160.back_ref, bf16[384,3072]{1,0:T(8,128)(2,1)S(1)} %copy-done.5), custom_call_target="tpu_custom_call" | custom-call | flops 5500000256 | bytes 1024 | tf_op jit(solution)/shard_map/early_gradient/pallas_call | solution.py:714
  146.5 2.1 %collective-permute-start.32 = (bf16[48,2432]{1,0:T(8,128)(2,1)S(1)}, bf16[48,2432]{1,0:T(8,128)(2,1)S(1)}, u32[]{:S(2)}, u32[]{:S(2)}) collective-permute-start(bf16[48,2432]{1,0:T(8,128)(2,1)S(1)} %get-tuple-element.170), channel_id=1, source_target_pairs={{0,2},{1,3},{2,0},{3,1},{4,5},{5,4},{6,7},{7,6},{8,10},{9,11},{10,... | collective-permute-start | bytes 700424 | tf_op jit(solution)/shard_map/ppermute | solution.py:859
  149.5 3.2 %input_gradient.1 = f32[1176,384]{1,0:T(8,128)} custom-call(bf16[1176,384]{1,0:T(8,128)(2,1)S(1)} %copy-done.2, f32[2,640,384]{2,1,0:T(8,128)S(1)} %get-tuple-element.116.middle_grad_ref, f32[8,384]{1,0:T(8,128)S(1)} %copy-done.9, f32[2,592,384]{2,1,0:T(8,128)S(1)} %early_gradient.1.early_ref, bf16[2,640,768]{2,1,0:T(8,128)(2,1)S(1)} %get-tuple-element.165.back_ref, ...), custom_call_target="tpu_custom_call" | custom-call | flops 4400000000 | bytes 1024 | tf_op jit(solution)/shard_map/input_gradient/pallas_call | solution.py:745
  153.5 3.4 %collective-permute-done.32.early_line_ref = bf16[48,2432]{1,0:T(8,128)(2,1)S(1)} collective-permute-done((bf16[48,2432]{1,0:T(8,128)(2,1)S(1)}, bf16[48,2432]{1,0:T(8,128)(2,1)S(1)}, u32[]{:S(2)}, u32[]{:S(2)}) %collective-permute-start.32) | collective-permute-done | bytes 233504 | tf_op jit(solution)/shard_map/ppermute | solution.py:859
  (93 shorter events, 17.1 us)
Async XLA Ops:
  2.5 8.0 %collective-permute-start = (bf16[64,1024]{1,0:T(8,128)(2,1)}, bf16[64,1024]{1,0:T(8,128)(2,1)S(1)}, u32[]{:S(2)}, u32[]{:S(2)}) collective-permute-start(bf16[64,1024]{1,0:T(8,128)(2,1)} %get-tuple-element.101.refs_0_), channel_id=1, source_target_pairs={{0,2},{1,3},{2,0},{3,1},{4,5},{5,4},{6,7},{7,6},{8,10},{9,11},{10,... | collective-permute-start | bytes 393224 | tf_op jit(solution)/shard_map/ppermute | solution.py:859
  6.6 8.7 %collective-permute-start.2 = (bf16[48,3072]{1,0:T(8,128)(2,1)S(1)}, bf16[48,3072]{1,0:T(8,128)(2,1)S(1)}, u32[]{:S(2)}, u32[]{:S(2)}) collective-permute-start(bf16[48,3072]{1,0:T(8,128)(2,1)S(1)} %copy-done.3), channel_id=1, source_target_pairs={{0,8},{4,20},{8,0},{12,28},{16,24},{20,4},{24,16},{28,12},{1,9},{5... | collective-permute-start | bytes 884744 | tf_op jit(solution)/shard_map/ppermute | solution.py:849
  8.1 7.7 %collective-permute-start.3 = (bf16[48,3072]{1,0:T(8,128)(2,1)S(1)}, bf16[48,3072]{1,0:T(8,128)(2,1)S(1)}, u32[]{:S(2)}, u32[]{:S(2)}) collective-permute-start(bf16[48,3072]{1,0:T(8,128)(2,1)S(1)} %copy-done.3), channel_id=1, source_target_pairs={{0,16},{4,12},{8,24},{12,4},{16,0},{20,28},{24,8},{28,20},{1,17},{... | collective-permute-start | bytes 884744 | tf_op jit(solution)/shard_map/ppermute | solution.py:849
  9.6 14.0 %collective-permute-start.5 = (bf16[48,3072]{1,0:T(8,128)(2,1)S(1)}, bf16[48,3072]{1,0:T(8,128)(2,1)S(1)}, u32[]{:S(2)}, u32[]{:S(2)}) collective-permute-start(bf16[48,3072]{1,0:T(8,128)(2,1)S(1)} %copy-done.3), channel_id=1, source_target_pairs={{0,4},{4,0},{8,12},{12,8},{16,20},{20,16},{24,28},{28,24},{1,5},{5... | collective-permute-start | bytes 884744 | tf_op jit(solution)/shard_map/ppermute | solution.py:843
  11.4 8.8 %collective-permute-start.1 = (bf16[2,64,1024]{2,1,0:T(8,128)(2,1)S(1)}, bf16[2,64,1024]{2,1,0:T(8,128)(2,1)S(1)}, u32[]{:S(2)}, u32[]{:S(2)}) collective-permute-start(bf16[2,64,1024]{2,1,0:T(8,128)(2,1)S(1)} %pad_maximum_fusion.1), channel_id=1, source_target_pairs={{0,1},{1,0},{2,3},{3,2},{4,6},{5,7},{6,4},{7,5},{8,9},{9,8},{10,11... | collective-permute-start | bytes 786440 | tf_op jit(solution)/shard_map/ppermute | solution.py:859
  15.3 8.9 %collective-permute-start.6 = (bf16[48,3072]{1,0:T(8,128)(2,1)S(1)}, bf16[48,3072]{1,0:T(8,128)(2,1)S(1)}, u32[]{:S(2)}, u32[]{:S(2)}) collective-permute-start(bf16[48,3072]{1,0:T(8,128)(2,1)S(1)} %collective-permute-done.2.refs_1_), channel_id=1, source_target_pairs={{0,4},{4,0},{8,12},{12,8},{16,20},{20,16},{24,28},{28,24},{1,5},{5... | collective-permute-start | bytes 884744 | tf_op jit(solution)/shard_map/ppermute | solution.py:843
  15.3 6.7 %collective-permute-start.4 = (bf16[48,3072]{1,0:T(8,128)(2,1)S(1)}, bf16[48,3072]{1,0:T(8,128)(2,1)S(1)}, u32[]{:S(2)}, u32[]{:S(2)}) collective-permute-start(bf16[48,3072]{1,0:T(8,128)(2,1)S(1)} %collective-permute-done.2.refs_1_), channel_id=1, source_target_pairs={{0,16},{4,12},{8,24},{12,4},{16,0},{20,28},{24,8},{28,20},{1,17},{... | collective-permute-start | bytes 884744 | tf_op jit(solution)/shard_map/ppermute | solution.py:849
  15.8 9.8 %collective-permute-start.7 = (bf16[48,3072]{1,0:T(8,128)(2,1)S(1)}, bf16[48,3072]{1,0:T(8,128)(2,1)S(1)}, u32[]{:S(2)}, u32[]{:S(2)}) collective-permute-start(bf16[48,3072]{1,0:T(8,128)(2,1)S(1)} %collective-permute-done.3.refs_2_), channel_id=1, source_target_pairs={{0,4},{4,0},{8,12},{12,8},{16,20},{20,16},{24,28},{28,24},{1,5},{5... | collective-permute-start | bytes 884744 | tf_op jit(solution)/shard_map/ppermute | solution.py:843
  22.0 3.6 %collective-permute-start.8 = (bf16[48,3072]{1,0:T(8,128)(2,1)S(1)}, bf16[48,3072]{1,0:T(8,128)(2,1)S(1)}, u32[]{:S(2)}, u32[]{:S(2)}) collective-permute-start(bf16[48,3072]{1,0:T(8,128)(2,1)S(1)} %collective-permute-done.4.refs_3_), channel_id=1, source_target_pairs={{0,4},{4,0},{8,12},{12,8},{16,20},{20,16},{24,28},{28,24},{1,5},{5... | collective-permute-start | bytes 884744 | tf_op jit(solution)/shard_map/ppermute | solution.py:843
  22.0 26.7 %collective-permute-start.9 = (bf16[48,5120]{1,0:T(8,128)(2,1)S(1)}, bf16[48,5120]{1,0:T(8,128)(2,1)S(1)}, u32[]{:S(2)}, u32[]{:S(2)}) collective-permute-start(bf16[48,5120]{1,0:T(8,128)(2,1)S(1)} %fusion.10.refs_5_), channel_id=1, source_target_pairs={{0,8},{4,12},{8,0},{12,4},{16,24},{20,28},{24,16},{28,20},{1,9},{5... | collective-permute-start | bytes 1474568 | tf_op jit(solution)/shard_map/ppermute | solution.py:843
  23.6 25.1 %collective-permute-start.10 = (bf16[48,5120]{1,0:T(8,128)(2,1)S(1)}, bf16[48,5120]{1,0:T(8,128)(2,1)S(1)}, u32[]{:S(2)}, u32[]{:S(2)}) collective-permute-start(bf16[48,5120]{1,0:T(8,128)(2,1)S(1)} %fusion.10.refs_5_), channel_id=1, source_target_pairs={{0,16},{4,20},{8,24},{12,28},{16,0},{20,4},{24,8},{28,12},{1,17},{... | collective-permute-start | bytes 1474568 | tf_op jit(solution)/shard_map/ppermute | solution.py:843
  24.1 24.6 %collective-permute-start.11 = (bf16[48,5120]{1,0:T(8,128)(2,1)S(1)}, bf16[48,5120]{1,0:T(8,128)(2,1)S(1)}, u32[]{:S(2)}, u32[]{:S(2)}) collective-permute-start(bf16[48,5120]{1,0:T(8,128)(2,1)S(1)} %fusion.10.refs_5_), channel_id=1, source_target_pairs={{0,24},{4,28},{8,16},{12,20},{16,8},{20,12},{24,0},{28,4},{1,25},{... | collective-permute-start | bytes 1474568 | tf_op jit(solution)/shard_map/ppermute | solution.py:843
  25.6 23.1 %collective-permute-start.12 = (bf16[48,5120]{1,0:T(8,128)(2,1)S(1)}, bf16[48,5120]{1,0:T(8,128)(2,1)S(1)}, u32[]{:S(2)}, u32[]{:S(2)}) collective-permute-start(bf16[48,5120]{1,0:T(8,128)(2,1)S(1)} %fusion.10.refs_5_), channel_id=1, source_target_pairs={{0,4},{4,0},{8,12},{12,8},{16,20},{20,16},{24,28},{28,24},{1,5},{5... | collective-permute-start | bytes 1474568 | tf_op jit(solution)/shard_map/ppermute | solution.py:843
  49.3 2.2 %collective-permute-start.14 = (bf16[48,5120]{1,0:T(8,128)(2,1)S(1)}, bf16[48,5120]{1,0:T(8,128)(2,1)S(1)}, u32[]{:S(2)}, u32[]{:S(2)}) collective-permute-start(bf16[48,5120]{1,0:T(8,128)(2,1)S(1)} %collective-permute-done.10.refs_7_), channel_id=1, source_target_pairs={{0,4},{4,0},{8,12},{12,8},{16,20},{20,16},{24,28},{28,24},{1,5},{5... | collective-permute-start | bytes 1474568 | tf_op jit(solution)/shard_map/ppermute | solution.py:843
  49.4 2.8 %collective-permute-start.15 = (bf16[48,5120]{1,0:T(8,128)(2,1)S(1)}, bf16[48,5120]{1,0:T(8,128)(2,1)S(1)}, u32[]{:S(2)}, u32[]{:S(2)}) collective-permute-start(bf16[48,5120]{1,0:T(8,128)(2,1)S(1)} %collective-permute-done.11.refs_8_), channel_id=1, source_target_pairs={{0,4},{4,0},{8,12},{12,8},{16,20},{20,16},{24,28},{28,24},{1,5},{5... | collective-permute-start | bytes 1474568 | tf_op jit(solution)/shard_map/ppermute | solution.py:843
  77.9 5.9 %collective-permute-start.16 = (bf16[4,5,48,1152]{3,2,1,0:T(8,128)(2,1)S(1)}, bf16[4,5,48,1152]{3,2,1,0:T(8,128)(2,1)S(1)}, u32[]{:S(2)}, u32[]{:S(2)}) collective-permute-start(bf16[4,5,48,1152]{3,2,1,0:T(8,128)(2,1)S(1)} %get-tuple-element.121), channel_id=1, source_target_pairs={{0,4},{4,0},{8,12},{12,8},{16,20},{20,16},{24,28},{28,24},{1,5},{5... | collective-permute-start | bytes 6635528 | tf_op jit(solution)/shard_map/ppermute | solution.py:843
  84.5 27.6 %collective-permute-start.17 = (bf16[5,48,1152]{2,1,0:T(8,128)(2,1)S(1)}, bf16[5,48,1152]{2,1,0:T(8,128)(2,1)S(1)}, u32[]{:S(2)}, u32[]{:S(2)}) collective-permute-start(bf16[5,48,1152]{2,1,0:T(8,128)(2,1)S(1)} %get-tuple-element.194), channel_id=1, source_target_pairs={{0,8},{4,12},{8,0},{12,4},{16,24},{20,28},{24,16},{28,20},{1,9},{5... | collective-permute-start | bytes 1658888 | tf_op jit(solution)/shard_map/ppermute | solution.py:843
  86.1 26.1 %collective-permute-start.18 = (bf16[5,48,1152]{2,1,0:T(8,128)(2,1)S(1)}, bf16[5,48,1152]{2,1,0:T(8,128)(2,1)S(1)}, u32[]{:S(2)}, u32[]{:S(2)}) collective-permute-start(bf16[5,48,1152]{2,1,0:T(8,128)(2,1)S(1)} %get-tuple-element.193), channel_id=1, source_target_pairs={{0,16},{4,20},{8,24},{12,28},{16,0},{20,4},{24,8},{28,12},{1,17},{... | collective-permute-start | bytes 1658888 | tf_op jit(solution)/shard_map/ppermute | solution.py:843
  86.7 25.6 %collective-permute-start.19 = (bf16[5,48,1152]{2,1,0:T(8,128)(2,1)S(1)}, bf16[5,48,1152]{2,1,0:T(8,128)(2,1)S(1)}, u32[]{:S(2)}, u32[]{:S(2)}) collective-permute-start(bf16[5,48,1152]{2,1,0:T(8,128)(2,1)S(1)} %get-tuple-element.192), channel_id=1, source_target_pairs={{0,24},{4,28},{8,16},{12,20},{16,8},{20,12},{24,0},{28,4},{1,25},{... | collective-permute-start | bytes 1658888 | tf_op jit(solution)/shard_map/ppermute | solution.py:843
  112.1 2.6 %collective-permute-start.20 = (bf16[4,48,2432]{2,1,0:T(8,128)(2,1)S(1)}, bf16[4,48,2432]{2,1,0:T(8,128)(2,1)S(1)}, u32[]{:S(2)}, u32[]{:S(2)}) collective-permute-start(bf16[4,48,2432]{2,1,0:T(8,128)(2,1)S(1)} %get-tuple-element.136), channel_id=1, source_target_pairs={{0,4},{4,0},{8,12},{12,8},{16,20},{20,16},{24,28},{28,24},{1,5},{5... | collective-permute-start | bytes 2801672 | tf_op jit(solution)/shard_map/ppermute | solution.py:843
  114.9 15.9 %collective-permute-start.21 = (bf16[3,48,1152]{2,1,0:T(8,128)(2,1)S(1)}, bf16[3,48,1152]{2,1,0:T(8,128)(2,1)S(1)}, u32[]{:S(2)}, u32[]{:S(2)}) collective-permute-start(bf16[3,48,1152]{2,1,0:T(8,128)(2,1)S(1)} %pad_maximum_fusion), channel_id=1, source_target_pairs={{0,2},{1,3},{2,0},{3,1},{4,5},{5,4},{6,7},{7,6},{8,10},{9,11},{10,... | collective-permute-start | bytes 995336 | tf_op jit(solution)/shard_map/ppermute | solution.py:859
  117.3 13.4 %collective-permute-start.22 = (bf16[48,2432]{1,0:T(8,128)(2,1)S(1)}, bf16[48,2432]{1,0:T(8,128)(2,1)S(1)}, u32[]{:S(2)}, u32[]{:S(2)}) collective-permute-start(bf16[48,2432]{1,0:T(8,128)(2,1)S(1)} %get-tuple-element.199), channel_id=1, source_target_pairs={{0,8},{4,12},{8,0},{12,4},{16,24},{20,28},{24,16},{28,20},{1,9},{5... | collective-permute-start | bytes 700424 | tf_op jit(solution)/shard_map/ppermute | solution.py:843
  118.9 11.9 %collective-permute-start.23 = (bf16[48,2432]{1,0:T(8,128)(2,1)S(1)}, bf16[48,2432]{1,0:T(8,128)(2,1)S(1)}, u32[]{:S(2)}, u32[]{:S(2)}) collective-permute-start(bf16[48,2432]{1,0:T(8,128)(2,1)S(1)} %get-tuple-element.198), channel_id=1, source_target_pairs={{0,16},{4,20},{8,24},{12,28},{16,0},{20,4},{24,8},{28,12},{1,17},{... | collective-permute-start | bytes 700424 | tf_op jit(solution)/shard_map/ppermute | solution.py:843
  120.4 10.3 %collective-permute-start.24 = (bf16[48,2432]{1,0:T(8,128)(2,1)S(1)}, bf16[48,2432]{1,0:T(8,128)(2,1)S(1)}, u32[]{:S(2)}, u32[]{:S(2)}) collective-permute-start(bf16[48,2432]{1,0:T(8,128)(2,1)S(1)} %get-tuple-element.197), channel_id=1, source_target_pairs={{0,24},{4,28},{8,16},{12,20},{16,8},{20,12},{24,0},{28,4},{1,25},{... | collective-permute-start | bytes 700424 | tf_op jit(solution)/shard_map/ppermute | solution.py:843
  131.0 8.7 %collective-permute-start.26 = (bf16[48,2432]{1,0:T(8,128)(2,1)S(1)}, bf16[48,2432]{1,0:T(8,128)(2,1)S(1)}, u32[]{:S(2)}, u32[]{:S(2)}) collective-permute-start(bf16[48,2432]{1,0:T(8,128)(2,1)S(1)} %fusion.8), channel_id=1, source_target_pairs={{0,1},{1,0},{2,3},{3,2},{4,6},{5,7},{6,4},{7,5},{8,9},{9,8},{10,11... | collective-permute-start | bytes 700424 | tf_op jit(solution)/shard_map/ppermute | solution.py:859
  132.9 6.8 %collective-permute-start.27 = (bf16[48,896]{1,0:T(8,128)(2,1)S(1)}, bf16[48,896]{1,0:T(8,128)(2,1)S(1)}, u32[]{:S(2)}, u32[]{:S(2)}) collective-permute-start(bf16[48,896]{1,0:T(8,128)(2,1)S(1)} %get-tuple-element.204), channel_id=1, source_target_pairs={{0,8},{4,12},{8,0},{12,4},{16,24},{20,28},{24,16},{28,20},{1,9},{5... | collective-permute-start | bytes 258056 | tf_op jit(solution)/shard_map/ppermute | solution.py:843
  134.4 5.4 %collective-permute-start.28 = (bf16[48,896]{1,0:T(8,128)(2,1)S(1)}, bf16[48,896]{1,0:T(8,128)(2,1)S(1)}, u32[]{:S(2)}, u32[]{:S(2)}) collective-permute-start(bf16[48,896]{1,0:T(8,128)(2,1)S(1)} %get-tuple-element.203), channel_id=1, source_target_pairs={{0,16},{4,20},{8,24},{12,28},{16,0},{20,4},{24,8},{28,12},{1,17},{... | collective-permute-start | bytes 258056 | tf_op jit(solution)/shard_map/ppermute | solution.py:843
  136.0 5.4 %collective-permute-start.29 = (bf16[48,896]{1,0:T(8,128)(2,1)S(1)}, bf16[48,896]{1,0:T(8,128)(2,1)S(1)}, u32[]{:S(2)}, u32[]{:S(2)}) collective-permute-start(bf16[48,896]{1,0:T(8,128)(2,1)S(1)} %get-tuple-element.202), channel_id=1, source_target_pairs={{0,24},{4,28},{8,16},{12,20},{16,8},{20,12},{24,0},{28,4},{1,25},{... | collective-permute-start | bytes 258056 | tf_op jit(solution)/shard_map/ppermute | solution.py:843
  136.4 16.3 %collective-permute-start.31 = (bf16[48,2304]{1,0:T(8,128)(2,1)S(1)}, bf16[48,2304]{1,0:T(8,128)(2,1)S(1)}, u32[]{:S(2)}, u32[]{:S(2)}) collective-permute-start(bf16[48,2304]{1,0:T(8,128)(2,1)S(1)} %pad_maximum_fusion.2), channel_id=1, source_target_pairs={{0,1},{1,0},{2,3},{3,2},{4,6},{5,7},{6,4},{7,5},{8,9},{9,8},{10,11... | collective-permute-start | bytes 663560 | tf_op jit(solution)/shard_map/ppermute | solution.py:859
  141.6 7.0 %collective-permute-start.30 = (bf16[48,896]{1,0:T(8,128)(2,1)S(1)}, bf16[48,896]{1,0:T(8,128)(2,1)S(1)}, u32[]{:S(2)}, u32[]{:S(2)}) collective-permute-start(bf16[48,896]{1,0:T(8,128)(2,1)S(1)} %fusion.11), channel_id=1, source_target_pairs={{0,2},{1,3},{2,0},{3,1},{4,5},{5,4},{6,7},{7,6},{8,10},{9,11},{10,... | collective-permute-start | bytes 258056 | tf_op jit(solution)/shard_map/ppermute | solution.py:859
  146.5 10.5 %collective-permute-start.32 = (bf16[48,2432]{1,0:T(8,128)(2,1)S(1)}, bf16[48,2432]{1,0:T(8,128)(2,1)S(1)}, u32[]{:S(2)}, u32[]{:S(2)}) collective-permute-start(bf16[48,2432]{1,0:T(8,128)(2,1)S(1)} %get-tuple-element.170), channel_id=1, source_target_pairs={{0,2},{1,3},{2,0},{3,1},{4,5},{5,4},{6,7},{7,6},{8,10},{9,11},{10,... | collective-permute-start | bytes 700424 | tf_op jit(solution)/shard_map/ppermute | solution.py:859
  148.7 4.9 %collective-permute-start.33 = (bf16[48,896]{1,0:T(8,128)(2,1)S(1)}, bf16[48,896]{1,0:T(8,128)(2,1)S(1)}, u32[]{:S(2)}, u32[]{:S(2)}) collective-permute-start(bf16[48,896]{1,0:T(8,128)(2,1)S(1)} %get-tuple-element.171), channel_id=1, source_target_pairs={{0,1},{1,0},{2,3},{3,2},{4,6},{5,7},{6,4},{7,5},{8,9},{9,8},{10,11... | collective-permute-start | bytes 258056 | tf_op jit(solution)/shard_map/ppermute | solution.py:859
  (13 other events, 143.0 us)
